TPU v7x, 32 devices: a whole 2x2x4 slice. The times are simulated.
32 devices in a mesh: freq: 2 (over y), row: 4 (over z), col: 2 (over x), cplx: 2 (over core).
Axes of the slice: x: 2, y: 2, z: 4, core: 2. Of those that a mesh axis runs over, the one named last changes fastest.
Arguments:
- u_bases: bfloat16 [8, 8, 2, 128, 512], P(('freq', 'row'), ('col', 'cplx')), parts along dimension 0
- v_bases: bfloat16 [8, 8, 2, 128, 512], P(('freq', 'row'), ('col', 'cplx')), parts along dimension 0
- tile_ranks: int32 [8, 8], P(('freq', 'row'), ('col', 'cplx')), parts along dimension 0, may hold values from 32 to 128, as said below
- u_unit: float32 [64, 2, 2048], P(('freq', 'col', 'cplx'), None, 'row'), parts along dimension 0, may hold values from -6 to 6
- v_unit: float32 [64, 2, 4096], P(('freq', 'row'), None, ('col', 'cplx')), parts along dimension 0, may hold values from -6 to 6
- x_solution: float32 [64, 2, 4096], P(('freq', 'row'), None, ('col', 'cplx')), parts along dimension 0, may hold values from -6 to 6
- w_direction: float32 [64, 2, 4096], P(('freq', 'row'), None, ('col', 'cplx')), parts along dimension 0, may hold values from -6 to 6
- alpha_prev: float32 [64], P('freq'), parts along dimension 0, may hold values from 0.5 to 2
- rhobar_prev: float32 [64], P('freq'), parts along dimension 0, may hold values from 0.5 to 2
- phibar_prev: float32 [64], P('freq'), parts along dimension 0, may hold values from 0.5 to 2
Outputs:
- x_next: float32 [64, 2, 4096], P(('freq', 'row'), None, ('col', 'cplx')), parts along dimension 0
- w_next: float32 [64, 2, 4096], P(('freq', 'row'), None, ('col', 'cplx')), parts along dimension 0
- u_next: float32 [64, 2, 2048], P(('freq', 'col', 'cplx'), None, 'row'), parts along dimension 0
- v_next: float32 [64, 2, 4096], P(('freq', 'row'), None, ('col', 'cplx')), parts along dimension 0
- alpha_next: float32 [64], P('freq'), parts along dimension 0
- rhobar_next: float32 [64], P('freq'), parts along dimension 0
- phibar_next: float32 [64], P('freq'), parts along dimension 0
There are 2 independent parts, one for each index of `freq`. A program takes and returns all parts, laid end to end along the dimension named above; each array names one. Nothing has to cross between parts.
Inputs may be any that keep to these rules, and one draw needn't show every extreme that they name: `tile_ranks`: some tile has rank 128.
All inputs are finite; a program needn't handle non-finite values.
Results may differ from a plain program's by a relative error of at most 0.011.
Values may be sent and summed in bfloat16 or wider, within the bound.
No kernel may reach another device: no remote copies, remote signals or barrier semaphores. Data moves between devices by JAX's collectives and lax.ppermute only.
A program may use at most 64 MiB of HBM per device.

v0:
```python
from functools import partial

import jax
import jax.numpy as jnp
from jax import lax
from jax.sharding import PartitionSpec as P

epsilon = 1e-06


def forward_terms(u_bases, v_bases, rank_live, portion):
    rows_here = portion.shape[0]
    product = partial(jnp.einsum, preferred_element_type=jnp.float32)
    columns = portion.reshape(rows_here, 2, v_bases.shape[1], v_bases.shape[4])
    right_re = v_bases[:, :, 0]
    right_im = v_bases[:, :, 1]
    left_re = u_bases[:, :, 0]
    left_im = u_bases[:, :, 1]
    coef_re = product("pqri,nqi->npqr", right_re, columns[:, 0]) + product(
        "pqri,nqi->npqr", right_im, columns[:, 1]
    )
    coef_im = product("pqri,nqi->npqr", right_re, columns[:, 1]) - product(
        "pqri,nqi->npqr", right_im, columns[:, 0]
    )
    coef_re = (coef_re * rank_live).astype(jnp.bfloat16)
    coef_im = (coef_im * rank_live).astype(jnp.bfloat16)
    out_re = product("pqri,npqr->npi", left_re, coef_re) - product(
        "pqri,npqr->npi", left_im, coef_im
    )
    out_im = product("pqri,npqr->npi", left_re, coef_im) + product(
        "pqri,npqr->npi", left_im, coef_re
    )
    return jnp.stack([out_re, out_im], 1).reshape(rows_here, 2, -1)


def adjoint_terms(u_bases, v_bases, rank_live, portion):
    rows_here = portion.shape[0]
    product = partial(jnp.einsum, preferred_element_type=jnp.float32)
    data_rows = portion.reshape(rows_here, 2, u_bases.shape[0], u_bases.shape[4])
    right_re = v_bases[:, :, 0]
    right_im = v_bases[:, :, 1]
    left_re = u_bases[:, :, 0]
    left_im = u_bases[:, :, 1]
    coef_re = product("pqri,npi->npqr", left_re, data_rows[:, 0]) + product(
        "pqri,npi->npqr", left_im, data_rows[:, 1]
    )
    coef_im = product("pqri,npi->npqr", left_re, data_rows[:, 1]) - product(
        "pqri,npi->npqr", left_im, data_rows[:, 0]
    )
    coef_re = (coef_re * rank_live).astype(jnp.bfloat16)
    coef_im = (coef_im * rank_live).astype(jnp.bfloat16)
    out_re = product("pqri,npqr->nqi", right_re, coef_re) - product(
        "pqri,npqr->nqi", right_im, coef_im
    )
    out_im = product("pqri,npqr->nqi", right_re, coef_im) + product(
        "pqri,npqr->nqi", right_im, coef_re
    )
    return jnp.stack([out_re, out_im], 1).reshape(rows_here, 2, -1)


def body(
    u_bases,
    v_bases,
    tile_ranks,
    u_unit,
    v_unit,
    x_solution,
    w_direction,
    alpha_prev,
    rhobar_prev,
    phibar_prev,
):
    tile_size = u_bases.shape[4]
    rank_live = (
        jnp.arange(u_bases.shape[3], dtype=jnp.int32)[None, None, :] < tile_ranks[:, :, None]
    ).astype(jnp.float32)
    row_devices = lax.axis_size("row")
    col_devices = lax.axis_size(("col", "cplx"))
    rows_total = u_bases.shape[0] * tile_size * row_devices
    cols_total = u_bases.shape[1] * tile_size * col_devices
    total_rhs = v_unit.shape[0] * row_devices
    own_u = u_unit.shape[0]
    u_first = lax.axis_index(("col", "cplx")) * own_u
    own_v = v_unit.shape[0]
    v_first = lax.axis_index("row") * own_v
    partials = forward_terms(
        u_bases,
        v_bases,
        rank_live,
        lax.all_gather(v_unit.astype(jnp.bfloat16), "row", axis=0, tiled=True),
    )
    forward = lax.psum_scatter(
        partials.astype(jnp.bfloat16), ("col", "cplx"), scatter_dimension=0, tiled=True
    ).astype(jnp.float32)
    alpha_own = lax.dynamic_slice_in_dim(alpha_prev, u_first, own_u)
    residual_u = forward - alpha_own[:, None, None] * u_unit
    squares = jnp.zeros((total_rhs,), jnp.float32)
    squares = lax.dynamic_update_slice_in_dim(
        squares, jnp.sum(residual_u * residual_u, axis=(1, 2)), u_first, 0
    )
    squares = lax.psum(squares, ("row", "col", "cplx"))
    beta_all = jnp.sqrt(squares / (2 * rows_total) + epsilon)
    u_next = residual_u / lax.dynamic_slice_in_dim(beta_all, u_first, own_u)[:, None, None]
    unit_all = lax.all_gather(u_next.astype(jnp.bfloat16), ("col", "cplx"), axis=0, tiled=True)
    back = lax.psum_scatter(
        adjoint_terms(u_bases, v_bases, rank_live, unit_all).astype(jnp.bfloat16),
        "row",
        scatter_dimension=0,
        tiled=True,
    ).astype(jnp.float32)
    beta_own = lax.dynamic_slice_in_dim(beta_all, v_first, own_v)
    residual_v = rows_total / cols_total * back - beta_own[:, None, None] * v_unit
    squares_v = jnp.zeros((total_rhs,), jnp.float32)
    squares_v = lax.dynamic_update_slice_in_dim(
        squares_v, jnp.sum(residual_v * residual_v, axis=(1, 2)), v_first, 0
    )
    squares_v = lax.psum(squares_v, ("row", "col", "cplx"))
    alpha_next = jnp.sqrt(squares_v / (2 * cols_total) + epsilon)
    v_next = residual_v / lax.dynamic_slice_in_dim(alpha_next, v_first, own_v)[:, None, None]
    rho_all = jnp.sqrt(rhobar_prev * rhobar_prev + beta_all * beta_all)
    cosine = rhobar_prev / rho_all
    sine = beta_all / rho_all
    theta = sine * alpha_next
    rhobar_next = -cosine * alpha_next
    phi_all = cosine * phibar_prev
    phibar_next = sine * phibar_prev
    step_x = lax.dynamic_slice_in_dim(phi_all / rho_all, v_first, own_v)
    step_w = lax.dynamic_slice_in_dim(theta / rho_all, v_first, own_v)
    x_next = x_solution + step_x[:, None, None] * w_direction
    w_next = v_next - step_w[:, None, None] * w_direction
    return (x_next, w_next, u_next, v_next, alpha_next, rhobar_next, phibar_next)


def solution(mesh):
    placed = (
        P(("freq", "row"), ("col", "cplx"), None, None, None),
        P(("freq", "row"), ("col", "cplx"), None, None, None),
        P(("freq", "row"), ("col", "cplx")),
        P(("freq", "col", "cplx"), None, "row"),
        P(("freq", "row"), None, ("col", "cplx")),
        P(("freq", "row"), None, ("col", "cplx")),
        P(("freq", "row"), None, ("col", "cplx")),
        P("freq"),
        P("freq"),
        P("freq"),
    )
    return jax.shard_map(
        body,
        mesh=mesh,
        in_specs=placed,
        out_specs=(
            P(("freq", "row"), None, ("col", "cplx")),
            P(("freq", "row"), None, ("col", "cplx")),
            P(("freq", "col", "cplx"), None, "row"),
            P(("freq", "row"), None, ("col", "cplx")),
            P("freq"),
            P("freq"),
            P("freq"),
        ),
        check_vma=False,
    )
```

profile of v0, /device:TPU:0, one launch (start us, length us, event | category | flops | bytes accessed | tf_op | source)
XLA Modules:
  0.0 146.6 jit_solution(3353079348399629683)
XLA Ops:
  7.2 0.6 copy-done.11
  7.9 0.9 convert_element_type.46
  8.8 15.1 %all_gather.6 = bf16[32,2,1024]{2,1,0:T(2,128)(2,1)S(1)} all-gather(bf16[8,2,1024]{2,1,0:T(2,128)(2,1)S(1)} %convert_element_type.46), channel_id=1, replica_groups=mesh['freq'=2,'row'=4,'col'=2,'cplx'=2] {'row'}, dimensions={0}, use_global_device_ids=true | all-gather | bytes 163840 | tf_op jit(solution)/shard_map/all_gather | solution.py:90
  24.6 0.2 fusion.21
  24.8 0.4 copy-done
  25.9 0.6 copy.66
  26.6 0.6 copy-done.12
  27.4 20.1 %reduce-scatter.7.cloned.1.call-done = bf16[8,1024]{1,0:T(8,128)(2,1)} async-done(((bf16[32,1024]{1,0:T(8,128)(2,1)}), bf16[8,1024]{1,0:T(8,128)(2,1)}) %reduce-scatter.7.cloned.1.call-update) | async-done | bytes 16400
  47.5 1.0 multiply_reduce_fusion.1
  48.5 0.2 dynamic_update_slice.6
  48.7 31.9 %psum.14 = f32[32]{0:T(128)S(1)} all-reduce(f32[32]{0:T(128)S(1)} %dynamic_update_slice.6), channel_id=1, replica_groups=mesh['freq'=2,'row'=4,'col'=2,'cplx'=2] {'row','col','cplx'}, use_global_device_ids=true, to_apply=%region_2.0 | all-reduce | flops 32 | bytes 256 | tf_op jit(solution)/shard_map/psum | solution.py:101
  80.6 0.5 fusion.66
  81.3 5.2 %all_gather.7 = bf16[32,2,512]{2,0,1:T(8,128)(2,1)S(1)} all-gather(bf16[8,2,512]{2,0,1:T(8,128)(2,1)S(1)} %get-tuple-element.36), channel_id=1, replica_groups=mesh['freq'=2,'row'=4,'col'=2,'cplx'=2] {'col','cplx'}, dimensions={0}, use_global_device_ids=true | all-gather | bytes 81920 | tf_op jit(solution)/shard_map/all_gather | solution.py:104
  88.2 0.7 copy.67
  88.9 0.6 copy.51
  89.6 15.9 %reduce-scatter.9.cloned.1.call-done = bf16[8,2048]{1,0:T(8,128)(2,1)} async-done(((bf16[32,2048]{1,0:T(8,128)(2,1)}), bf16[8,2048]{1,0:T(8,128)(2,1)}) %reduce-scatter.9.cloned.1.call-update) | async-done | bytes 32784
  105.5 1.0 multiply_reduce_fusion
  106.5 0.2 dynamic_update_slice.7
  106.8 29.5 %psum.15 = f32[32]{0:T(128)S(1)} all-reduce(f32[32]{0:T(128)S(1)} %dynamic_update_slice.7), channel_id=1, replica_groups=mesh['freq'=2,'row'=4,'col'=2,'cplx'=2] {'row','col','cplx'}, use_global_device_ids=true, to_apply=%region_5.0 | all-reduce | flops 32 | bytes 256 | tf_op jit(solution)/shard_map/psum | solution.py:117
  136.3 0.5 negate_multiply_fusion
  136.9 0.4 copy-done.10
  137.5 0.7 copy.50
  138.2 0.7 copy.52
  139.0 0.7 multiply_add_fusion
  (60 shorter events, 3.9 us)
Async XLA Ops:
  7.2 0.7 copy-start.11
  7.2 16.8 %copy-start.1 = (bf16[1,2,2,128,512]{4,3,2,1,0:T(8,128)(2,1)S(1)}, bf16[1,2,2,128,512]{4,3,2,1,0:T(8,128)(2,1)}, u32[]{:S(2)}) copy-start(bf16[1,2,2,128,512]{4,3,2,1,0:T(8,128)(2,1)} %param.11) | copy-start | bytes 1572868
  7.2 40.3 %reduce-scatter.7.cloned.1.call-start = ((), (), s32[]{:S(2)}) async-start(), calls=%async_computation.2 | async-start | bytes 81920
  24.2 1.1 copy-start
  26.6 20.9 %copy-start.5 = (f32[8,2,512]{2,1,0:T(2,128)S(1)}, f32[8,2,512]{2,1,0:T(2,128)}, u32[]{:S(2)}) copy-start(f32[8,2,512]{2,1,0:T(2,128)} %param.13) | copy-start | bytes 98308
  26.6 78.9 %reduce-scatter.9.cloned.1.call-start = ((), (), s32[]{:S(2)}) async-start(), calls=%async_computation.3 | async-start | bytes 163840
  26.6 0.7 copy-start.12
  47.5 33.7 %copy-start.7 = (bf16[8,1024]{1,0:T(8,128)(2,1)S(1)}, bf16[8,1024]{1,0:T(8,128)(2,1)}, u32[]{:S(2)}) copy-start(bf16[8,1024]{1,0:T(8,128)(2,1)} %reduce-scatter.7.cloned.1.call-done) | copy-start | bytes 49156
  48.7 31.9 %copy-start.8 = (f32[32]{0:T(128)S(1)}, f32[32]{0:T(128)}, u32[]{:S(2)}) copy-start(f32[32]{0:T(128)} %param.19) | copy-start | bytes 388
  48.7 31.9 %copy-start.9 = (f32[32]{0:T(128)S(1)}, f32[32]{0:T(128)}, u32[]{:S(2)}) copy-start(f32[32]{0:T(128)} %param.18) | copy-start | bytes 388
  88.9 16.6 %copy-start.2 = (f32[8,2,1024]{2,1,0:T(2,128)S(1)}, f32[8,2,1024]{2,1,0:T(2,128)}, u32[]{:S(2)}) copy-start(f32[8,2,1024]{2,1,0:T(2,128)} %param.14) | copy-start | bytes 196612
  89.6 47.8 %copy-start.3 = (f32[8,2,1024]{2,1,0:T(2,128)S(1)}, f32[8,2,1024]{2,1,0:T(2,128)}, u32[]{:S(2)}) copy-start(f32[8,2,1024]{2,1,0:T(2,128)} %param.16) | copy-start | bytes 196612
  105.5 31.9 %copy-start.4 = (bf16[8,2048]{1,0:T(8,128)(2,1)S(1)}, bf16[8,2048]{1,0:T(8,128)(2,1)}, u32[]{:S(2)}) copy-start(bf16[8,2048]{1,0:T(8,128)(2,1)} %reduce-scatter.9.cloned.1.call-done) | copy-start | bytes 98308
  136.8 0.5 copy-start.10
  138.2 0.8 copy-start.6
Sparse Core Ops, SparseCore 0:
  26.7 20.7 reduce-scatter.6
  89.1 16.4 reduce-scatter.8
where the time goes:
time: 147 us
  blocking collectives  81.6 us (56%)
  waiting for transfers between devices  36.1 us (25%)
  between operations  14.2 us (10%)
  local copies, waits for them, and re-layouts  6.78 us (5%)
  other arithmetic  4.93 us (3%)
  matrix products  2.81 us (2%)
    unnamed x4, waiting for transfers between devices  36.1 us
    psum x1, blocking collectives, body(): squares = lax.psum(squares, ('row', 'col', 'cplx'))  31.9 us
    psum x1, blocking collectives, body(): squares_v = lax.psum(squares_v, ('row', 'col', 'cplx'))  29.5 us
    all_gather x1, blocking collectives, body(): lax.all_gather(v_unit.astype(jnp.bfloat16), 'row', axis=0, tiled=True)  15.1 us
    unnamed x31, local copies, waits for them, and re-layouts  5.54 us
    all_gather x1, blocking collectives, body(): lax.all_gather(u_next.astype(jnp.bfloat16), ('col', 'cplx'), axis=0, tile...  5.23 us
  transfers between devices with their start and end apart: 2, of which 2 were waited for; matrix products, arithmetic and copies ran while one was open for 0% of the time, Pallas kernels for 0%

commit v1 on v0

v1 whole, which is shorter than its diff:
```python
from functools import partial

import jax
import jax.numpy as jnp
from jax import lax
from jax.experimental import pallas as pl
from jax.experimental.pallas import tpu as pltpu
from jax.sharding import PartitionSpec as P

epsilon = 1e-06
shrink = 2.0**-20
f32 = jnp.float32
bf16 = jnp.bfloat16


def call(kernel, outs, *args, scratch=()):
    in_specs = [
        pl.BlockSpec(memory_space=pltpu.SMEM if a.dtype == jnp.int32 else pltpu.VMEM) for a in args
    ]
    return pl.pallas_call(
        kernel,
        out_shape=[jax.ShapeDtypeStruct(s, d) for s, d in outs],
        in_specs=in_specs,
        out_specs=[pl.BlockSpec(memory_space=pltpu.VMEM)] * len(outs),
        scratch_shapes=list(scratch),
        compiler_params=pltpu.CompilerParams(vmem_limit_bytes=40 * 2**20),
    )(*args)


def iota(shape, dim):
    return lax.broadcasted_iota(jnp.int32, shape, dim)


def to_lanes(column, place, lanes):
    rows = column.shape[0]
    here = iota((rows, lanes), 1) == place
    return jnp.sum(jnp.where(here, column, 0.0), axis=0, keepdims=True)


def to_column(lane_values, first, rows):
    lanes = lane_values.shape[1]
    here = iota((rows, lanes), 1) == iota((rows, lanes), 0) + first
    return jnp.sum(jnp.where(here, lane_values, 0.0), axis=1, keepdims=True)


def dot(a, b, transposed):
    return lax.dot_general(a, b, (((1,), (1 if transposed else 0,)), ((), ())), preferred_element_type=f32)


def through(inner, outer, ranks_ref, x, own):
    total = []
    tiles, _, ranks, size = inner.shape[1:]
    for q in range(tiles):
        g = dot(x(q), inner[0, q].reshape(2 * ranks, size), True)
        rows = g.shape[0]
        g = g.reshape(rows // (2 * own), 2, own, 2 * ranks)
        live = iota((1, 1, ranks), 2) < ranks_ref[0, q]
        re = jnp.where(live, g[:, 0, :, :ranks] + g[:, 1, :, ranks:], 0.0)
        im = jnp.where(live, g[:, 1, :, :ranks] - g[:, 0, :, ranks:], 0.0)
        both = jnp.stack([jnp.concatenate([re, -im], 2), jnp.concatenate([im, re], 2)], 1)
        both = both.reshape(rows, 2 * ranks).astype(bf16)
        total.append(dot(both, outer[0, q].reshape(2 * ranks, size), False))
    return total


def pack_kernel(v_ref, out_ref):
    own = v_ref.shape[0]
    out_ref[...] = jnp.concatenate([v_ref[:, 0, :], v_ref[:, 1, :]], 0).astype(bf16)


def forward_kernel(n_row, own_v, own_u, where_ref, ranks_ref, u_bases, v_bases, u_ref, alpha_ref, *refs):
    blocks, (low_ref, own_ref, total) = refs[:n_row], refs[n_row:]
    p, c = where_ref[0], where_ref[1]
    size = v_bases.shape[4]
    x = jnp.concatenate([b[...] for b in blocks], 0)
    parts = through(v_bases, u_bases, ranks_ref, lambda q: x[:, q * size : (q + 1) * size], own_v)
    total[...] = sum(parts[1:], parts[0])
    many = own_u // own_v
    for b in range(many):
        at = pl.ds(pl.multiple_of(((c * many + b) ^ p) * 2 * own_v, 2 * own_v), 2 * own_v)
        alpha = to_column(alpha_ref[...], c * own_u + b * own_v, own_v)
        mine = slice(b * own_v, (b + 1) * own_v)
        shift = jnp.concatenate([alpha * u_ref[mine, 0, :], alpha * u_ref[mine, 1, :]], 0)
        left = total[at, :] - shift
        own_ref[b * 2 * own_v : (b + 1) * 2 * own_v, :] = left
        total[at, :] = left
    low_ref[...] = total[...].astype(bf16)


def adjoint_kernel(n_row, n_got, own_v, own_u, lanes, where_ref, ranks_ref, u_bases, v_bases, own_ref, sum_ref, *refs):
    got, outs, own_out, total = refs[:n_got], refs[n_got : n_got + n_row], refs[n_got + n_row], refs[-1]
    p, c = where_ref[0], where_ref[1]
    many = own_u // own_v
    for b in range(many):
        at = pl.ds(pl.multiple_of(((c * many + b) ^ p) * 2 * own_v, 2 * own_v), 2 * own_v)
        mine = slice(b * 2 * own_v, (b + 1) * 2 * own_v)
        acc = own_ref[mine, :]
        for g in got:
            acc = acc + g[at, :].astype(f32)
        own_out[mine, :] = acc
    res = sum_ref[...].astype(f32) + got[-1][...].astype(f32)
    rows = res.shape[0]
    squares = jnp.sum(res * res, axis=1, keepdims=True)
    row = iota((rows, 1), 0)
    place = ((row // (2 * own_v)) ^ p) * own_v + row % own_v
    beta2 = to_lanes(squares, place, lanes)
    high = beta2.astype(bf16)
    low = (beta2 - high.astype(f32)).astype(bf16)
    tail = jnp.where(iota((2 * own_v, lanes), 0) == 0, high.astype(f32), low.astype(f32)).astype(bf16)
    x = (res * shrink).astype(bf16)
    parts = through(u_bases, v_bases, ranks_ref, lambda q: x, own_v)
    wide = parts[0].shape[1]
    for k, out in enumerate(outs):
        for q, part in enumerate(parts):
            out[:, q * wide : (q + 1) * wide] = part[k * 2 * own_v : (k + 1) * 2 * own_v].astype(bf16)
        out[:, len(parts) * wide :] = tail


def pairs(values):
    while len(values) > 1:
        values = [a + b for a, b in zip(values[::2], values[1::2])]
    return values[0]


def residual_kernel(n_row, rows_total, cols_total, lanes, where_ref, v_ref, *refs):
    blocks, (res_ref, beta_ref, norm_ref) = refs[:n_row], refs[n_row:]
    p = where_ref[0]
    own_v, _, wide = v_ref.shape
    beta2 = pairs([b[0:1, wide:].astype(f32) + b[1:2, wide:].astype(f32) for b in blocks])
    beta = jnp.sqrt(beta2 / (2 * rows_total) + epsilon)
    beta_ref[...] = beta
    mine = to_column(beta, p * own_v, own_v)
    scale = rows_total / cols_total / shrink / mine
    squares = None
    for i in range(2):
        half = slice(i * own_v, (i + 1) * own_v)
        back = pairs([b[half, :wide].astype(f32) for b in blocks])
        res = scale * back - mine * v_ref[:, i, :]
        res_ref[half, :] = res
        here = jnp.sum(res * res, axis=1, keepdims=True)
        squares = here if squares is None else squares + here
    place = iota((own_v, 1), 0) + p * own_v
    norm_ref[...] = jnp.broadcast_to(to_lanes(squares, place, lanes), norm_ref.shape)


def update_kernel(
    cols_total,
    where_ref,
    norms_ref,
    beta_ref,
    res_ref,
    own_ref,
    x_ref,
    w_ref,
    rhobar_ref,
    phibar_ref,
    x_out,
    w_out,
    u_out,
    v_out,
    alpha_out,
    rhobar_out,
    phibar_out,
):
    p, c = where_ref[0], where_ref[1]
    own_v = x_ref.shape[0]
    own_u = u_out.shape[0]
    many = own_u // own_v
    rhs = alpha_out.shape[1]
    beta = beta_ref[:, :rhs]
    rhobar, phibar = rhobar_ref[...], phibar_ref[...]
    alpha2 = jnp.sum(norms_ref[...], axis=0, keepdims=True)[:, :rhs]
    alpha = jnp.sqrt(alpha2 / (2 * cols_total) + epsilon)
    rho = jnp.sqrt(rhobar * rhobar + beta * beta)
    cosine = rhobar / rho
    sine = beta / rho
    alpha_out[...] = alpha
    rhobar_out[...] = -cosine * alpha
    phibar_out[...] = sine * phibar
    step_x = to_column(cosine * phibar / rho, p * own_v, own_v)
    step_w = to_column(sine * alpha / rho, p * own_v, own_v)
    alpha_own = to_column(alpha, p * own_v, own_v)
    for i in range(2):
        w = w_ref[:, i, :]
        v = res_ref[i * own_v : (i + 1) * own_v, :] / alpha_own
        x_out[:, i, :] = x_ref[:, i, :] + step_x * w
        v_out[:, i, :] = v
        w_out[:, i, :] = v - step_w * w
    for b in range(many):
        beta_own = to_column(beta, c * own_u + b * own_v, own_v)
        for i in range(2):
            u = own_ref[(2 * b + i) * own_v : (2 * b + i + 1) * own_v, :]
            u_out[b * own_v : (b + 1) * own_v, i, :] = u / beta_own


def flip(x, axes, mask):
    return lax.ppermute(x, axes, [(i, i ^ mask) for i in range(lax.axis_size(axes))])


def body(
    u_bases,
    v_bases,
    tile_ranks,
    u_unit,
    v_unit,
    x_solution,
    w_direction,
    alpha_prev,
    rhobar_prev,
    phibar_prev,
):
    tile_size = u_bases.shape[4]
    n_row = lax.axis_size("row")
    n_cplx = lax.axis_size("cplx")
    n_cols = lax.axis_size(("col", "cplx"))
    rows_total = tile_size * n_row
    cols_total = u_bases.shape[1] * tile_size * n_cols
    own_u, own_v = u_unit.shape[0], v_unit.shape[0]
    wide = v_unit.shape[2]
    rhs = own_v * n_row
    lanes = -(-rhs // 128) * 128
    block = 2 * own_v
    where = jnp.stack([lax.axis_index("row"), lax.axis_index(("col", "cplx"))]).astype(jnp.int32)

    (v_low,) = call(pack_kernel, [((block, wide), bf16)], v_unit)
    blocks = [v_low] + [flip(v_low, "row", k) for k in range(1, n_row)]
    low, own = call(
        partial(forward_kernel, n_row, own_v, own_u),
        [((2 * rhs, tile_size), bf16), ((2 * own_u, tile_size), f32)],
        where,
        tile_ranks,
        u_bases,
        v_bases,
        u_unit,
        alpha_prev[None],
        *blocks,
        scratch=[pltpu.VMEM((2 * rhs, tile_size), f32)],
    )
    got = [flip(low, "cplx", 1)]
    mask = n_cplx
    while mask < n_cols:
        low = (low.astype(f32) + got[-1].astype(f32)).astype(bf16)
        got.append(flip(low, ("col", "cplx"), mask + 1))
        mask *= 2
    *outs, own = call(
        partial(adjoint_kernel, n_row, len(got), own_v, own_u, lanes),
        [((block, wide + lanes), bf16)] * n_row + [((2 * own_u, tile_size), f32)],
        where,
        tile_ranks,
        u_bases,
        v_bases,
        own,
        low,
        *got,
        scratch=[pltpu.VMEM((8, 128), f32)],
    )
    blocks = [outs[0]] + [flip(outs[k], "row", k) for k in range(1, n_row)]
    devices = n_row * n_cols
    residual_v, beta, norms = call(
        partial(residual_kernel, n_row, rows_total, cols_total, lanes),
        [((block, wide), f32), ((1, lanes), f32), ((devices, lanes), f32)],
        where,
        v_unit,
        *blocks,
    )
    norms = lax.all_to_all(norms[:, None], ("row", "col", "cplx"), 0, 0)[:, 0]
    x_next, w_next, u_next, v_next, alpha, rhobar, phibar = call(
        partial(update_kernel, cols_total),
        [(x_solution.shape, f32), (w_direction.shape, f32), (u_unit.shape, f32), (v_unit.shape, f32)] + [((1, rhs), f32)] * 3,
        where,
        norms,
        beta,
        residual_v,
        own,
        x_solution,
        w_direction,
        rhobar_prev[None],
        phibar_prev[None],
    )
    return (x_next, w_next, u_next, v_next, alpha[0], rhobar[0], phibar[0])


def solution(mesh):
    placed = (
        P(("freq", "row"), ("col", "cplx"), None, None, None),
        P(("freq", "row"), ("col", "cplx"), None, None, None),
        P(("freq", "row"), ("col", "cplx")),
        P(("freq", "col", "cplx"), None, "row"),
        P(("freq", "row"), None, ("col", "cplx")),
        P(("freq", "row"), None, ("col", "cplx")),
        P(("freq", "row"), None, ("col", "cplx")),
        P("freq"),
        P("freq"),
        P("freq"),
    )
    return jax.shard_map(
        body,
        mesh=mesh,
        in_specs=placed,
        out_specs=(
            P(("freq", "row"), None, ("col", "cplx")),
            P(("freq", "row"), None, ("col", "cplx")),
            P(("freq", "col", "cplx"), None, "row"),
            P(("freq", "row"), None, ("col", "cplx")),
            P("freq"),
            P("freq"),
            P("freq"),
        ),
        check_vma=False,
    )
```

time: 147 us -> 43.1 us (0.29)
  blocking collectives: 81.6 us -> 10.8 us
  waiting for transfers between devices: 36.1 us -> 11.6 us
  between operations: 14.2 us -> 0.72 us
  starting transfers between devices: 0.08 us -> 11.6 us
  other arithmetic: 4.93 us -> 0.1 us
  Pallas kernels: 0 us -> 4.36 us
  local copies, waits for them, and re-layouts: 6.78 us -> 3.6 us
  matrix products: 2.81 us -> 0 us
    psum x2 -> x0, blocking collectives: 61.4 us -> none  [the longest x1 31.9 us: body(): squares = lax.psum(squares, ('row', 'col', 'cplx'))]
    unnamed x4 -> x0, waiting for transfers between devices: 36.1 us -> none
    all_gather x2 -> x0, blocking collectives: 20.3 us -> none  [the longest x1 15.1 us: body(): lax.all_gather(v_unit.astype(jnp.bfloat16), 'row', axis=0, tiled=True)]
    ppermute x0 -> x8, waiting for transfers between devices: none -> 11.6 us  [flip(): lax.ppermute(x, axes, [(i, i ^ mask) for i in range(lax.axis_size(axes))])]
    ppermute x0 -> x8, starting transfers between devices: none -> 11.6 us  [flip(): lax.ppermute(x, axes, [(i, i ^ mask) for i in range(lax.axis_size(axes))])]
    all_to_all x0 -> x1, blocking collectives: none -> 10.8 us  [body(): norms = lax.all_to_all(norms[:, None], ('row', 'col', 'cplx'), 0, 0)[:, 0]]
    pallas_call x0 -> x5, Pallas kernels: none -> 4.36 us  [call(): pl.pallas_call(kernel, out_shape=[jax.ShapeDtypeStruct(s, d) for s, d in...]
    dot_general x16 -> x0, matrix products: 2.81 us -> none  [the longest x1 0.23 us: forward_terms(): product('pqri,nqi->npqr', right_im, columns[:, 0])]
  transfers between devices with their start and end apart: 2 -> 8, of which waited for: 2 -> 6; matrix products, arithmetic and copies ran while one was open for 0% -> 0% of each run, Pallas kernels for 0% -> 0%
where the time goes in v1:
time: 43.1 us; the launch traced here: 42.8 us
  starting transfers between devices  11.6 us (27%)
  waiting for transfers between devices  11.6 us (27%)
  blocking collectives  10.8 us (25%)
  Pallas kernels  4.36 us (10%)
  local copies, waits for them, and re-layouts  3.6 us (8%)
  between operations  0.72 us (2%)
    ppermute x8, waiting for transfers between devices, flip(): lax.ppermute(x, axes, [(i, i ^ mask) for i in range(lax.axis_size(axes))])  11.6 us
    ppermute x8, starting transfers between devices, flip(): lax.ppermute(x, axes, [(i, i ^ mask) for i in range(lax.axis_size(axes))])  11.6 us
    all_to_all x1, blocking collectives, body(): norms = lax.all_to_all(norms[:, None], ('row', 'col', 'cplx'), 0, 0)[:, 0]  10.8 us
    pallas_call x5, Pallas kernels, call(): pl.pallas_call(kernel, out_shape=[jax.ShapeDtypeStruct(s, d) for s, d in...  4.36 us
    unnamed x26, local copies, waits for them, and re-layouts  3.6 us
  transfers between devices with their start and end apart: 8, of which 6 were waited for; matrix products, arithmetic and copies ran while one was open for 0% of the time, Pallas kernels for 0%

profile of v1, /device:TPU:0, one launch (start us, length us, event | category | flops | bytes accessed | tf_op | source)
XLA Modules:
  0.0 42.8 jit_solution(14564010232300484743)
XLA Ops:
  0.6 0.8 %copy-done.4 = f32[8,2,1024]{2,1,0:T(2,128)S(1)} copy-done((f32[8,2,1024]{2,1,0:T(2,128)S(1)}, f32[8,2,1024]{2,1,0:T(2,128)}, u32[]{:S(2)}) %copy-start.4) | copy-done | bytes 65560
  1.5 5.1 %collective-permute-start.2 = (bf16[16,1024]{1,0:T(8,128)(2,1)S(1)}, bf16[16,1024]{1,0:T(8,128)(2,1)S(1)}, u32[]{:S(2)}, u32[]{:S(2)}) collective-permute-start(bf16[16,1024]{1,0:T(8,128)(2,1)S(1)} %shard_map.153.refs_0_), channel_id=1, source_target_pairs={{0,12},{4,8},{8,4},{12,0},{1,13},{5,9},{9,5},{13,1},{2,14},{6,10},... | collective-permute-start | bytes 98312 | tf_op jit(solution)/shard_map/ppermute | solution.py:197
  6.6 0.6 %collective-permute-start = (bf16[16,1024]{1,0:T(8,128)(2,1)S(1)}, bf16[16,1024]{1,0:T(8,128)(2,1)S(1)}, u32[]{:S(2)}, u32[]{:S(2)}) collective-permute-start(bf16[16,1024]{1,0:T(8,128)(2,1)S(1)} %shard_map.153.refs_0_), channel_id=1, source_target_pairs={{0,4},{4,0},{8,12},{12,8},{1,5},{5,1},{9,13},{13,9},{2,6},{6,2},{1... | collective-permute-start | bytes 98312 | tf_op jit(solution)/shard_map/ppermute | solution.py:197
  7.3 0.1 pad_add_fusion.where_ref
  7.3 1.2 %collective-permute-done.2.refs_3_ = bf16[16,1024]{1,0:T(8,128)(2,1)S(1)} collective-permute-done((bf16[16,1024]{1,0:T(8,128)(2,1)S(1)}, bf16[16,1024]{1,0:T(8,128)(2,1)S(1)}, u32[]{:S(2)}, u32[]{:S(2)}) %collective-permute-start.2) | collective-permute-done | bytes 32800 | tf_op jit(solution)/shard_map/ppermute | solution.py:197
  8.5 2.9 %collective-permute-done.1.refs_2_ = bf16[16,1024]{1,0:T(8,128)(2,1)S(1)} collective-permute-done((bf16[16,1024]{1,0:T(8,128)(2,1)S(1)}, bf16[16,1024]{1,0:T(8,128)(2,1)S(1)}, u32[]{:S(2)}, u32[]{:S(2)}) %collective-permute-start.1) | collective-permute-done | bytes 32800 | tf_op jit(solution)/shard_map/ppermute | solution.py:197
  11.5 1.0 %copy-done = bf16[1,2,2,128,512]{4,3,2,1,0:T(8,128)(2,1)S(1)} copy-done((bf16[1,2,2,128,512]{4,3,2,1,0:T(8,128)(2,1)S(1)}, bf16[1,2,2,128,512]{4,3,2,1,0:T(8,128)(2,1)}, u32[]{:S(2)}) %copy-start) | copy-done | bytes 524312
  12.5 1.0 %copy-done.2 = bf16[1,2,2,128,512]{4,3,2,1,0:T(8,128)(2,1)S(1)} copy-done((bf16[1,2,2,128,512]{4,3,2,1,0:T(8,128)(2,1)S(1)}, bf16[1,2,2,128,512]{4,3,2,1,0:T(8,128)(2,1)}, u32[]{:S(2)}) %copy-start.2) | copy-done | bytes 524312
  13.5 1.0 %shard_map.154 = (bf16[64,512]{1,0:T(8,128)(2,1)S(1)}, f32[16,512]{1,0:T(8,128)S(1)}) custom-call(s32[2]{0:T(128)S(1)} %pad_add_fusion.where_ref, s32[1,2]{1,0:T(1,128)S(1)} %copy-done.9, bf16[1,2,2,128,512]{4,3,2,1,0:T(8,128)(2,1)S(1)} %copy-done, bf16[1,2,2,128,512]{4,3,2,1,0:T(8,128)(2,1)S(1)} %copy-done.2, f32[8,2,512]{2,1,0:T(2,128)S(1)} %copy-done.8, ...), custom_call_target="tpu_custom_call" | custom-call | tf_op jit(solution)/shard_map/pallas_call | solution.py:20
  14.5 0.1 collective-permute-start.3
  14.6 1.2 %collective-permute-done.3.refs_0_ = bf16[64,512]{1,0:T(8,128)(2,1)S(1)} collective-permute-done((bf16[64,512]{1,0:T(8,128)(2,1)S(1)}, bf16[64,512]{1,0:T(8,128)(2,1)S(1)}, u32[]{:S(2)}, u32[]{:S(2)}) %collective-permute-start.3) | collective-permute-done | bytes 65568 | tf_op jit(solution)/shard_map/ppermute | solution.py:197
  15.9 1.3 %collective-permute-start.4 = (bf16[64,512]{1,0:T(8,128)(2,1)S(1)}, bf16[64,512]{1,0:T(8,128)(2,1)S(1)}, u32[]{:S(2)}, u32[]{:S(2)}) collective-permute-start(bf16[64,512]{1,0:T(8,128)(2,1)S(1)} %add_convert_fusion.sum_ref), channel_id=1, source_target_pairs={{0,3},{1,2},{2,1},{3,0},{4,7},{5,6},{6,5},{7,4},{8,11},{9,10},{10,... | collective-permute-start | bytes 196616 | tf_op jit(solution)/shard_map/ppermute | solution.py:197
  17.2 2.8 %collective-permute-done.4.refs_1_ = bf16[64,512]{1,0:T(8,128)(2,1)S(1)} collective-permute-done((bf16[64,512]{1,0:T(8,128)(2,1)S(1)}, bf16[64,512]{1,0:T(8,128)(2,1)S(1)}, u32[]{:S(2)}, u32[]{:S(2)}) %collective-permute-start.4) | collective-permute-done | bytes 65568 | tf_op jit(solution)/shard_map/ppermute | solution.py:197
  20.0 1.3 %shard_map.155 = (bf16[16,1152]{1,0:T(8,128)(2,1)S(1)}, bf16[16,1152]{1,0:T(8,128)(2,1)S(1)}, bf16[16,1152]{1,0:T(8,128)(2,1)S(1)}, bf16[16,1152]{1,0:T(8,128)(2,1)S(1)}, f32[16,512]{1,0:T(8,128)S(1)}) custom-call(s32[2]{0:T(128)S(1)} %pad_add_fusion.where_ref, s32[1,2]{1,0:T(1,128)S(1)} %copy-done.9, bf16[1,2,2,128,512]{4,3,2,1,0:T(8,128)(2,1)S(1)} %copy-done.1, ...), custom_call_target="tpu_custom_call" | custom-call | tf_op jit(solution)/shard_map/pallas_call | solution.py:20
  21.3 0.1 collective-permute-start.5
  21.4 2.1 %collective-permute-start.6 = (bf16[16,1152]{1,0:T(8,128)(2,1)S(1)}, bf16[16,1152]{1,0:T(8,128)(2,1)S(1)}, u32[]{:S(2)}, u32[]{:S(2)}) collective-permute-start(bf16[16,1152]{1,0:T(8,128)(2,1)S(1)} %get-tuple-element.28), channel_id=1, source_target_pairs={{0,8},{4,12},{8,0},{12,4},{1,9},{5,13},{9,1},{13,5},{2,10},{6,14},... | collective-permute-start | bytes 110600 | tf_op jit(solution)/shard_map/ppermute | solution.py:197
  23.4 2.3 %collective-permute-start.7 = (bf16[16,1152]{1,0:T(8,128)(2,1)S(1)}, bf16[16,1152]{1,0:T(8,128)(2,1)S(1)}, u32[]{:S(2)}, u32[]{:S(2)}) collective-permute-start(bf16[16,1152]{1,0:T(8,128)(2,1)S(1)} %get-tuple-element.29), channel_id=1, source_target_pairs={{0,12},{4,8},{8,4},{12,0},{1,13},{5,9},{9,5},{13,1},{2,14},{6,10},... | collective-permute-start | bytes 110600 | tf_op jit(solution)/shard_map/ppermute | solution.py:197
  25.7 0.6 %collective-permute-done.6.refs_2_ = bf16[16,1152]{1,0:T(8,128)(2,1)S(1)} collective-permute-done((bf16[16,1152]{1,0:T(8,128)(2,1)S(1)}, bf16[16,1152]{1,0:T(8,128)(2,1)S(1)}, u32[]{:S(2)}, u32[]{:S(2)}) %collective-permute-start.6) | collective-permute-done | bytes 36896 | tf_op jit(solution)/shard_map/ppermute | solution.py:197
  26.3 2.9 %collective-permute-done.7.refs_3_ = bf16[16,1152]{1,0:T(8,128)(2,1)S(1)} collective-permute-done((bf16[16,1152]{1,0:T(8,128)(2,1)S(1)}, bf16[16,1152]{1,0:T(8,128)(2,1)S(1)}, u32[]{:S(2)}, u32[]{:S(2)}) %collective-permute-start.7) | collective-permute-done | bytes 36896 | tf_op jit(solution)/shard_map/ppermute | solution.py:197
  29.2 0.7 %shard_map.156 = (f32[16,1024]{1,0:T(8,128)S(1)}, f32[1,128]{1,0:T(1,128)S(1)}, f32[16,128]{1,0:T(8,128)S(1)}) custom-call(s32[2]{0:T(128)S(1)} %pad_add_fusion.where_ref, f32[8,2,1024]{2,1,0:T(2,128)S(1)} %copy-done.5, bf16[16,1152]{1,0:T(8,128)(2,1)S(1)} %get-tuple-element.26.refs_0_, bf16[16,1152]{1,0:T(8,128)(2,1)S(1)} %collective-permute-done.5.refs_1_, ...), custom_call_target="tpu_custom_call" | custom-call | tf_op jit(solution)/shard_map/pallas_call | solution.py:20
  29.9 10.8 %all_to_all.5 = f32[16,1,128]{2,1,0:T(1,128)S(1)} all-to-all(f32[16,1,128]{2,1,0:T(1,128)S(1)} %bitcast.13), channel_id=1, replica_groups=mesh['freq'=2,'row'=4,'col'=2,'cplx'=2] {'row','col','cplx'}, dimensions={0} | all-to-all | bytes 16384 | tf_op jit(solution)/shard_map/all_to_all | solution.py:266
  40.8 0.6 %copy-done.11 = f32[32]{0:T(128)S(1)} copy-done((f32[32]{0:T(128)S(1)}, f32[32]{0:T(128)}, u32[]{:S(2)}) %copy-start.11) | copy-done | bytes 152
  41.4 0.0 copy-done.12
  41.4 1.3 %shard_map.157 = (f32[8,2,1024]{2,1,0:T(2,128)}, f32[8,2,1024]{2,1,0:T(2,128)}, f32[8,2,512]{2,1,0:T(2,128)}, f32[8,2,1024]{2,1,0:T(2,128)}, f32[1,32]{1,0:T(1,128)}, /*index=5*/f32[1,32]{1,0:T(1,128)}, f32[1,32]{1,0:T(1,128)}) custom-call(s32[2]{0:T(128)S(1)} %pad_add_fusion.where_ref, f32[16,128]{1,0:T(8,128)S(1)} %bitcast.12, ...), custom_call_target="tpu_custom_call" | custom-call | tf_op jit(solution)/shard_map/pallas_call | solution.py:20
  (26 shorter events, 0.1 us)
Async XLA Ops:
  0.6 0.8 %copy-start.4 = (f32[8,2,1024]{2,1,0:T(2,128)S(1)}, f32[8,2,1024]{2,1,0:T(2,128)}, u32[]{:S(2)}) copy-start(f32[8,2,1024]{2,1,0:T(2,128)} %v_ref.3) | copy-start | bytes 196612
  1.5 10.0 %copy-start.8 = (f32[8,2,512]{2,1,0:T(2,128)S(1)}, f32[8,2,512]{2,1,0:T(2,128)}, u32[]{:S(2)}) copy-start(f32[8,2,512]{2,1,0:T(2,128)} %u_ref.1) | copy-start | bytes 98308
  1.5 7.0 %collective-permute-start.2 = (bf16[16,1024]{1,0:T(8,128)(2,1)S(1)}, bf16[16,1024]{1,0:T(8,128)(2,1)S(1)}, u32[]{:S(2)}, u32[]{:S(2)}) collective-permute-start(bf16[16,1024]{1,0:T(8,128)(2,1)S(1)} %shard_map.153.refs_0_), channel_id=1, source_target_pairs={{0,12},{4,8},{8,4},{12,0},{1,13},{5,9},{9,5},{13,1},{2,14},{6,10},... | collective-permute-start | bytes 98312 | tf_op jit(solution)/shard_map/ppermute | solution.py:197
  6.6 4.8 %collective-permute-start.1 = (bf16[16,1024]{1,0:T(8,128)(2,1)S(1)}, bf16[16,1024]{1,0:T(8,128)(2,1)S(1)}, u32[]{:S(2)}, u32[]{:S(2)}) collective-permute-start(bf16[16,1024]{1,0:T(8,128)(2,1)S(1)} %shard_map.153.refs_0_), channel_id=1, source_target_pairs={{0,8},{4,12},{8,0},{12,4},{1,9},{5,13},{9,1},{13,5},{2,10},{6,14},... | collective-permute-start | bytes 98312 | tf_op jit(solution)/shard_map/ppermute | solution.py:197
  6.6 4.8 %collective-permute-start = (bf16[16,1024]{1,0:T(8,128)(2,1)S(1)}, bf16[16,1024]{1,0:T(8,128)(2,1)S(1)}, u32[]{:S(2)}, u32[]{:S(2)}) collective-permute-start(bf16[16,1024]{1,0:T(8,128)(2,1)S(1)} %shard_map.153.refs_0_), channel_id=1, source_target_pairs={{0,4},{4,0},{8,12},{12,8},{1,5},{5,1},{9,13},{13,9},{2,6},{6,2},{1... | collective-permute-start | bytes 98312 | tf_op jit(solution)/shard_map/ppermute | solution.py:197
  7.3 4.1 %copy-start.9 = (s32[1,2]{1,0:T(1,128)S(1)}, s32[1,2]{1,0:T(1,128)}, u32[]{:S(2)}) copy-start(s32[1,2]{1,0:T(1,128)} %ranks_ref.3) | copy-start | bytes 28
  7.3 4.1 %copy-start.10 = (f32[32]{0:T(128)S(1)}, f32[32]{0:T(128)}, u32[]{:S(2)}) copy-start(f32[32]{0:T(128)} %param.17) | copy-start | bytes 388
  11.4 1.0 %copy-start = (bf16[1,2,2,128,512]{4,3,2,1,0:T(8,128)(2,1)S(1)}, bf16[1,2,2,128,512]{4,3,2,1,0:T(8,128)(2,1)}, u32[]{:S(2)}) copy-start(bf16[1,2,2,128,512]{4,3,2,1,0:T(8,128)(2,1)} %u_bases.3) | copy-start | bytes 1572868
  12.5 1.0 %copy-start.2 = (bf16[1,2,2,128,512]{4,3,2,1,0:T(8,128)(2,1)S(1)}, bf16[1,2,2,128,512]{4,3,2,1,0:T(8,128)(2,1)}, u32[]{:S(2)}) copy-start(bf16[1,2,2,128,512]{4,3,2,1,0:T(8,128)(2,1)} %v_bases.3) | copy-start | bytes 1572868
  13.5 6.5 %copy-start.1 = (bf16[1,2,2,128,512]{4,3,2,1,0:T(8,128)(2,1)S(1)}, bf16[1,2,2,128,512]{4,3,2,1,0:T(8,128)(2,1)}, u32[]{:S(2)}) copy-start(bf16[1,2,2,128,512]{4,3,2,1,0:T(8,128)(2,1)} %u_bases.3) | copy-start | bytes 1572868
  13.5 6.5 %copy-start.3 = (bf16[1,2,2,128,512]{4,3,2,1,0:T(8,128)(2,1)S(1)}, bf16[1,2,2,128,512]{4,3,2,1,0:T(8,128)(2,1)}, u32[]{:S(2)}) copy-start(bf16[1,2,2,128,512]{4,3,2,1,0:T(8,128)(2,1)} %v_bases.3) | copy-start | bytes 1572868
  14.5 1.3 %collective-permute-start.3 = (bf16[64,512]{1,0:T(8,128)(2,1)S(1)}, bf16[64,512]{1,0:T(8,128)(2,1)S(1)}, u32[]{:S(2)}, u32[]{:S(2)}) collective-permute-start(bf16[64,512]{1,0:T(8,128)(2,1)S(1)} %get-tuple-element.25), channel_id=1, source_target_pairs={{0,1},{1,0},{2,3},{3,2},{4,5},{5,4},{6,7},{7,6},{8,9},{9,8},{10,11... | collective-permute-start | bytes 196616 | tf_op jit(solution)/shard_map/ppermute | solution.py:197
  15.9 4.1 %collective-permute-start.4 = (bf16[64,512]{1,0:T(8,128)(2,1)S(1)}, bf16[64,512]{1,0:T(8,128)(2,1)S(1)}, u32[]{:S(2)}, u32[]{:S(2)}) collective-permute-start(bf16[64,512]{1,0:T(8,128)(2,1)S(1)} %add_convert_fusion.sum_ref), channel_id=1, source_target_pairs={{0,3},{1,2},{2,1},{3,0},{4,7},{5,6},{6,5},{7,4},{8,11},{9,10},{10,... | collective-permute-start | bytes 196616 | tf_op jit(solution)/shard_map/ppermute | solution.py:197
  20.0 9.2 %copy-start.5 = (f32[8,2,1024]{2,1,0:T(2,128)S(1)}, f32[8,2,1024]{2,1,0:T(2,128)}, u32[]{:S(2)}) copy-start(f32[8,2,1024]{2,1,0:T(2,128)} %v_ref.3) | copy-start | bytes 196612
  21.3 4.5 %collective-permute-start.5 = (bf16[16,1152]{1,0:T(8,128)(2,1)S(1)}, bf16[16,1152]{1,0:T(8,128)(2,1)S(1)}, u32[]{:S(2)}, u32[]{:S(2)}) collective-permute-start(bf16[16,1152]{1,0:T(8,128)(2,1)S(1)} %get-tuple-element.27), channel_id=1, source_target_pairs={{0,4},{4,0},{8,12},{12,8},{1,5},{5,1},{9,13},{13,9},{2,6},{6,2},{1... | collective-permute-start | bytes 110600 | tf_op jit(solution)/shard_map/ppermute | solution.py:197
  21.4 4.9 %collective-permute-start.6 = (bf16[16,1152]{1,0:T(8,128)(2,1)S(1)}, bf16[16,1152]{1,0:T(8,128)(2,1)S(1)}, u32[]{:S(2)}, u32[]{:S(2)}) collective-permute-start(bf16[16,1152]{1,0:T(8,128)(2,1)S(1)} %get-tuple-element.28), channel_id=1, source_target_pairs={{0,8},{4,12},{8,0},{12,4},{1,9},{5,13},{9,1},{13,5},{2,10},{6,14},... | collective-permute-start | bytes 110600 | tf_op jit(solution)/shard_map/ppermute | solution.py:197
  23.4 5.8 %collective-permute-start.7 = (bf16[16,1152]{1,0:T(8,128)(2,1)S(1)}, bf16[16,1152]{1,0:T(8,128)(2,1)S(1)}, u32[]{:S(2)}, u32[]{:S(2)}) collective-permute-start(bf16[16,1152]{1,0:T(8,128)(2,1)S(1)} %get-tuple-element.29), channel_id=1, source_target_pairs={{0,12},{4,8},{8,4},{12,0},{1,13},{5,9},{9,5},{13,1},{2,14},{6,10},... | collective-permute-start | bytes 110600 | tf_op jit(solution)/shard_map/ppermute | solution.py:197
  29.2 11.5 %copy-start.6 = (f32[8,2,1024]{2,1,0:T(2,128)S(1)}, f32[8,2,1024]{2,1,0:T(2,128)}, u32[]{:S(2)}) copy-start(f32[8,2,1024]{2,1,0:T(2,128)} %x_ref.1) | copy-start | bytes 196612
  29.2 11.5 %copy-start.7 = (f32[8,2,1024]{2,1,0:T(2,128)S(1)}, f32[8,2,1024]{2,1,0:T(2,128)}, u32[]{:S(2)}) copy-start(f32[8,2,1024]{2,1,0:T(2,128)} %w_ref.1) | copy-start | bytes 196612
  40.7 0.7 %copy-start.11 = (f32[32]{0:T(128)S(1)}, f32[32]{0:T(128)}, u32[]{:S(2)}) copy-start(f32[32]{0:T(128)} %param.18) | copy-start | bytes 388
  40.7 0.7 %copy-start.12 = (f32[32]{0:T(128)S(1)}, f32[32]{0:T(128)}, u32[]{:S(2)}) copy-start(f32[32]{0:T(128)} %param.19) | copy-start | bytes 388

commit v2 on v1

--- a/solution.py
+++ b/solution.py
@@ -13,9 +13,9 @@
 bf16 = jnp.bfloat16
 
 
-def call(kernel, outs, *args, scratch=()):
+def call(kernel, outs, *args, scratch=(), vmem=12, hbm=False, cost=None):
     in_specs = [
-        pl.BlockSpec(memory_space=pltpu.SMEM if a.dtype == jnp.int32 else pltpu.VMEM) for a in args
+        pl.BlockSpec(memory_space=pltpu.HBM if hbm else pltpu.SMEM if a.dtype == jnp.int32 else pltpu.VMEM) for a in args
     ]
     return pl.pallas_call(
         kernel,
@@ -23,7 +23,8 @@
         in_specs=in_specs,
         out_specs=[pl.BlockSpec(memory_space=pltpu.VMEM)] * len(outs),
         scratch_shapes=list(scratch),
-        compiler_params=pltpu.CompilerParams(vmem_limit_bytes=40 * 2**20),
+        compiler_params=pltpu.CompilerParams(vmem_limit_bytes=vmem * 2**20),
+        cost_estimate=cost,
     )(*args)
 
 
@@ -68,6 +69,15 @@
     out_ref[...] = jnp.concatenate([v_ref[:, 0, :], v_ref[:, 1, :]], 0).astype(bf16)
 
 
+def load_kernel(many, *refs):
+    ins, outs, sems = refs[:many], refs[many:-1], refs[-1]
+    copies = [pltpu.make_async_copy(a, b, sems.at[i]) for i, (a, b) in enumerate(zip(ins, outs))]
+    for copy in copies:
+        copy.start()
+    for copy in copies:
+        copy.wait()
+
+
 def forward_kernel(n_row, own_v, own_u, where_ref, ranks_ref, u_bases, v_bases, u_ref, alpha_ref, *refs):
     blocks, (low_ref, own_ref, total) = refs[:n_row], refs[n_row:]
     p, c = where_ref[0], where_ref[1]
@@ -78,7 +88,7 @@
     many = own_u // own_v
     for b in range(many):
         at = pl.ds(pl.multiple_of(((c * many + b) ^ p) * 2 * own_v, 2 * own_v), 2 * own_v)
-        alpha = to_column(alpha_ref[...], c * own_u + b * own_v, own_v)
+        alpha = to_column(alpha_ref[0:1, :], c * own_u + b * own_v, own_v)
         mine = slice(b * own_v, (b + 1) * own_v)
         shift = jnp.concatenate([alpha * u_ref[mine, 0, :], alpha * u_ref[mine, 1, :]], 0)
         left = total[at, :] - shift
@@ -88,7 +98,7 @@
 
 
 def adjoint_kernel(n_row, n_got, own_v, own_u, lanes, where_ref, ranks_ref, u_bases, v_bases, own_ref, sum_ref, *refs):
-    got, outs, own_out, total = refs[:n_got], refs[n_got : n_got + n_row], refs[n_got + n_row], refs[-1]
+    got, outs, own_out = refs[:n_got], refs[n_got : n_got + n_row], refs[n_got + n_row]
     p, c = where_ref[0], where_ref[1]
     many = own_u // own_v
     for b in range(many):
@@ -124,6 +134,7 @@
 
 def residual_kernel(n_row, rows_total, cols_total, lanes, where_ref, v_ref, *refs):
     blocks, (res_ref, beta_ref, norm_ref) = refs[:n_row], refs[n_row:]
+    blocks = [blocks[0], blocks[-1], *blocks[1:-1]]
     p = where_ref[0]
     own_v, _, wide = v_ref.shape
     beta2 = pairs([b[0:1, wide:].astype(f32) + b[1:2, wide:].astype(f32) for b in blocks])
@@ -140,49 +151,30 @@
         here = jnp.sum(res * res, axis=1, keepdims=True)
         squares = here if squares is None else squares + here
     place = iota((own_v, 1), 0) + p * own_v
-    norm_ref[...] = jnp.broadcast_to(to_lanes(squares, place, lanes), norm_ref.shape)
-
-
-def update_kernel(
-    cols_total,
-    where_ref,
-    norms_ref,
-    beta_ref,
-    res_ref,
-    own_ref,
-    x_ref,
-    w_ref,
-    rhobar_ref,
-    phibar_ref,
-    x_out,
-    w_out,
-    u_out,
-    v_out,
-    alpha_out,
-    rhobar_out,
-    phibar_out,
-):
+    norm_ref[...] = to_lanes(squares, place, lanes)
+
+
+def turn(beta, scalars_ref):
+    rhobar, phibar = scalars_ref[1:2, :], scalars_ref[2:3, :]
+    rho = jnp.sqrt(rhobar * rhobar + beta * beta)
+    return rho, rhobar / rho, beta / rho, phibar
+
+
+def vectors_kernel(cols_total, where_ref, norms_ref, beta_ref, res_ref, own_ref, x_ref, w_ref, scalars_ref, x_out, w_out, u_out, v_out):
     p, c = where_ref[0], where_ref[1]
     own_v = x_ref.shape[0]
     own_u = u_out.shape[0]
     many = own_u // own_v
-    rhs = alpha_out.shape[1]
+    rhs = scalars_ref.shape[1]
     beta = beta_ref[:, :rhs]
-    rhobar, phibar = rhobar_ref[...], phibar_ref[...]
-    alpha2 = jnp.sum(norms_ref[...], axis=0, keepdims=True)[:, :rhs]
+    rho, cosine, sine, phibar = turn(beta, scalars_ref)
+    alpha2 = to_column(norms_ref[...], p * own_v, own_v)
     alpha = jnp.sqrt(alpha2 / (2 * cols_total) + epsilon)
-    rho = jnp.sqrt(rhobar * rhobar + beta * beta)
-    cosine = rhobar / rho
-    sine = beta / rho
-    alpha_out[...] = alpha
-    rhobar_out[...] = -cosine * alpha
-    phibar_out[...] = sine * phibar
     step_x = to_column(cosine * phibar / rho, p * own_v, own_v)
-    step_w = to_column(sine * alpha / rho, p * own_v, own_v)
-    alpha_own = to_column(alpha, p * own_v, own_v)
+    step_w = to_column(sine / rho, p * own_v, own_v) * alpha
     for i in range(2):
         w = w_ref[:, i, :]
-        v = res_ref[i * own_v : (i + 1) * own_v, :] / alpha_own
+        v = res_ref[i * own_v : (i + 1) * own_v, :] / alpha
         x_out[:, i, :] = x_ref[:, i, :] + step_x * w
         v_out[:, i, :] = v
         w_out[:, i, :] = v - step_w * w
@@ -191,6 +183,17 @@
         for i in range(2):
             u = own_ref[(2 * b + i) * own_v : (2 * b + i + 1) * own_v, :]
             u_out[b * own_v : (b + 1) * own_v, i, :] = u / beta_own
+
+
+def scalars_kernel(n_row, cols_total, beta_ref, scalars_ref, *refs):
+    norms, (alpha_out, rhobar_out, phibar_out) = refs[:n_row], refs[n_row:]
+    rhs = scalars_ref.shape[1]
+    rho, cosine, sine, phibar = turn(beta_ref[:, :rhs], scalars_ref)
+    alpha2 = sum([n[...] for n in norms[1:]], norms[0][...])[:, :rhs]
+    alpha = jnp.sqrt(alpha2 / (2 * cols_total) + epsilon)
+    alpha_out[...] = alpha
+    rhobar_out[...] = -cosine * alpha
+    phibar_out[...] = sine * phibar
 
 
 def flip(x, axes, mask):
@@ -222,7 +225,9 @@
     block = 2 * own_v
     where = jnp.stack([lax.axis_index("row"), lax.axis_index(("col", "cplx"))]).astype(jnp.int32)
 
-    (v_low,) = call(pack_kernel, [((block, wide), bf16)], v_unit)
+    vmem = 8 + rhs // 16
+    scalars = jnp.stack([alpha_prev, rhobar_prev, phibar_prev])
+    (v_low,) = call(pack_kernel, [((block, wide), bf16)], v_unit, cost=pl.CostEstimate(flops=10**10, bytes_accessed=2**26, transcendentals=0))
     blocks = [v_low] + [flip(v_low, "row", k) for k in range(1, n_row)]
     low, own = call(
         partial(forward_kernel, n_row, own_v, own_u),
@@ -232,9 +237,10 @@
         u_bases,
         v_bases,
         u_unit,
-        alpha_prev[None],
+        scalars,
         *blocks,
         scratch=[pltpu.VMEM((2 * rhs, tile_size), f32)],
+        vmem=vmem,
     )
     got = [flip(low, "cplx", 1)]
     mask = n_cplx
@@ -252,21 +258,26 @@
         own,
         low,
         *got,
-        scratch=[pltpu.VMEM((8, 128), f32)],
-    )
-    blocks = [outs[0]] + [flip(outs[k], "row", k) for k in range(1, n_row)]
-    devices = n_row * n_cols
+        vmem=vmem,
+    )
+    order = [*range(2, n_row), 1]
+    blocks = [outs[0]] + [flip(outs[k], "row", k) for k in order]
     residual_v, beta, norms = call(
         partial(residual_kernel, n_row, rows_total, cols_total, lanes),
-        [((block, wide), f32), ((1, lanes), f32), ((devices, lanes), f32)],
+        [((block, wide), f32), ((1, lanes), f32), ((1, lanes), f32)],
         where,
         v_unit,
         *blocks,
     )
-    norms = lax.all_to_all(norms[:, None], ("row", "col", "cplx"), 0, 0)[:, 0]
-    x_next, w_next, u_next, v_next, alpha, rhobar, phibar = call(
-        partial(update_kernel, cols_total),
-        [(x_solution.shape, f32), (w_direction.shape, f32), (u_unit.shape, f32), (v_unit.shape, f32)] + [((1, rhs), f32)] * 3,
+    norms = norms + flip(norms, "cplx", 1)
+    mask = n_cplx
+    while mask < n_cols:
+        norms = norms + flip(norms, ("col", "cplx"), mask + 1)
+        mask *= 2
+    norms_all = [norms] + [flip(norms, ("row", "col", "cplx"), k * n_cols + 1) for k in order]
+    x_next, w_next, u_next, v_next = call(
+        partial(vectors_kernel, cols_total),
+        [(x_solution.shape, f32), (w_direction.shape, f32), (u_unit.shape, f32), (v_unit.shape, f32)],
         where,
         norms,
         beta,
@@ -274,8 +285,11 @@
         own,
         x_solution,
         w_direction,
-        rhobar_prev[None],
-        phibar_prev[None],
+        scalars,
+        cost=pl.CostEstimate(flops=10**9, bytes_accessed=2**23, transcendentals=0),
+    )
+    alpha, rhobar, phibar = call(
+        partial(scalars_kernel, n_row, cols_total), [((1, rhs), f32)] * 3, beta, scalars, *norms_all
     )
     return (x_next, w_next, u_next, v_next, alpha[0], rhobar[0], phibar[0])
 

time: 43.1 us -> 38.7 us (0.90)
  blocking collectives: 10.8 us -> 0 us
  waiting for transfers between devices: 11.6 us -> 16.8 us
  starting transfers between devices: 11.6 us -> 15 us
  local copies, waits for them, and re-layouts: 3.6 us -> 0.97 us
  Pallas kernels: 4.36 us -> 4.91 us
    all_to_all x1 -> x0, blocking collectives: 10.8 us -> none  [body(): norms = lax.all_to_all(norms[:, None], ('row', 'col', 'cplx'), 0, 0)[:, 0]]
    ppermute x8 -> x13, waiting for transfers between devices: 11.6 us -> 16.8 us  [flip(): lax.ppermute(x, axes, [(i, i ^ mask) for i in range(lax.axis_size(axes))])]
    ppermute x8 -> x13, starting transfers between devices: 11.6 us -> 15 us  [flip(): lax.ppermute(x, axes, [(i, i ^ mask) for i in range(lax.axis_size(axes))])]
    unnamed x26 -> x22, local copies, waits for them, and re-layouts: 3.6 us -> 0.97 us
    pallas_call x5 -> x6, Pallas kernels: 4.36 us -> 4.91 us  [call(): pl.pallas_call(kernel, out_shape=[jax.ShapeDtypeStruct(s, d) for s, d in...]
  transfers between devices with their start and end apart: 8 -> 13, of which waited for: 6 -> 10; matrix products, arithmetic and copies ran while one was open for 0% -> 0% of each run, Pallas kernels for 0% -> 4%
where the time goes in v2:
time: 38.7 us; the launch traced here: 38.5 us
  waiting for transfers between devices  16.8 us (43%)
  starting transfers between devices  15 us (39%)
  Pallas kernels  4.91 us (13%)
  local copies, waits for them, and re-layouts  0.97 us (3%)
  between operations  0.76 us (2%)
    ppermute x13, waiting for transfers between devices, flip(): lax.ppermute(x, axes, [(i, i ^ mask) for i in range(lax.axis_size(axes))])  16.8 us
    ppermute x13, starting transfers between devices, flip(): lax.ppermute(x, axes, [(i, i ^ mask) for i in range(lax.axis_size(axes))])  15 us
    pallas_call x6, Pallas kernels, call(): pl.pallas_call(kernel, out_shape=[jax.ShapeDtypeStruct(s, d) for s, d in...  4.91 us
    unnamed x22, local copies, waits for them, and re-layouts  0.97 us
  transfers between devices with their start and end apart: 13, of which 10 were waited for; matrix products, arithmetic and copies ran while one was open for 0% of the time, Pallas kernels for 4%

profile of v2, /device:TPU:0, one launch (start us, length us, event | category | flops | bytes accessed | tf_op | source)
XLA Modules:
  0.0 38.5 jit_solution(7684742247312782933)
XLA Ops:
  0.7 0.9 %copy-done.2 = f32[8,2,1024]{2,1,0:T(2,128)S(1)} copy-done((f32[8,2,1024]{2,1,0:T(2,128)S(1)}, f32[8,2,1024]{2,1,0:T(2,128)}, u32[]{:S(2)}) %copy-start.2) | copy-done | bytes 65560
  1.6 5.1 %collective-permute-start.2 = (bf16[16,1024]{1,0:T(8,128)(2,1)S(1)}, bf16[16,1024]{1,0:T(8,128)(2,1)S(1)}, u32[]{:S(2)}, u32[]{:S(2)}) collective-permute-start(bf16[16,1024]{1,0:T(8,128)(2,1)S(1)} %shard_map.153.refs_0_), channel_id=1, source_target_pairs={{0,12},{4,8},{8,4},{12,0},{1,13},{5,9},{9,5},{13,1},{2,14},{6,10},... | collective-permute-start | bytes 98312 | tf_op jit(solution)/shard_map/ppermute | solution.py:200
  6.7 0.6 %collective-permute-start = (bf16[16,1024]{1,0:T(8,128)(2,1)S(1)}, bf16[16,1024]{1,0:T(8,128)(2,1)S(1)}, u32[]{:S(2)}, u32[]{:S(2)}) collective-permute-start(bf16[16,1024]{1,0:T(8,128)(2,1)S(1)} %shard_map.153.refs_0_), channel_id=1, source_target_pairs={{0,4},{4,0},{8,12},{12,8},{1,5},{5,1},{9,13},{13,9},{2,6},{6,2},{1... | collective-permute-start | bytes 98312 | tf_op jit(solution)/shard_map/ppermute | solution.py:200
  7.5 1.1 %collective-permute-done.2.refs_3_ = bf16[16,1024]{1,0:T(8,128)(2,1)S(1)} collective-permute-done((bf16[16,1024]{1,0:T(8,128)(2,1)S(1)}, bf16[16,1024]{1,0:T(8,128)(2,1)S(1)}, u32[]{:S(2)}, u32[]{:S(2)}) %collective-permute-start.2) | collective-permute-done | bytes 32800 | tf_op jit(solution)/shard_map/ppermute | solution.py:200
  8.6 2.9 %collective-permute-done.1.refs_2_ = bf16[16,1024]{1,0:T(8,128)(2,1)S(1)} collective-permute-done((bf16[16,1024]{1,0:T(8,128)(2,1)S(1)}, bf16[16,1024]{1,0:T(8,128)(2,1)S(1)}, u32[]{:S(2)}, u32[]{:S(2)}) %collective-permute-start.1) | collective-permute-done | bytes 32800 | tf_op jit(solution)/shard_map/ppermute | solution.py:200
  11.6 1.0 %shard_map.154 = (bf16[64,512]{1,0:T(8,128)(2,1)S(1)}, f32[16,512]{1,0:T(8,128)S(1)}) custom-call(s32[2]{0:T(128)S(1)} %pad_add_fusion.where_ref, s32[1,2]{1,0:T(1,128)S(1)} %copy-done.5, bf16[1,2,2,128,512]{4,3,2,1,0:T(8,128)(2,1)S(1)} %copy-done, bf16[1,2,2,128,512]{4,3,2,1,0:T(8,128)(2,1)S(1)} %copy-done.1, f32[8,2,512]{2,1,0:T(2,128)S(1)} %copy-done.4, ...), custom_call_target="tpu_custom_call" | custom-call | tf_op jit(solution)/shard_map/pallas_call | solution.py:20
  12.7 1.2 %collective-permute-done.3.refs_0_ = bf16[64,512]{1,0:T(8,128)(2,1)S(1)} collective-permute-done((bf16[64,512]{1,0:T(8,128)(2,1)S(1)}, bf16[64,512]{1,0:T(8,128)(2,1)S(1)}, u32[]{:S(2)}, u32[]{:S(2)}) %collective-permute-start.3) | collective-permute-done | bytes 65568 | tf_op jit(solution)/shard_map/ppermute | solution.py:200
  13.9 1.3 %collective-permute-start.4 = (bf16[64,512]{1,0:T(8,128)(2,1)S(1)}, bf16[64,512]{1,0:T(8,128)(2,1)S(1)}, u32[]{:S(2)}, u32[]{:S(2)}) collective-permute-start(bf16[64,512]{1,0:T(8,128)(2,1)S(1)} %add_convert_fusion.sum_ref), channel_id=1, source_target_pairs={{0,3},{1,2},{2,1},{3,0},{4,7},{5,6},{6,5},{7,4},{8,11},{9,10},{10,... | collective-permute-start | bytes 196616 | tf_op jit(solution)/shard_map/ppermute | solution.py:200
  15.3 2.8 %collective-permute-done.4.refs_1_ = bf16[64,512]{1,0:T(8,128)(2,1)S(1)} collective-permute-done((bf16[64,512]{1,0:T(8,128)(2,1)S(1)}, bf16[64,512]{1,0:T(8,128)(2,1)S(1)}, u32[]{:S(2)}, u32[]{:S(2)}) %collective-permute-start.4) | collective-permute-done | bytes 65568 | tf_op jit(solution)/shard_map/ppermute | solution.py:200
  18.1 1.3 %shard_map.155 = (bf16[16,1152]{1,0:T(8,128)(2,1)S(1)}, bf16[16,1152]{1,0:T(8,128)(2,1)S(1)}, bf16[16,1152]{1,0:T(8,128)(2,1)S(1)}, bf16[16,1152]{1,0:T(8,128)(2,1)S(1)}, f32[16,512]{1,0:T(8,128)S(1)}) custom-call(s32[2]{0:T(128)S(1)} %pad_add_fusion.where_ref, s32[1,2]{1,0:T(1,128)S(1)} %copy-done.5, bf16[1,2,2,128,512]{4,3,2,1,0:T(8,128)(2,1)S(1)} %copy-done, ...), custom_call_target="tpu_custom_call" | custom-call | tf_op jit(solution)/shard_map/pallas_call | solution.py:20
  19.3 2.1 %collective-permute-start.5 = (bf16[16,1152]{1,0:T(8,128)(2,1)S(1)}, bf16[16,1152]{1,0:T(8,128)(2,1)S(1)}, u32[]{:S(2)}, u32[]{:S(2)}) collective-permute-start(bf16[16,1152]{1,0:T(8,128)(2,1)S(1)} %get-tuple-element.27), channel_id=1, source_target_pairs={{0,8},{4,12},{8,0},{12,4},{1,9},{5,13},{9,1},{13,5},{2,10},{6,14},... | collective-permute-start | bytes 110600 | tf_op jit(solution)/shard_map/ppermute | solution.py:200
  21.5 1.3 %collective-permute-start.7 = (bf16[16,1152]{1,0:T(8,128)(2,1)S(1)}, bf16[16,1152]{1,0:T(8,128)(2,1)S(1)}, u32[]{:S(2)}, u32[]{:S(2)}) collective-permute-start(bf16[16,1152]{1,0:T(8,128)(2,1)S(1)} %get-tuple-element.29), channel_id=1, source_target_pairs={{0,4},{4,0},{8,12},{12,8},{1,5},{5,1},{9,13},{13,9},{2,6},{6,2},{1... | collective-permute-start | bytes 110600 | tf_op jit(solution)/shard_map/ppermute | solution.py:200
  22.9 1.7 %collective-permute-done.5.refs_1_ = bf16[16,1152]{1,0:T(8,128)(2,1)S(1)} collective-permute-done((bf16[16,1152]{1,0:T(8,128)(2,1)S(1)}, bf16[16,1152]{1,0:T(8,128)(2,1)S(1)}, u32[]{:S(2)}, u32[]{:S(2)}) %collective-permute-start.5) | collective-permute-done | bytes 36896 | tf_op jit(solution)/shard_map/ppermute | solution.py:200
  24.6 2.5 %collective-permute-done.6.refs_2_ = bf16[16,1152]{1,0:T(8,128)(2,1)S(1)} collective-permute-done((bf16[16,1152]{1,0:T(8,128)(2,1)S(1)}, bf16[16,1152]{1,0:T(8,128)(2,1)S(1)}, u32[]{:S(2)}, u32[]{:S(2)}) %collective-permute-start.6) | collective-permute-done | bytes 36896 | tf_op jit(solution)/shard_map/ppermute | solution.py:200
  27.2 0.7 %shard_map.156 = (f32[16,1024]{1,0:T(8,128)S(1)}, f32[1,128]{1,0:T(1,128)S(1)}, f32[1,128]{1,0:T(1,128)S(1)}) custom-call(s32[2]{0:T(128)S(1)} %pad_add_fusion.where_ref, f32[8,2,1024]{2,1,0:T(2,128)S(1)} %copy-done.3, bf16[16,1152]{1,0:T(8,128)(2,1)S(1)} %get-tuple-element.26.refs_0_, bf16[16,1152]{1,0:T(8,128)(2,1)S(1)} %collective-permute-done.5.refs_1_, ...), custom_call_target="tpu_custom_call" | custom-call | tf_op jit(solution)/shard_map/pallas_call | solution.py:20
  27.9 1.1 %collective-permute-done.8 = f32[1,128]{1,0:T(1,128)S(1)} collective-permute-done((f32[1,128]{1,0:T(1,128)S(1)}, f32[1,128]{1,0:T(1,128)S(1)}, u32[]{:S(2)}, u32[]{:S(2)}) %collective-permute-start.8) | collective-permute-done | bytes 544 | tf_op jit(solution)/shard_map/ppermute | solution.py:200
  29.1 1.3 %collective-permute-start.9 = (f32[1,128]{1,0:T(1,128)S(1)}, f32[1,128]{1,0:T(1,128)S(1)}, u32[]{:S(2)}, u32[]{:S(2)}) collective-permute-start(f32[1,128]{1,0:T(1,128)S(1)} %add.14), channel_id=1, source_target_pairs={{0,3},{1,2},{2,1},{3,0},{4,7},{5,6},{6,5},{7,4},{8,11},{9,10},{10,... | collective-permute-start | bytes 1544 | tf_op jit(solution)/shard_map/ppermute | solution.py:200
  30.4 1.7 %collective-permute-done.9 = f32[1,128]{1,0:T(1,128)S(1)} collective-permute-done((f32[1,128]{1,0:T(1,128)S(1)}, f32[1,128]{1,0:T(1,128)S(1)}, u32[]{:S(2)}, u32[]{:S(2)}) %collective-permute-start.9) | collective-permute-done | bytes 544 | tf_op jit(solution)/shard_map/ppermute | solution.py:200
  32.0 2.1 %collective-permute-start.11 = (f32[1,128]{1,0:T(1,128)S(1)}, f32[1,128]{1,0:T(1,128)S(1)}, u32[]{:S(2)}, u32[]{:S(2)}) collective-permute-start(f32[1,128]{1,0:T(1,128)S(1)} %add.15.norms_ref.refs_0_), channel_id=1, source_target_pairs={{0,13},{1,12},{2,15},{3,14},{4,9},{5,8},{6,11},{7,10},{8,5},{9,4},... | collective-permute-start | bytes 1544 | tf_op jit(solution)/shard_map/ppermute | solution.py:200
  34.1 0.9 %collective-permute-start.10 = (f32[1,128]{1,0:T(1,128)S(1)}, f32[1,128]{1,0:T(1,128)S(1)}, u32[]{:S(2)}, u32[]{:S(2)}) collective-permute-start(f32[1,128]{1,0:T(1,128)S(1)} %add.15.norms_ref.refs_0_), channel_id=1, source_target_pairs={{0,9},{1,8},{2,11},{3,10},{4,13},{5,12},{6,15},{7,14},{8,1},{9,0},... | collective-permute-start | bytes 1544 | tf_op jit(solution)/shard_map/ppermute | solution.py:200
  35.0 1.4 %shard_map.157 = (f32[8,2,1024]{2,1,0:T(2,128)}, f32[8,2,1024]{2,1,0:T(2,128)}, f32[8,2,512]{2,1,0:T(2,128)}, f32[8,2,1024]{2,1,0:T(2,128)}) custom-call(s32[2]{0:T(128)S(1)} %pad_add_fusion.where_ref, f32[1,128]{1,0:T(1,128)S(1)} %add.15.norms_ref.refs_0_, f32[1,128]{1,0:T(1,128)S(1)} %get-tuple-element.31.beta_ref, ...), custom_call_target="tpu_custom_call" | custom-call | flops 1000000000 | bytes 8388608 | tf_op jit(solution)/shard_map/pallas_call | solution.py:20
  36.4 0.4 collective-permute-done.11.refs_2_
  36.8 1.2 %collective-permute-done.10.refs_1_ = f32[1,128]{1,0:T(1,128)S(1)} collective-permute-done((f32[1,128]{1,0:T(1,128)S(1)}, f32[1,128]{1,0:T(1,128)S(1)}, u32[]{:S(2)}, u32[]{:S(2)}) %collective-permute-start.10) | collective-permute-done | bytes 544 | tf_op jit(solution)/shard_map/ppermute | solution.py:200
  38.0 0.5 %shard_map.158 = (f32[1,32]{1,0:T(1,128)}, f32[1,32]{1,0:T(1,128)}, f32[1,32]{1,0:T(1,128)}) custom-call(f32[1,128]{1,0:T(1,128)S(1)} %get-tuple-element.31.beta_ref, f32[3,32]{1,0:T(4,128)S(1)} %pad_maximum_fusion.alpha_ref.scalars_ref, f32[1,128]{1,0:T(1,128)S(1)} %add.15.norms_ref.refs_0_, f32[1,128]{1,0:T(1,128)S(1)} %collective-permute-done.10.refs_1_, ...), custom_call_target="tpu_custom_call" | custom-call | tf_op jit(solution)/shard_map/pallas_call | solution.py:20
  (35 shorter events, 0.4 us)
Async XLA Ops:
  0.6 10.9 %copy-start.1 = (bf16[1,2,2,128,512]{4,3,2,1,0:T(8,128)(2,1)S(1)}, bf16[1,2,2,128,512]{4,3,2,1,0:T(8,128)(2,1)}, u32[]{:S(2)}) copy-start(bf16[1,2,2,128,512]{4,3,2,1,0:T(8,128)(2,1)} %v_bases.3) | copy-start | bytes 1572868
  0.6 10.9 %copy-start = (bf16[1,2,2,128,512]{4,3,2,1,0:T(8,128)(2,1)S(1)}, bf16[1,2,2,128,512]{4,3,2,1,0:T(8,128)(2,1)}, u32[]{:S(2)}) copy-start(bf16[1,2,2,128,512]{4,3,2,1,0:T(8,128)(2,1)} %u_bases.3) | copy-start | bytes 1572868
  0.7 0.9 %copy-start.2 = (f32[8,2,1024]{2,1,0:T(2,128)S(1)}, f32[8,2,1024]{2,1,0:T(2,128)}, u32[]{:S(2)}) copy-start(f32[8,2,1024]{2,1,0:T(2,128)} %v_ref.3) | copy-start | bytes 196612
  1.6 5.8 %copy-start.8 = (f32[32]{0:T(128)S(1)}, f32[32]{0:T(128)}, u32[]{:S(2)}) copy-start(f32[32]{0:T(128)} %param.19) | copy-start | bytes 388
  1.6 5.8 %copy-start.9 = (f32[32]{0:T(128)S(1)}, f32[32]{0:T(128)}, u32[]{:S(2)}) copy-start(f32[32]{0:T(128)} %param.18) | copy-start | bytes 388
  1.6 5.8 %copy-start.10 = (f32[32]{0:T(128)S(1)}, f32[32]{0:T(128)}, u32[]{:S(2)}) copy-start(f32[32]{0:T(128)} %param.17) | copy-start | bytes 388
  1.6 10.0 %copy-start.4 = (f32[8,2,512]{2,1,0:T(2,128)S(1)}, f32[8,2,512]{2,1,0:T(2,128)}, u32[]{:S(2)}) copy-start(f32[8,2,512]{2,1,0:T(2,128)} %u_ref.1) | copy-start | bytes 98308
  1.6 7.0 %collective-permute-start.2 = (bf16[16,1024]{1,0:T(8,128)(2,1)S(1)}, bf16[16,1024]{1,0:T(8,128)(2,1)S(1)}, u32[]{:S(2)}, u32[]{:S(2)}) collective-permute-start(bf16[16,1024]{1,0:T(8,128)(2,1)S(1)} %shard_map.153.refs_0_), channel_id=1, source_target_pairs={{0,12},{4,8},{8,4},{12,0},{1,13},{5,9},{9,5},{13,1},{2,14},{6,10},... | collective-permute-start | bytes 98312 | tf_op jit(solution)/shard_map/ppermute | solution.py:200
  6.7 4.8 %collective-permute-start.1 = (bf16[16,1024]{1,0:T(8,128)(2,1)S(1)}, bf16[16,1024]{1,0:T(8,128)(2,1)S(1)}, u32[]{:S(2)}, u32[]{:S(2)}) collective-permute-start(bf16[16,1024]{1,0:T(8,128)(2,1)S(1)} %shard_map.153.refs_0_), channel_id=1, source_target_pairs={{0,8},{4,12},{8,0},{12,4},{1,9},{5,13},{9,1},{13,5},{2,10},{6,14},... | collective-permute-start | bytes 98312 | tf_op jit(solution)/shard_map/ppermute | solution.py:200
  6.7 4.8 %collective-permute-start = (bf16[16,1024]{1,0:T(8,128)(2,1)S(1)}, bf16[16,1024]{1,0:T(8,128)(2,1)S(1)}, u32[]{:S(2)}, u32[]{:S(2)}) collective-permute-start(bf16[16,1024]{1,0:T(8,128)(2,1)S(1)} %shard_map.153.refs_0_), channel_id=1, source_target_pairs={{0,4},{4,0},{8,12},{12,8},{1,5},{5,1},{9,13},{13,9},{2,6},{6,2},{1... | collective-permute-start | bytes 98312 | tf_op jit(solution)/shard_map/ppermute | solution.py:200
  7.4 4.2 %copy-start.5 = (s32[1,2]{1,0:T(1,128)S(1)}, s32[1,2]{1,0:T(1,128)}, u32[]{:S(2)}) copy-start(s32[1,2]{1,0:T(1,128)} %ranks_ref.3) | copy-start | bytes 28
  12.6 1.3 %collective-permute-start.3 = (bf16[64,512]{1,0:T(8,128)(2,1)S(1)}, bf16[64,512]{1,0:T(8,128)(2,1)S(1)}, u32[]{:S(2)}, u32[]{:S(2)}) collective-permute-start(bf16[64,512]{1,0:T(8,128)(2,1)S(1)} %get-tuple-element.25), channel_id=1, source_target_pairs={{0,1},{1,0},{2,3},{3,2},{4,5},{5,4},{6,7},{7,6},{8,9},{9,8},{10,11... | collective-permute-start | bytes 196616 | tf_op jit(solution)/shard_map/ppermute | solution.py:200
  13.9 4.1 %collective-permute-start.4 = (bf16[64,512]{1,0:T(8,128)(2,1)S(1)}, bf16[64,512]{1,0:T(8,128)(2,1)S(1)}, u32[]{:S(2)}, u32[]{:S(2)}) collective-permute-start(bf16[64,512]{1,0:T(8,128)(2,1)S(1)} %add_convert_fusion.sum_ref), channel_id=1, source_target_pairs={{0,3},{1,2},{2,1},{3,0},{4,7},{5,6},{6,5},{7,4},{8,11},{9,10},{10,... | collective-permute-start | bytes 196616 | tf_op jit(solution)/shard_map/ppermute | solution.py:200
  18.1 9.1 %copy-start.3 = (f32[8,2,1024]{2,1,0:T(2,128)S(1)}, f32[8,2,1024]{2,1,0:T(2,128)}, u32[]{:S(2)}) copy-start(f32[8,2,1024]{2,1,0:T(2,128)} %v_ref.3) | copy-start | bytes 196612
  19.3 5.3 %collective-permute-start.5 = (bf16[16,1152]{1,0:T(8,128)(2,1)S(1)}, bf16[16,1152]{1,0:T(8,128)(2,1)S(1)}, u32[]{:S(2)}, u32[]{:S(2)}) collective-permute-start(bf16[16,1152]{1,0:T(8,128)(2,1)S(1)} %get-tuple-element.27), channel_id=1, source_target_pairs={{0,8},{4,12},{8,0},{12,4},{1,9},{5,13},{9,1},{13,5},{2,10},{6,14},... | collective-permute-start | bytes 110600 | tf_op jit(solution)/shard_map/ppermute | solution.py:200
  21.4 5.8 %collective-permute-start.6 = (bf16[16,1152]{1,0:T(8,128)(2,1)S(1)}, bf16[16,1152]{1,0:T(8,128)(2,1)S(1)}, u32[]{:S(2)}, u32[]{:S(2)}) collective-permute-start(bf16[16,1152]{1,0:T(8,128)(2,1)S(1)} %get-tuple-element.28), channel_id=1, source_target_pairs={{0,12},{4,8},{8,4},{12,0},{1,13},{5,9},{9,5},{13,1},{2,14},{6,10},... | collective-permute-start | bytes 110600 | tf_op jit(solution)/shard_map/ppermute | solution.py:200
  21.5 5.6 %collective-permute-start.7 = (bf16[16,1152]{1,0:T(8,128)(2,1)S(1)}, bf16[16,1152]{1,0:T(8,128)(2,1)S(1)}, u32[]{:S(2)}, u32[]{:S(2)}) collective-permute-start(bf16[16,1152]{1,0:T(8,128)(2,1)S(1)} %get-tuple-element.29), channel_id=1, source_target_pairs={{0,4},{4,0},{8,12},{12,8},{1,5},{5,1},{9,13},{13,9},{2,6},{6,2},{1... | collective-permute-start | bytes 110600 | tf_op jit(solution)/shard_map/ppermute | solution.py:200
  27.2 7.9 %copy-start.6 = (f32[8,2,1024]{2,1,0:T(2,128)S(1)}, f32[8,2,1024]{2,1,0:T(2,128)}, u32[]{:S(2)}) copy-start(f32[8,2,1024]{2,1,0:T(2,128)} %x_ref.1) | copy-start | bytes 196612
  27.2 7.9 %copy-start.7 = (f32[8,2,1024]{2,1,0:T(2,128)S(1)}, f32[8,2,1024]{2,1,0:T(2,128)}, u32[]{:S(2)}) copy-start(f32[8,2,1024]{2,1,0:T(2,128)} %w_ref.1) | copy-start | bytes 196612
  27.9 1.1 %collective-permute-start.8 = (f32[1,128]{1,0:T(1,128)S(1)}, f32[1,128]{1,0:T(1,128)S(1)}, u32[]{:S(2)}, u32[]{:S(2)}) collective-permute-start(f32[1,128]{1,0:T(1,128)S(1)} %get-tuple-element.30), channel_id=1, source_target_pairs={{0,1},{1,0},{2,3},{3,2},{4,5},{5,4},{6,7},{7,6},{8,9},{9,8},{10,11... | collective-permute-start | bytes 1544 | tf_op jit(solution)/shard_map/ppermute | solution.py:200
  29.1 3.0 %collective-permute-start.9 = (f32[1,128]{1,0:T(1,128)S(1)}, f32[1,128]{1,0:T(1,128)S(1)}, u32[]{:S(2)}, u32[]{:S(2)}) collective-permute-start(f32[1,128]{1,0:T(1,128)S(1)} %add.14), channel_id=1, source_target_pairs={{0,3},{1,2},{2,1},{3,0},{4,7},{5,6},{6,5},{7,4},{8,11},{9,10},{10,... | collective-permute-start | bytes 1544 | tf_op jit(solution)/shard_map/ppermute | solution.py:200
  32.0 4.4 %collective-permute-start.12 = (f32[1,128]{1,0:T(1,128)S(1)}, f32[1,128]{1,0:T(1,128)S(1)}, u32[]{:S(2)}, u32[]{:S(2)}) collective-permute-start(f32[1,128]{1,0:T(1,128)S(1)} %add.15.norms_ref.refs_0_), channel_id=1, source_target_pairs={{0,5},{1,4},{2,7},{3,6},{4,1},{5,0},{6,3},{7,2},{8,13},{9,12},{10,... | collective-permute-start | bytes 1544 | tf_op jit(solution)/shard_map/ppermute | solution.py:200
  32.0 4.8 %collective-permute-start.11 = (f32[1,128]{1,0:T(1,128)S(1)}, f32[1,128]{1,0:T(1,128)S(1)}, u32[]{:S(2)}, u32[]{:S(2)}) collective-permute-start(f32[1,128]{1,0:T(1,128)S(1)} %add.15.norms_ref.refs_0_), channel_id=1, source_target_pairs={{0,13},{1,12},{2,15},{3,14},{4,9},{5,8},{6,11},{7,10},{8,5},{9,4},... | collective-permute-start | bytes 1544 | tf_op jit(solution)/shard_map/ppermute | solution.py:200
  34.1 3.9 %collective-permute-start.10 = (f32[1,128]{1,0:T(1,128)S(1)}, f32[1,128]{1,0:T(1,128)S(1)}, u32[]{:S(2)}, u32[]{:S(2)}) collective-permute-start(f32[1,128]{1,0:T(1,128)S(1)} %add.15.norms_ref.refs_0_), channel_id=1, source_target_pairs={{0,9},{1,8},{2,11},{3,10},{4,13},{5,12},{6,15},{7,14},{8,1},{9,0},... | collective-permute-start | bytes 1544 | tf_op jit(solution)/shard_map/ppermute | solution.py:200

commit v3 on v2

--- a/solution.py
+++ b/solution.py
@@ -13,10 +13,8 @@
 bf16 = jnp.bfloat16
 
 
-def call(kernel, outs, *args, scratch=(), vmem=12, hbm=False, cost=None):
-    in_specs = [
-        pl.BlockSpec(memory_space=pltpu.HBM if hbm else pltpu.SMEM if a.dtype == jnp.int32 else pltpu.VMEM) for a in args
-    ]
+def call(kernel, outs, *args, scratch=(), vmem=12, cost=None):
+    in_specs = [pl.BlockSpec(memory_space=pltpu.VMEM)] * len(args)
     return pl.pallas_call(
         kernel,
         out_shape=[jax.ShapeDtypeStruct(s, d) for s, d in outs],
@@ -48,42 +46,37 @@
     return lax.dot_general(a, b, (((1,), (1 if transposed else 0,)), ((), ())), preferred_element_type=f32)
 
 
-def through(inner, outer, ranks_ref, x, own):
+def through(inner, outer, live_ref, x, own):
     total = []
     tiles, _, ranks, size = inner.shape[1:]
     for q in range(tiles):
         g = dot(x(q), inner[0, q].reshape(2 * ranks, size), True)
         rows = g.shape[0]
         g = g.reshape(rows // (2 * own), 2, own, 2 * ranks)
-        live = iota((1, 1, ranks), 2) < ranks_ref[0, q]
-        re = jnp.where(live, g[:, 0, :, :ranks] + g[:, 1, :, ranks:], 0.0)
-        im = jnp.where(live, g[:, 1, :, :ranks] - g[:, 0, :, ranks:], 0.0)
+        live = live_ref[q : q + 1, :]
+        re = (g[:, 0, :, :ranks] + g[:, 1, :, ranks:]) * live
+        im = (g[:, 1, :, :ranks] - g[:, 0, :, ranks:]) * live
         both = jnp.stack([jnp.concatenate([re, -im], 2), jnp.concatenate([im, re], 2)], 1)
         both = both.reshape(rows, 2 * ranks).astype(bf16)
         total.append(dot(both, outer[0, q].reshape(2 * ranks, size), False))
     return total
 
 
+def in_order(blocks, order):
+    return [blocks[0]] + [blocks[1 + order.index(k)] for k in range(1, len(blocks))]
+
+
 def pack_kernel(v_ref, out_ref):
     own = v_ref.shape[0]
     out_ref[...] = jnp.concatenate([v_ref[:, 0, :], v_ref[:, 1, :]], 0).astype(bf16)
 
 
-def load_kernel(many, *refs):
-    ins, outs, sems = refs[:many], refs[many:-1], refs[-1]
-    copies = [pltpu.make_async_copy(a, b, sems.at[i]) for i, (a, b) in enumerate(zip(ins, outs))]
-    for copy in copies:
-        copy.start()
-    for copy in copies:
-        copy.wait()
-
-
-def forward_kernel(n_row, own_v, own_u, where_ref, ranks_ref, u_bases, v_bases, u_ref, alpha_ref, *refs):
-    blocks, (low_ref, own_ref, total) = refs[:n_row], refs[n_row:]
-    p, c = where_ref[0], where_ref[1]
+def forward_kernel(n_row, order, own_v, own_u, live_ref, u_bases, v_bases, u_ref, alpha_ref, *refs):
+    blocks, (low_ref, own_ref, total) = in_order(refs[:n_row], order), refs[n_row:]
+    p, c = lax.axis_index("row"), lax.axis_index(("col", "cplx"))
     size = v_bases.shape[4]
     x = jnp.concatenate([b[...] for b in blocks], 0)
-    parts = through(v_bases, u_bases, ranks_ref, lambda q: x[:, q * size : (q + 1) * size], own_v)
+    parts = through(v_bases, u_bases, live_ref, lambda q: x[:, q * size : (q + 1) * size], own_v)
     total[...] = sum(parts[1:], parts[0])
     many = own_u // own_v
     for b in range(many):
@@ -97,9 +90,9 @@
     low_ref[...] = total[...].astype(bf16)
 
 
-def adjoint_kernel(n_row, n_got, own_v, own_u, lanes, where_ref, ranks_ref, u_bases, v_bases, own_ref, sum_ref, *refs):
+def adjoint_kernel(n_row, n_got, own_v, own_u, lanes, live_ref, u_bases, v_bases, own_ref, sum_ref, *refs):
     got, outs, own_out = refs[:n_got], refs[n_got : n_got + n_row], refs[n_got + n_row]
-    p, c = where_ref[0], where_ref[1]
+    p, c = lax.axis_index("row"), lax.axis_index(("col", "cplx"))
     many = own_u // own_v
     for b in range(many):
         at = pl.ds(pl.multiple_of(((c * many + b) ^ p) * 2 * own_v, 2 * own_v), 2 * own_v)
@@ -118,7 +111,7 @@
     low = (beta2 - high.astype(f32)).astype(bf16)
     tail = jnp.where(iota((2 * own_v, lanes), 0) == 0, high.astype(f32), low.astype(f32)).astype(bf16)
     x = (res * shrink).astype(bf16)
-    parts = through(u_bases, v_bases, ranks_ref, lambda q: x, own_v)
+    parts = through(u_bases, v_bases, live_ref, lambda q: x, own_v)
     wide = parts[0].shape[1]
     for k, out in enumerate(outs):
         for q, part in enumerate(parts):
@@ -132,10 +125,9 @@
     return values[0]
 
 
-def residual_kernel(n_row, rows_total, cols_total, lanes, where_ref, v_ref, *refs):
-    blocks, (res_ref, beta_ref, norm_ref) = refs[:n_row], refs[n_row:]
-    blocks = [blocks[0], blocks[-1], *blocks[1:-1]]
-    p = where_ref[0]
+def residual_kernel(n_row, order, rows_total, cols_total, lanes, v_ref, *refs):
+    blocks, (res_ref, beta_ref, norm_ref) = in_order(refs[:n_row], order), refs[n_row:]
+    p = lax.axis_index("row")
     own_v, _, wide = v_ref.shape
     beta2 = pairs([b[0:1, wide:].astype(f32) + b[1:2, wide:].astype(f32) for b in blocks])
     beta = jnp.sqrt(beta2 / (2 * rows_total) + epsilon)
@@ -160,8 +152,8 @@
     return rho, rhobar / rho, beta / rho, phibar
 
 
-def vectors_kernel(cols_total, where_ref, norms_ref, beta_ref, res_ref, own_ref, x_ref, w_ref, scalars_ref, x_out, w_out, u_out, v_out):
-    p, c = where_ref[0], where_ref[1]
+def vectors_kernel(cols_total, norms_ref, beta_ref, res_ref, own_ref, x_ref, w_ref, scalars_ref, x_out, w_out, u_out, v_out):
+    p, c = lax.axis_index("row"), lax.axis_index(("col", "cplx"))
     own_v = x_ref.shape[0]
     own_u = u_out.shape[0]
     many = own_u // own_v
@@ -223,17 +215,19 @@
     rhs = own_v * n_row
     lanes = -(-rhs // 128) * 128
     block = 2 * own_v
-    where = jnp.stack([lax.axis_index("row"), lax.axis_index(("col", "cplx"))]).astype(jnp.int32)
+    live = (jnp.arange(u_bases.shape[3], dtype=jnp.int32)[None] < tile_ranks[0][:, None]).astype(f32)
 
     vmem = 8 + rhs // 16
+    first = [1, *range(n_row - 1, 1, -1)]
+    second = [*range(2, n_row), 1]
+    third = first
     scalars = jnp.stack([alpha_prev, rhobar_prev, phibar_prev])
     (v_low,) = call(pack_kernel, [((block, wide), bf16)], v_unit, cost=pl.CostEstimate(flops=10**10, bytes_accessed=2**26, transcendentals=0))
-    blocks = [v_low] + [flip(v_low, "row", k) for k in range(1, n_row)]
+    blocks = [v_low] + [flip(v_low, "row", k) for k in first]
     low, own = call(
-        partial(forward_kernel, n_row, own_v, own_u),
+        partial(forward_kernel, n_row, first, own_v, own_u),
         [((2 * rhs, tile_size), bf16), ((2 * own_u, tile_size), f32)],
-        where,
-        tile_ranks,
+        live,
         u_bases,
         v_bases,
         u_unit,
@@ -251,8 +245,7 @@
     *outs, own = call(
         partial(adjoint_kernel, n_row, len(got), own_v, own_u, lanes),
         [((block, wide + lanes), bf16)] * n_row + [((2 * own_u, tile_size), f32)],
-        where,
-        tile_ranks,
+        live,
         u_bases,
         v_bases,
         own,
@@ -260,12 +253,10 @@
         *got,
         vmem=vmem,
     )
-    order = [*range(2, n_row), 1]
-    blocks = [outs[0]] + [flip(outs[k], "row", k) for k in order]
+    blocks = [outs[0]] + [flip(outs[k], "row", k) for k in second]
     residual_v, beta, norms = call(
-        partial(residual_kernel, n_row, rows_total, cols_total, lanes),
+        partial(residual_kernel, n_row, second, rows_total, cols_total, lanes),
         [((block, wide), f32), ((1, lanes), f32), ((1, lanes), f32)],
-        where,
         v_unit,
         *blocks,
     )
@@ -274,11 +265,10 @@
     while mask < n_cols:
         norms = norms + flip(norms, ("col", "cplx"), mask + 1)
         mask *= 2
-    norms_all = [norms] + [flip(norms, ("row", "col", "cplx"), k * n_cols + 1) for k in order]
+    norms_all = [norms] + [flip(norms, ("row", "col", "cplx"), k * n_cols + 1) for k in third]
     x_next, w_next, u_next, v_next = call(
         partial(vectors_kernel, cols_total),
         [(x_solution.shape, f32), (w_direction.shape, f32), (u_unit.shape, f32), (v_unit.shape, f32)],
-        where,
         norms,
         beta,
         residual_v,

time: 38.7 us -> 35.8 us (0.925)
  Pallas kernels: 4.91 us -> 2.74 us
  waiting for transfers between devices: 16.8 us -> 15.4 us
  local copies, waits for them, and re-layouts: 0.97 us -> 1.63 us
    pallas_call x6, Pallas kernels: 4.91 us -> 2.74 us  [call(): pl.pallas_call(kernel, out_shape=[jax.ShapeDtypeStruct(s, d) for s, d in...]
    ppermute x13, waiting for transfers between devices: 16.8 us -> 15.4 us  [flip(): lax.ppermute(x, axes, [(i, i ^ mask) for i in range(lax.axis_size(axes))])]
    unnamed x22 -> x20, local copies, waits for them, and re-layouts: 0.97 us -> 1.63 us
  transfers between devices with their start and end apart: 13 -> 13, of which waited for: 10 -> 8; matrix products, arithmetic and copies ran while one was open for 0% -> 0% of each run, Pallas kernels for 4% -> 2%
where the time goes in v3:
time: 35.8 us; the launch traced here: 35.6 us
  waiting for transfers between devices  15.4 us (43%)
  starting transfers between devices  15 us (42%)
  Pallas kernels  2.74 us (8%)
  local copies, waits for them, and re-layouts  1.63 us (5%)
  between operations  0.74 us (2%)
    ppermute x13, waiting for transfers between devices, flip(): lax.ppermute(x, axes, [(i, i ^ mask) for i in range(lax.axis_size(axes))])  15.4 us
    ppermute x13, starting transfers between devices, flip(): lax.ppermute(x, axes, [(i, i ^ mask) for i in range(lax.axis_size(axes))])  15 us
    pallas_call x6, Pallas kernels, call(): pl.pallas_call(kernel, out_shape=[jax.ShapeDtypeStruct(s, d) for s, d in...  2.74 us
    unnamed x20, local copies, waits for them, and re-layouts  1.63 us
  transfers between devices with their start and end apart: 13, of which 8 were waited for; matrix products, arithmetic and copies ran while one was open for 0% of the time, Pallas kernels for 2%

profile of v3, /device:TPU:0, one launch (start us, length us, event | category | flops | bytes accessed | tf_op | source)
XLA Modules:
  0.0 35.6 jit_solution(1306458568579154903)
XLA Ops:
  0.7 0.9 %copy-done.2 = f32[8,2,1024]{2,1,0:T(2,128)S(1)} copy-done((f32[8,2,1024]{2,1,0:T(2,128)S(1)}, f32[8,2,1024]{2,1,0:T(2,128)}, u32[]{:S(2)}) %copy-start.2) | copy-done | bytes 65560
  1.6 4.1 %collective-permute-start.2 = (bf16[16,1024]{1,0:T(8,128)(2,1)S(1)}, bf16[16,1024]{1,0:T(8,128)(2,1)S(1)}, u32[]{:S(2)}, u32[]{:S(2)}) collective-permute-start(bf16[16,1024]{1,0:T(8,128)(2,1)S(1)} %shard_map.153.refs_0_), channel_id=1, source_target_pairs={{0,8},{4,12},{8,0},{12,4},{1,9},{5,13},{9,1},{13,5},{2,10},{6,14},... | collective-permute-start | bytes 98312 | tf_op jit(solution)/shard_map/ppermute | solution.py:192
  5.7 1.3 %collective-permute-start.1 = (bf16[16,1024]{1,0:T(8,128)(2,1)S(1)}, bf16[16,1024]{1,0:T(8,128)(2,1)S(1)}, u32[]{:S(2)}, u32[]{:S(2)}) collective-permute-start(bf16[16,1024]{1,0:T(8,128)(2,1)S(1)} %shard_map.153.refs_0_), channel_id=1, source_target_pairs={{0,12},{4,8},{8,4},{12,0},{1,13},{5,9},{9,5},{13,1},{2,14},{6,10},... | collective-permute-start | bytes 98312 | tf_op jit(solution)/shard_map/ppermute | solution.py:192
  7.4 0.6 %copy-done.6 = f32[32]{0:T(128)S(1)} copy-done((f32[32]{0:T(128)S(1)}, f32[32]{0:T(128)}, u32[]{:S(2)}) %copy-start.6) | copy-done | bytes 152
  8.1 3.3 %collective-permute-done.1.refs_2_ = bf16[16,1024]{1,0:T(8,128)(2,1)S(1)} collective-permute-done((bf16[16,1024]{1,0:T(8,128)(2,1)S(1)}, bf16[16,1024]{1,0:T(8,128)(2,1)S(1)}, u32[]{:S(2)}, u32[]{:S(2)}) %collective-permute-start.1) | collective-permute-done | bytes 32800 | tf_op jit(solution)/shard_map/ppermute | solution.py:192
  11.4 0.5 %shard_map.154 = (bf16[64,512]{1,0:T(8,128)(2,1)S(1)}, f32[16,512]{1,0:T(8,128)S(1)}) custom-call(f32[2,128]{1,0:T(2,128)S(1)} %compare_convert_fusion.live_ref, bf16[1,2,2,128,512]{4,3,2,1,0:T(8,128)(2,1)S(1)} %copy-done, bf16[1,2,2,128,512]{4,3,2,1,0:T(8,128)(2,1)S(1)} %copy-done.1, f32[8,2,512]{2,1,0:T(2,128)S(1)} %copy-done.3, ...), custom_call_target="tpu_custom_call" | custom-call | tf_op jit(solution)/shard_map/pallas_call | solution.py:18
  12.0 1.2 %collective-permute-done.3.refs_0_ = bf16[64,512]{1,0:T(8,128)(2,1)S(1)} collective-permute-done((bf16[64,512]{1,0:T(8,128)(2,1)S(1)}, bf16[64,512]{1,0:T(8,128)(2,1)S(1)}, u32[]{:S(2)}, u32[]{:S(2)}) %collective-permute-start.3) | collective-permute-done | bytes 65568 | tf_op jit(solution)/shard_map/ppermute | solution.py:192
  13.3 1.3 %collective-permute-start.4 = (bf16[64,512]{1,0:T(8,128)(2,1)S(1)}, bf16[64,512]{1,0:T(8,128)(2,1)S(1)}, u32[]{:S(2)}, u32[]{:S(2)}) collective-permute-start(bf16[64,512]{1,0:T(8,128)(2,1)S(1)} %add_convert_fusion.sum_ref), channel_id=1, source_target_pairs={{0,3},{1,2},{2,1},{3,0},{4,7},{5,6},{6,5},{7,4},{8,11},{9,10},{10,... | collective-permute-start | bytes 196616 | tf_op jit(solution)/shard_map/ppermute | solution.py:192
  14.6 2.8 %collective-permute-done.4.refs_1_ = bf16[64,512]{1,0:T(8,128)(2,1)S(1)} collective-permute-done((bf16[64,512]{1,0:T(8,128)(2,1)S(1)}, bf16[64,512]{1,0:T(8,128)(2,1)S(1)}, u32[]{:S(2)}, u32[]{:S(2)}) %collective-permute-start.4) | collective-permute-done | bytes 65568 | tf_op jit(solution)/shard_map/ppermute | solution.py:192
  17.4 0.7 %shard_map.155 = (bf16[16,1152]{1,0:T(8,128)(2,1)S(1)}, bf16[16,1152]{1,0:T(8,128)(2,1)S(1)}, bf16[16,1152]{1,0:T(8,128)(2,1)S(1)}, bf16[16,1152]{1,0:T(8,128)(2,1)S(1)}, f32[16,512]{1,0:T(8,128)S(1)}) custom-call(f32[2,128]{1,0:T(2,128)S(1)} %compare_convert_fusion.live_ref, bf16[1,2,2,128,512]{4,3,2,1,0:T(8,128)(2,1)S(1)} %copy-done, ...), custom_call_target="tpu_custom_call" | custom-call | tf_op jit(solution)/shard_map/pallas_call | solution.py:18
  18.1 1.3 %collective-permute-start.5 = (bf16[16,1152]{1,0:T(8,128)(2,1)S(1)}, bf16[16,1152]{1,0:T(8,128)(2,1)S(1)}, u32[]{:S(2)}, u32[]{:S(2)}) collective-permute-start(bf16[16,1152]{1,0:T(8,128)(2,1)S(1)} %get-tuple-element.27), channel_id=1, source_target_pairs={{0,8},{4,12},{8,0},{12,4},{1,9},{5,13},{9,1},{13,5},{2,10},{6,14},... | collective-permute-start | bytes 110600 | tf_op jit(solution)/shard_map/ppermute | solution.py:192
  19.4 1.0 %collective-permute-start.6 = (bf16[16,1152]{1,0:T(8,128)(2,1)S(1)}, bf16[16,1152]{1,0:T(8,128)(2,1)S(1)}, u32[]{:S(2)}, u32[]{:S(2)}) collective-permute-start(bf16[16,1152]{1,0:T(8,128)(2,1)S(1)} %get-tuple-element.28), channel_id=1, source_target_pairs={{0,12},{4,8},{8,4},{12,0},{1,13},{5,9},{9,5},{13,1},{2,14},{6,10},... | collective-permute-start | bytes 110600 | tf_op jit(solution)/shard_map/ppermute | solution.py:192
  20.4 1.2 %collective-permute-start.7 = (bf16[16,1152]{1,0:T(8,128)(2,1)S(1)}, bf16[16,1152]{1,0:T(8,128)(2,1)S(1)}, u32[]{:S(2)}, u32[]{:S(2)}) collective-permute-start(bf16[16,1152]{1,0:T(8,128)(2,1)S(1)} %get-tuple-element.29), channel_id=1, source_target_pairs={{0,4},{4,0},{8,12},{12,8},{1,5},{5,1},{9,13},{13,9},{2,6},{6,2},{1... | collective-permute-start | bytes 110600 | tf_op jit(solution)/shard_map/ppermute | solution.py:192
  21.7 1.7 %collective-permute-done.5.refs_1_ = bf16[16,1152]{1,0:T(8,128)(2,1)S(1)} collective-permute-done((bf16[16,1152]{1,0:T(8,128)(2,1)S(1)}, bf16[16,1152]{1,0:T(8,128)(2,1)S(1)}, u32[]{:S(2)}, u32[]{:S(2)}) %collective-permute-start.5) | collective-permute-done | bytes 36896 | tf_op jit(solution)/shard_map/ppermute | solution.py:192
  23.4 1.8 %collective-permute-done.6.refs_2_ = bf16[16,1152]{1,0:T(8,128)(2,1)S(1)} collective-permute-done((bf16[16,1152]{1,0:T(8,128)(2,1)S(1)}, bf16[16,1152]{1,0:T(8,128)(2,1)S(1)}, u32[]{:S(2)}, u32[]{:S(2)}) %collective-permute-start.6) | collective-permute-done | bytes 36896 | tf_op jit(solution)/shard_map/ppermute | solution.py:192
  25.4 1.1 %collective-permute-done.8 = f32[1,128]{1,0:T(1,128)S(1)} collective-permute-done((f32[1,128]{1,0:T(1,128)S(1)}, f32[1,128]{1,0:T(1,128)S(1)}, u32[]{:S(2)}, u32[]{:S(2)}) %collective-permute-start.8) | collective-permute-done | bytes 544 | tf_op jit(solution)/shard_map/ppermute | solution.py:192
  26.5 1.3 %collective-permute-start.9 = (f32[1,128]{1,0:T(1,128)S(1)}, f32[1,128]{1,0:T(1,128)S(1)}, u32[]{:S(2)}, u32[]{:S(2)}) collective-permute-start(f32[1,128]{1,0:T(1,128)S(1)} %add.10), channel_id=1, source_target_pairs={{0,3},{1,2},{2,1},{3,0},{4,7},{5,6},{6,5},{7,4},{8,11},{9,10},{10,... | collective-permute-start | bytes 1544 | tf_op jit(solution)/shard_map/ppermute | solution.py:192
  27.8 1.7 %collective-permute-done.9 = f32[1,128]{1,0:T(1,128)S(1)} collective-permute-done((f32[1,128]{1,0:T(1,128)S(1)}, f32[1,128]{1,0:T(1,128)S(1)}, u32[]{:S(2)}, u32[]{:S(2)}) %collective-permute-start.9) | collective-permute-done | bytes 544 | tf_op jit(solution)/shard_map/ppermute | solution.py:192
  29.5 0.8 %collective-permute-start.12 = (f32[1,128]{1,0:T(1,128)S(1)}, f32[1,128]{1,0:T(1,128)S(1)}, u32[]{:S(2)}, u32[]{:S(2)}) collective-permute-start(f32[1,128]{1,0:T(1,128)S(1)} %add.11.norms_ref.refs_0_), channel_id=1, source_target_pairs={{0,9},{1,8},{2,11},{3,10},{4,13},{5,12},{6,15},{7,14},{8,1},{9,0},... | collective-permute-start | bytes 1544 | tf_op jit(solution)/shard_map/ppermute | solution.py:192
  30.3 1.7 %collective-permute-start.11 = (f32[1,128]{1,0:T(1,128)S(1)}, f32[1,128]{1,0:T(1,128)S(1)}, u32[]{:S(2)}, u32[]{:S(2)}) collective-permute-start(f32[1,128]{1,0:T(1,128)S(1)} %add.11.norms_ref.refs_0_), channel_id=1, source_target_pairs={{0,13},{1,12},{2,15},{3,14},{4,9},{5,8},{6,11},{7,10},{8,5},{9,4},... | collective-permute-start | bytes 1544 | tf_op jit(solution)/shard_map/ppermute | solution.py:192
  32.0 0.5 %collective-permute-start.10 = (f32[1,128]{1,0:T(1,128)S(1)}, f32[1,128]{1,0:T(1,128)S(1)}, u32[]{:S(2)}, u32[]{:S(2)}) collective-permute-start(f32[1,128]{1,0:T(1,128)S(1)} %add.11.norms_ref.refs_0_), channel_id=1, source_target_pairs={{0,5},{1,4},{2,7},{3,6},{4,1},{5,0},{6,3},{7,2},{8,13},{9,12},{10,... | collective-permute-start | bytes 1544 | tf_op jit(solution)/shard_map/ppermute | solution.py:192
  32.5 0.8 %shard_map.157 = (f32[8,2,1024]{2,1,0:T(2,128)}, f32[8,2,1024]{2,1,0:T(2,128)}, f32[8,2,512]{2,1,0:T(2,128)}, f32[8,2,1024]{2,1,0:T(2,128)}) custom-call(f32[1,128]{1,0:T(1,128)S(1)} %add.11.norms_ref.refs_0_, f32[1,128]{1,0:T(1,128)S(1)} %get-tuple-element.31.beta_ref, f32[16,1024]{1,0:T(8,128)S(1)} %get-tuple-element.32.res_ref, ...), custom_call_target="tpu_custom_call" | custom-call | flops 1000000000 | bytes 8388608 | tf_op jit(solution)/shard_map/pallas_call | solution.py:18
  33.3 1.7 %collective-permute-done.11.refs_2_ = f32[1,128]{1,0:T(1,128)S(1)} collective-permute-done((f32[1,128]{1,0:T(1,128)S(1)}, f32[1,128]{1,0:T(1,128)S(1)}, u32[]{:S(2)}, u32[]{:S(2)}) %collective-permute-start.11) | collective-permute-done | bytes 544 | tf_op jit(solution)/shard_map/ppermute | solution.py:192
  35.1 0.5 %shard_map.158 = (f32[1,32]{1,0:T(1,128)}, f32[1,32]{1,0:T(1,128)}, f32[1,32]{1,0:T(1,128)}) custom-call(f32[1,128]{1,0:T(1,128)S(1)} %get-tuple-element.31.beta_ref, f32[3,32]{1,0:T(4,128)S(1)} %pad_maximum_fusion.alpha_ref.scalars_ref, f32[1,128]{1,0:T(1,128)S(1)} %add.11.norms_ref.refs_0_, f32[1,128]{1,0:T(1,128)S(1)} %collective-permute-done.10.refs_1_, ...), custom_call_target="tpu_custom_call" | custom-call | tf_op jit(solution)/shard_map/pallas_call | solution.py:18
  (33 shorter events, 0.7 us)
Async XLA Ops:
  0.6 10.8 %copy-start.1 = (bf16[1,2,2,128,512]{4,3,2,1,0:T(8,128)(2,1)S(1)}, bf16[1,2,2,128,512]{4,3,2,1,0:T(8,128)(2,1)}, u32[]{:S(2)}) copy-start(bf16[1,2,2,128,512]{4,3,2,1,0:T(8,128)(2,1)} %v_bases.3) | copy-start | bytes 1572868
  0.6 10.8 %copy-start = (bf16[1,2,2,128,512]{4,3,2,1,0:T(8,128)(2,1)S(1)}, bf16[1,2,2,128,512]{4,3,2,1,0:T(8,128)(2,1)}, u32[]{:S(2)}) copy-start(bf16[1,2,2,128,512]{4,3,2,1,0:T(8,128)(2,1)} %u_bases.3) | copy-start | bytes 1572868
  0.7 0.9 %copy-start.2 = (f32[8,2,1024]{2,1,0:T(2,128)S(1)}, f32[8,2,1024]{2,1,0:T(2,128)}, u32[]{:S(2)}) copy-start(f32[8,2,1024]{2,1,0:T(2,128)} %v_ref.3) | copy-start | bytes 196612
  1.6 9.9 %copy-start.3 = (f32[8,2,512]{2,1,0:T(2,128)S(1)}, f32[8,2,512]{2,1,0:T(2,128)}, u32[]{:S(2)}) copy-start(f32[8,2,512]{2,1,0:T(2,128)} %u_ref.1) | copy-start | bytes 98308
  1.6 5.7 %copy-start.9 = (s32[1,2]{1,0:T(1,128)S(1)}, s32[1,2]{1,0:T(1,128)}, u32[]{:S(2)}) copy-start(s32[1,2]{1,0:T(1,128)} %param.12) | copy-start | bytes 28
  1.6 6.5 %collective-permute-start.2 = (bf16[16,1024]{1,0:T(8,128)(2,1)S(1)}, bf16[16,1024]{1,0:T(8,128)(2,1)S(1)}, u32[]{:S(2)}, u32[]{:S(2)}) collective-permute-start(bf16[16,1024]{1,0:T(8,128)(2,1)S(1)} %shard_map.153.refs_0_), channel_id=1, source_target_pairs={{0,8},{4,12},{8,0},{12,4},{1,9},{5,13},{9,1},{13,5},{2,10},{6,14},... | collective-permute-start | bytes 98312 | tf_op jit(solution)/shard_map/ppermute | solution.py:192
  5.7 5.7 %collective-permute-start.1 = (bf16[16,1024]{1,0:T(8,128)(2,1)S(1)}, bf16[16,1024]{1,0:T(8,128)(2,1)S(1)}, u32[]{:S(2)}, u32[]{:S(2)}) collective-permute-start(bf16[16,1024]{1,0:T(8,128)(2,1)S(1)} %shard_map.153.refs_0_), channel_id=1, source_target_pairs={{0,12},{4,8},{8,4},{12,0},{1,13},{5,9},{9,5},{13,1},{2,14},{6,10},... | collective-permute-start | bytes 98312 | tf_op jit(solution)/shard_map/ppermute | solution.py:192
  7.1 4.4 %collective-permute-start = (bf16[16,1024]{1,0:T(8,128)(2,1)S(1)}, bf16[16,1024]{1,0:T(8,128)(2,1)S(1)}, u32[]{:S(2)}, u32[]{:S(2)}) collective-permute-start(bf16[16,1024]{1,0:T(8,128)(2,1)S(1)} %shard_map.153.refs_0_), channel_id=1, source_target_pairs={{0,4},{4,0},{8,12},{12,8},{1,5},{5,1},{9,13},{13,9},{2,6},{6,2},{1... | collective-permute-start | bytes 98312 | tf_op jit(solution)/shard_map/ppermute | solution.py:192
  7.4 0.7 %copy-start.6 = (f32[32]{0:T(128)S(1)}, f32[32]{0:T(128)}, u32[]{:S(2)}) copy-start(f32[32]{0:T(128)} %param.19) | copy-start | bytes 388
  7.4 0.7 %copy-start.7 = (f32[32]{0:T(128)S(1)}, f32[32]{0:T(128)}, u32[]{:S(2)}) copy-start(f32[32]{0:T(128)} %param.18) | copy-start | bytes 388
  7.4 0.7 %copy-start.8 = (f32[32]{0:T(128)S(1)}, f32[32]{0:T(128)}, u32[]{:S(2)}) copy-start(f32[32]{0:T(128)} %param.17) | copy-start | bytes 388
  11.9 1.3 %collective-permute-start.3 = (bf16[64,512]{1,0:T(8,128)(2,1)S(1)}, bf16[64,512]{1,0:T(8,128)(2,1)S(1)}, u32[]{:S(2)}, u32[]{:S(2)}) collective-permute-start(bf16[64,512]{1,0:T(8,128)(2,1)S(1)} %get-tuple-element.25), channel_id=1, source_target_pairs={{0,1},{1,0},{2,3},{3,2},{4,5},{5,4},{6,7},{7,6},{8,9},{9,8},{10,11... | collective-permute-start | bytes 196616 | tf_op jit(solution)/shard_map/ppermute | solution.py:192
  13.3 4.1 %collective-permute-start.4 = (bf16[64,512]{1,0:T(8,128)(2,1)S(1)}, bf16[64,512]{1,0:T(8,128)(2,1)S(1)}, u32[]{:S(2)}, u32[]{:S(2)}) collective-permute-start(bf16[64,512]{1,0:T(8,128)(2,1)S(1)} %add_convert_fusion.sum_ref), channel_id=1, source_target_pairs={{0,3},{1,2},{2,1},{3,0},{4,7},{5,6},{6,5},{7,4},{8,11},{9,10},{10,... | collective-permute-start | bytes 196616 | tf_op jit(solution)/shard_map/ppermute | solution.py:192
  18.1 5.3 %collective-permute-start.5 = (bf16[16,1152]{1,0:T(8,128)(2,1)S(1)}, bf16[16,1152]{1,0:T(8,128)(2,1)S(1)}, u32[]{:S(2)}, u32[]{:S(2)}) collective-permute-start(bf16[16,1152]{1,0:T(8,128)(2,1)S(1)} %get-tuple-element.27), channel_id=1, source_target_pairs={{0,8},{4,12},{8,0},{12,4},{1,9},{5,13},{9,1},{13,5},{2,10},{6,14},... | collective-permute-start | bytes 110600 | tf_op jit(solution)/shard_map/ppermute | solution.py:192
  19.4 5.8 %collective-permute-start.6 = (bf16[16,1152]{1,0:T(8,128)(2,1)S(1)}, bf16[16,1152]{1,0:T(8,128)(2,1)S(1)}, u32[]{:S(2)}, u32[]{:S(2)}) collective-permute-start(bf16[16,1152]{1,0:T(8,128)(2,1)S(1)} %get-tuple-element.28), channel_id=1, source_target_pairs={{0,12},{4,8},{8,4},{12,0},{1,13},{5,9},{9,5},{13,1},{2,14},{6,10},... | collective-permute-start | bytes 110600 | tf_op jit(solution)/shard_map/ppermute | solution.py:192
  20.4 4.7 %collective-permute-start.7 = (bf16[16,1152]{1,0:T(8,128)(2,1)S(1)}, bf16[16,1152]{1,0:T(8,128)(2,1)S(1)}, u32[]{:S(2)}, u32[]{:S(2)}) collective-permute-start(bf16[16,1152]{1,0:T(8,128)(2,1)S(1)} %get-tuple-element.29), channel_id=1, source_target_pairs={{0,4},{4,0},{8,12},{12,8},{1,5},{5,1},{9,13},{13,9},{2,6},{6,2},{1... | collective-permute-start | bytes 110600 | tf_op jit(solution)/shard_map/ppermute | solution.py:192
  25.2 7.3 %copy-start.4 = (f32[8,2,1024]{2,1,0:T(2,128)S(1)}, f32[8,2,1024]{2,1,0:T(2,128)}, u32[]{:S(2)}) copy-start(f32[8,2,1024]{2,1,0:T(2,128)} %x_ref.1) | copy-start | bytes 196612
  25.2 7.3 %copy-start.5 = (f32[8,2,1024]{2,1,0:T(2,128)S(1)}, f32[8,2,1024]{2,1,0:T(2,128)}, u32[]{:S(2)}) copy-start(f32[8,2,1024]{2,1,0:T(2,128)} %w_ref.1) | copy-start | bytes 196612
  25.4 1.1 %collective-permute-start.8 = (f32[1,128]{1,0:T(1,128)S(1)}, f32[1,128]{1,0:T(1,128)S(1)}, u32[]{:S(2)}, u32[]{:S(2)}) collective-permute-start(f32[1,128]{1,0:T(1,128)S(1)} %get-tuple-element.30), channel_id=1, source_target_pairs={{0,1},{1,0},{2,3},{3,2},{4,5},{5,4},{6,7},{7,6},{8,9},{9,8},{10,11... | collective-permute-start | bytes 1544 | tf_op jit(solution)/shard_map/ppermute | solution.py:192
  26.5 3.0 %collective-permute-start.9 = (f32[1,128]{1,0:T(1,128)S(1)}, f32[1,128]{1,0:T(1,128)S(1)}, u32[]{:S(2)}, u32[]{:S(2)}) collective-permute-start(f32[1,128]{1,0:T(1,128)S(1)} %add.10), channel_id=1, source_target_pairs={{0,3},{1,2},{2,1},{3,0},{4,7},{5,6},{6,5},{7,4},{8,11},{9,10},{10,... | collective-permute-start | bytes 1544 | tf_op jit(solution)/shard_map/ppermute | solution.py:192
  29.5 3.9 %collective-permute-start.12 = (f32[1,128]{1,0:T(1,128)S(1)}, f32[1,128]{1,0:T(1,128)S(1)}, u32[]{:S(2)}, u32[]{:S(2)}) collective-permute-start(f32[1,128]{1,0:T(1,128)S(1)} %add.11.norms_ref.refs_0_), channel_id=1, source_target_pairs={{0,9},{1,8},{2,11},{3,10},{4,13},{5,12},{6,15},{7,14},{8,1},{9,0},... | collective-permute-start | bytes 1544 | tf_op jit(solution)/shard_map/ppermute | solution.py:192
  30.3 4.8 %collective-permute-start.11 = (f32[1,128]{1,0:T(1,128)S(1)}, f32[1,128]{1,0:T(1,128)S(1)}, u32[]{:S(2)}, u32[]{:S(2)}) collective-permute-start(f32[1,128]{1,0:T(1,128)S(1)} %add.11.norms_ref.refs_0_), channel_id=1, source_target_pairs={{0,13},{1,12},{2,15},{3,14},{4,9},{5,8},{6,11},{7,10},{8,5},{9,4},... | collective-permute-start | bytes 1544 | tf_op jit(solution)/shard_map/ppermute | solution.py:192
  32.0 3.1 %collective-permute-start.10 = (f32[1,128]{1,0:T(1,128)S(1)}, f32[1,128]{1,0:T(1,128)S(1)}, u32[]{:S(2)}, u32[]{:S(2)}) collective-permute-start(f32[1,128]{1,0:T(1,128)S(1)} %add.11.norms_ref.refs_0_), channel_id=1, source_target_pairs={{0,5},{1,4},{2,7},{3,6},{4,1},{5,0},{6,3},{7,2},{8,13},{9,12},{10,... | collective-permute-start | bytes 1544 | tf_op jit(solution)/shard_map/ppermute | solution.py:192

commit v4 on v3

--- a/solution.py
+++ b/solution.py
@@ -72,10 +72,12 @@
 
 
 def forward_kernel(n_row, order, own_v, own_u, live_ref, u_bases, v_bases, u_ref, alpha_ref, *refs):
-    blocks, (low_ref, own_ref, total) = in_order(refs[:n_row], order), refs[n_row:]
+    blocks, (low_ref, own_ref, kept_ref, total) = in_order(refs[:n_row], order), refs[n_row:]
     p, c = lax.axis_index("row"), lax.axis_index(("col", "cplx"))
     size = v_bases.shape[4]
     x = jnp.concatenate([b[...] for b in blocks], 0)
+    kept_ref[0] = blocks[0][...]
+    kept_ref[1] = blocks[n_row // 2][...]
     parts = through(v_bases, u_bases, live_ref, lambda q: x[:, q * size : (q + 1) * size], own_v)
     total[...] = sum(parts[1:], parts[0])
     many = own_u // own_v
@@ -109,14 +111,17 @@
     beta2 = to_lanes(squares, place, lanes)
     high = beta2.astype(bf16)
     low = (beta2 - high.astype(f32)).astype(bf16)
-    tail = jnp.where(iota((2 * own_v, lanes), 0) == 0, high.astype(f32), low.astype(f32)).astype(bf16)
+    tail = jnp.where(iota((16, lanes), 0) == 0, high.astype(f32), low.astype(f32)).astype(bf16)
     x = (res * shrink).astype(bf16)
     parts = through(u_bases, v_bases, live_ref, lambda q: x, own_v)
-    wide = parts[0].shape[1]
+    wide = jnp.concatenate(parts, 1).astype(bf16)
+    strips = wide.shape[1] // lanes
     for k, out in enumerate(outs):
-        for q, part in enumerate(parts):
-            out[:, q * wide : (q + 1) * wide] = part[k * 2 * own_v : (k + 1) * 2 * own_v].astype(bf16)
-        out[:, len(parts) * wide :] = tail
+        for i, j in enumerate((k, k ^ (n_row // 2))):
+            for t in range(strips):
+                at = (i * strips + t) * 2 * own_v
+                out[at : at + 2 * own_v, :] = wide[j * 2 * own_v : (j + 1) * 2 * own_v, t * lanes : (t + 1) * lanes]
+        out[2 * strips * 2 * own_v :, :] = tail
 
 
 def pairs(values):
@@ -125,25 +130,36 @@
     return values[0]
 
 
-def residual_kernel(n_row, order, rows_total, cols_total, lanes, v_ref, *refs):
+def residual_kernel(n_row, order, rows_total, cols_total, lanes, v_ref, kept_ref, *refs):
     blocks, (res_ref, beta_ref, norm_ref) = in_order(refs[:n_row], order), refs[n_row:]
     p = lax.axis_index("row")
     own_v, _, wide = v_ref.shape
-    beta2 = pairs([b[0:1, wide:].astype(f32) + b[1:2, wide:].astype(f32) for b in blocks])
+    strips = wide // lanes
+    end = 2 * strips * 2 * own_v
+    beta2 = pairs([b[end : end + 1, :].astype(f32) + b[end + 1 : end + 2, :].astype(f32) for b in blocks])
     beta = jnp.sqrt(beta2 / (2 * rows_total) + epsilon)
     beta_ref[...] = beta
-    mine = to_column(beta, p * own_v, own_v)
-    scale = rows_total / cols_total / shrink / mine
-    squares = None
-    for i in range(2):
-        half = slice(i * own_v, (i + 1) * own_v)
-        back = pairs([b[half, :wide].astype(f32) for b in blocks])
-        res = scale * back - mine * v_ref[:, i, :]
-        res_ref[half, :] = res
-        here = jnp.sum(res * res, axis=1, keepdims=True)
-        squares = here if squares is None else squares + here
-    place = iota((own_v, 1), 0) + p * own_v
-    norm_ref[...] = to_lanes(squares, place, lanes)
+    norms = jnp.zeros((1, lanes), f32)
+    for h, row in enumerate((p, p ^ (n_row // 2))):
+        beta_here = to_column(beta, row * own_v, own_v)
+        beta_here = jnp.concatenate([beta_here, beta_here], 0)
+        scale = rows_total / cols_total / shrink / beta_here
+        squares = jnp.zeros((own_v, lanes), f32)
+        for t in range(strips):
+            at = (h * strips + t) * 2 * own_v
+            back = scale * pairs([b[at : at + 2 * own_v, :].astype(f32) for b in blocks])
+            strip = slice(t * lanes, (t + 1) * lanes)
+            low = beta_here * kept_ref[h, :, strip].astype(f32)
+            for i in range(2):
+                half = slice(i * own_v, (i + 1) * own_v)
+                if h == 0:
+                    res_ref[half, strip] = back[half] - beta_here[half] * v_ref[:, i, strip]
+                res = back[half] - low[half]
+                squares = squares + res * res
+        squares = jnp.sum(squares, axis=1, keepdims=True)
+        place = iota((own_v, 1), 0) + row * own_v
+        norms = norms + to_lanes(squares, place, lanes)
+    norm_ref[...] = norms
 
 
 def turn(beta, scalars_ref):
@@ -152,7 +168,7 @@
     return rho, rhobar / rho, beta / rho, phibar
 
 
-def vectors_kernel(cols_total, norms_ref, beta_ref, res_ref, own_ref, x_ref, w_ref, scalars_ref, x_out, w_out, u_out, v_out):
+def vectors_kernel(cols_total, norms_ref, got_ref, beta_ref, res_ref, own_ref, x_ref, w_ref, scalars_ref, x_out, w_out, u_out, v_out, sum_out):
     p, c = lax.axis_index("row"), lax.axis_index(("col", "cplx"))
     own_v = x_ref.shape[0]
     own_u = u_out.shape[0]
@@ -160,7 +176,9 @@
     rhs = scalars_ref.shape[1]
     beta = beta_ref[:, :rhs]
     rho, cosine, sine, phibar = turn(beta, scalars_ref)
-    alpha2 = to_column(norms_ref[...], p * own_v, own_v)
+    norms = norms_ref[...] + got_ref[...]
+    sum_out[...] = norms
+    alpha2 = to_column(norms, p * own_v, own_v)
     alpha = jnp.sqrt(alpha2 / (2 * cols_total) + epsilon)
     step_x = to_column(cosine * phibar / rho, p * own_v, own_v)
     step_w = to_column(sine / rho, p * own_v, own_v) * alpha
@@ -177,8 +195,8 @@
             u_out[b * own_v : (b + 1) * own_v, i, :] = u / beta_own
 
 
-def scalars_kernel(n_row, cols_total, beta_ref, scalars_ref, *refs):
-    norms, (alpha_out, rhobar_out, phibar_out) = refs[:n_row], refs[n_row:]
+def scalars_kernel(cols_total, beta_ref, scalars_ref, *refs):
+    norms, (alpha_out, rhobar_out, phibar_out) = refs[:-3], refs[-3:]
     rhs = scalars_ref.shape[1]
     rho, cosine, sine, phibar = turn(beta_ref[:, :rhs], scalars_ref)
     alpha2 = sum([n[...] for n in norms[1:]], norms[0][...])[:, :rhs]
@@ -186,6 +204,10 @@
     alpha_out[...] = alpha
     rhobar_out[...] = -cosine * alpha
     phibar_out[...] = sine * phibar
+
+
+def third_of(x):
+    return x
 
 
 def flip(x, axes, mask):
@@ -219,14 +241,13 @@
 
     vmem = 8 + rhs // 16
     first = [1, *range(n_row - 1, 1, -1)]
-    second = [*range(2, n_row), 1]
-    third = first
+    second = [2, 1, *range(3, n_row)]
     scalars = jnp.stack([alpha_prev, rhobar_prev, phibar_prev])
     (v_low,) = call(pack_kernel, [((block, wide), bf16)], v_unit, cost=pl.CostEstimate(flops=10**10, bytes_accessed=2**26, transcendentals=0))
     blocks = [v_low] + [flip(v_low, "row", k) for k in first]
-    low, own = call(
+    low, own, kept = call(
         partial(forward_kernel, n_row, first, own_v, own_u),
-        [((2 * rhs, tile_size), bf16), ((2 * own_u, tile_size), f32)],
+        [((2 * rhs, tile_size), bf16), ((2 * own_u, tile_size), f32), ((2, block, wide), bf16)],
         live,
         u_bases,
         v_bases,
@@ -244,7 +265,7 @@
         mask *= 2
     *outs, own = call(
         partial(adjoint_kernel, n_row, len(got), own_v, own_u, lanes),
-        [((block, wide + lanes), bf16)] * n_row + [((2 * own_u, tile_size), f32)],
+        [((2 * block * (wide // lanes) + 16, lanes), bf16)] * n_row + [((2 * own_u, tile_size), f32)],
         live,
         u_bases,
         v_bases,
@@ -253,23 +274,26 @@
         *got,
         vmem=vmem,
     )
-    blocks = [outs[0]] + [flip(outs[k], "row", k) for k in second]
+    sums = [outs[0]] + [flip(outs[k], "row", k) for k in second]
     residual_v, beta, norms = call(
         partial(residual_kernel, n_row, second, rows_total, cols_total, lanes),
         [((block, wide), f32), ((1, lanes), f32), ((1, lanes), f32)],
         v_unit,
-        *blocks,
+        kept,
+        *sums,
     )
     norms = norms + flip(norms, "cplx", 1)
     mask = n_cplx
-    while mask < n_cols:
+    while 2 * mask < n_cols:
         norms = norms + flip(norms, ("col", "cplx"), mask + 1)
         mask *= 2
-    norms_all = [norms] + [flip(norms, ("row", "col", "cplx"), k * n_cols + 1) for k in third]
-    x_next, w_next, u_next, v_next = call(
+    across = [mask] + [k * n_cols + m for k in range(1, n_row // 2) for m in (0, mask)]
+    got = [flip(norms, ("row", "col", "cplx"), m + 1) for m in across]
+    x_next, w_next, u_next, v_next, norms = call(
         partial(vectors_kernel, cols_total),
-        [(x_solution.shape, f32), (w_direction.shape, f32), (u_unit.shape, f32), (v_unit.shape, f32)],
+        [(x_solution.shape, f32), (w_direction.shape, f32), (u_unit.shape, f32), (v_unit.shape, f32), ((1, lanes), f32)],
         norms,
+        got[0],
         beta,
         residual_v,
         own,
@@ -279,7 +303,7 @@
         cost=pl.CostEstimate(flops=10**9, bytes_accessed=2**23, transcendentals=0),
     )
     alpha, rhobar, phibar = call(
-        partial(scalars_kernel, n_row, cols_total), [((1, rhs), f32)] * 3, beta, scalars, *norms_all
+        partial(scalars_kernel, cols_total), [((1, rhs), f32)] * 3, beta, scalars, norms, *third_of(got[1:])
     )
     return (x_next, w_next, u_next, v_next, alpha[0], rhobar[0], phibar[0])
 

time: 35.8 us -> 34.3 us (0.958)
  waiting for transfers between devices: 15.4 us -> 14.2 us
  starting transfers between devices: 15 us -> 14.6 us
    ppermute x13 -> x12, waiting for transfers between devices: 15.4 us -> 14.2 us  [flip(): lax.ppermute(x, axes, [(i, i ^ mask) for i in range(lax.axis_size(axes))])]
    ppermute x13 -> x12, starting transfers between devices: 15 us -> 14.6 us  [flip(): lax.ppermute(x, axes, [(i, i ^ mask) for i in range(lax.axis_size(axes))])]
  transfers between devices with their start and end apart: 13 -> 12, of which waited for: 8 -> 8; matrix products, arithmetic and copies ran while one was open for 0% -> 0% of each run, Pallas kernels for 2% -> 2%
where the time goes in v4:
time: 34.3 us; the launch traced here: 34.1 us
  starting transfers between devices  14.6 us (43%)
  waiting for transfers between devices  14.2 us (41%)
  Pallas kernels  2.82 us (8%)
  local copies, waits for them, and re-layouts  1.63 us (5%)
  between operations  0.74 us (2%)
    ppermute x12, starting transfers between devices, flip(): lax.ppermute(x, axes, [(i, i ^ mask) for i in range(lax.axis_size(axes))])  14.6 us
    ppermute x12, waiting for transfers between devices, flip(): lax.ppermute(x, axes, [(i, i ^ mask) for i in range(lax.axis_size(axes))])  14.2 us
    pallas_call x6, Pallas kernels, call(): pl.pallas_call(kernel, out_shape=[jax.ShapeDtypeStruct(s, d) for s, d in...  2.82 us
    unnamed x20, local copies, waits for them, and re-layouts  1.63 us
  transfers between devices with their start and end apart: 12, of which 8 were waited for; matrix products, arithmetic and copies ran while one was open for 0% of the time, Pallas kernels for 2%

profile of v4, /device:TPU:0, one launch (start us, length us, event | category | flops | bytes accessed | tf_op | source)
XLA Modules:
  0.0 34.1 jit_solution(7778250961633615073)
XLA Ops:
  0.7 0.9 %copy-done.2 = f32[8,2,1024]{2,1,0:T(2,128)S(1)} copy-done((f32[8,2,1024]{2,1,0:T(2,128)S(1)}, f32[8,2,1024]{2,1,0:T(2,128)}, u32[]{:S(2)}) %copy-start.2) | copy-done | bytes 65560
  1.6 4.1 %collective-permute-start.2 = (bf16[16,1024]{1,0:T(8,128)(2,1)S(1)}, bf16[16,1024]{1,0:T(8,128)(2,1)S(1)}, u32[]{:S(2)}, u32[]{:S(2)}) collective-permute-start(bf16[16,1024]{1,0:T(8,128)(2,1)S(1)} %shard_map.153.refs_0_), channel_id=1, source_target_pairs={{0,8},{4,12},{8,0},{12,4},{1,9},{5,13},{9,1},{13,5},{2,10},{6,14},... | collective-permute-start | bytes 98312 | tf_op jit(solution)/shard_map/ppermute | solution.py:214
  5.7 1.3 %collective-permute-start.1 = (bf16[16,1024]{1,0:T(8,128)(2,1)S(1)}, bf16[16,1024]{1,0:T(8,128)(2,1)S(1)}, u32[]{:S(2)}, u32[]{:S(2)}) collective-permute-start(bf16[16,1024]{1,0:T(8,128)(2,1)S(1)} %shard_map.153.refs_0_), channel_id=1, source_target_pairs={{0,12},{4,8},{8,4},{12,0},{1,13},{5,9},{9,5},{13,1},{2,14},{6,10},... | collective-permute-start | bytes 98312 | tf_op jit(solution)/shard_map/ppermute | solution.py:214
  7.4 0.6 %copy-done.6 = f32[32]{0:T(128)S(1)} copy-done((f32[32]{0:T(128)S(1)}, f32[32]{0:T(128)}, u32[]{:S(2)}) %copy-start.6) | copy-done | bytes 152
  8.1 3.3 %collective-permute-done.1.refs_2_ = bf16[16,1024]{1,0:T(8,128)(2,1)S(1)} collective-permute-done((bf16[16,1024]{1,0:T(8,128)(2,1)S(1)}, bf16[16,1024]{1,0:T(8,128)(2,1)S(1)}, u32[]{:S(2)}, u32[]{:S(2)}) %collective-permute-start.1) | collective-permute-done | bytes 32800 | tf_op jit(solution)/shard_map/ppermute | solution.py:214
  11.4 0.5 %shard_map.154 = (bf16[64,512]{1,0:T(8,128)(2,1)S(1)}, f32[16,512]{1,0:T(8,128)S(1)}, bf16[2,16,1024]{2,1,0:T(8,128)(2,1)S(1)}) custom-call(f32[2,128]{1,0:T(2,128)S(1)} %compare_convert_fusion.live_ref, bf16[1,2,2,128,512]{4,3,2,1,0:T(8,128)(2,1)S(1)} %copy-done, bf16[1,2,2,128,512]{4,3,2,1,0:T(8,128)(2,1)S(1)} %copy-done.1, f32[8,2,512]{2,1,0:T(2,128)S(1)} %copy-done.3, ...), custom_call_target="tpu_custom_call" | custom-call | tf_op jit(solution)/shard_map/pallas_call | solution.py:18
  12.0 1.2 %collective-permute-done.3.refs_0_ = bf16[64,512]{1,0:T(8,128)(2,1)S(1)} collective-permute-done((bf16[64,512]{1,0:T(8,128)(2,1)S(1)}, bf16[64,512]{1,0:T(8,128)(2,1)S(1)}, u32[]{:S(2)}, u32[]{:S(2)}) %collective-permute-start.3) | collective-permute-done | bytes 65568 | tf_op jit(solution)/shard_map/ppermute | solution.py:214
  13.3 1.3 %collective-permute-start.4 = (bf16[64,512]{1,0:T(8,128)(2,1)S(1)}, bf16[64,512]{1,0:T(8,128)(2,1)S(1)}, u32[]{:S(2)}, u32[]{:S(2)}) collective-permute-start(bf16[64,512]{1,0:T(8,128)(2,1)S(1)} %add_convert_fusion.sum_ref), channel_id=1, source_target_pairs={{0,3},{1,2},{2,1},{3,0},{4,7},{5,6},{6,5},{7,4},{8,11},{9,10},{10,... | collective-permute-start | bytes 196616 | tf_op jit(solution)/shard_map/ppermute | solution.py:214
  14.6 2.8 %collective-permute-done.4.refs_1_ = bf16[64,512]{1,0:T(8,128)(2,1)S(1)} collective-permute-done((bf16[64,512]{1,0:T(8,128)(2,1)S(1)}, bf16[64,512]{1,0:T(8,128)(2,1)S(1)}, u32[]{:S(2)}, u32[]{:S(2)}) %collective-permute-start.4) | collective-permute-done | bytes 65568 | tf_op jit(solution)/shard_map/ppermute | solution.py:214
  17.4 0.7 %shard_map.155 = (bf16[272,128]{1,0:T(8,128)(2,1)S(1)}, bf16[272,128]{1,0:T(8,128)(2,1)S(1)}, bf16[272,128]{1,0:T(8,128)(2,1)S(1)}, bf16[272,128]{1,0:T(8,128)(2,1)S(1)}, f32[16,512]{1,0:T(8,128)S(1)}) custom-call(f32[2,128]{1,0:T(2,128)S(1)} %compare_convert_fusion.live_ref, bf16[1,2,2,128,512]{4,3,2,1,0:T(8,128)(2,1)S(1)} %copy-done, ...), custom_call_target="tpu_custom_call" | custom-call | tf_op jit(solution)/shard_map/pallas_call | solution.py:18
  18.1 1.3 %collective-permute-start.5 = (bf16[272,128]{1,0:T(8,128)(2,1)S(1)}, bf16[272,128]{1,0:T(8,128)(2,1)S(1)}, u32[]{:S(2)}, u32[]{:S(2)}) collective-permute-start(bf16[272,128]{1,0:T(8,128)(2,1)S(1)} %get-tuple-element.30), channel_id=1, source_target_pairs={{0,8},{4,12},{8,0},{12,4},{1,9},{5,13},{9,1},{13,5},{2,10},{6,14},... | collective-permute-start | bytes 208904 | tf_op jit(solution)/shard_map/ppermute | solution.py:214
  19.4 1.4 %collective-permute-start.6 = (bf16[272,128]{1,0:T(8,128)(2,1)S(1)}, bf16[272,128]{1,0:T(8,128)(2,1)S(1)}, u32[]{:S(2)}, u32[]{:S(2)}) collective-permute-start(bf16[272,128]{1,0:T(8,128)(2,1)S(1)} %get-tuple-element.31), channel_id=1, source_target_pairs={{0,4},{4,0},{8,12},{12,8},{1,5},{5,1},{9,13},{13,9},{2,6},{6,2},{1... | collective-permute-start | bytes 208904 | tf_op jit(solution)/shard_map/ppermute | solution.py:214
  20.8 1.8 %collective-permute-start.7 = (bf16[272,128]{1,0:T(8,128)(2,1)S(1)}, bf16[272,128]{1,0:T(8,128)(2,1)S(1)}, u32[]{:S(2)}, u32[]{:S(2)}) collective-permute-start(bf16[272,128]{1,0:T(8,128)(2,1)S(1)} %get-tuple-element.32), channel_id=1, source_target_pairs={{0,12},{4,8},{8,4},{12,0},{1,13},{5,9},{9,5},{13,1},{2,14},{6,10},... | collective-permute-start | bytes 208904 | tf_op jit(solution)/shard_map/ppermute | solution.py:214
  22.6 1.7 %collective-permute-done.5.refs_1_ = bf16[272,128]{1,0:T(8,128)(2,1)S(1)} collective-permute-done((bf16[272,128]{1,0:T(8,128)(2,1)S(1)}, bf16[272,128]{1,0:T(8,128)(2,1)S(1)}, u32[]{:S(2)}, u32[]{:S(2)}) %collective-permute-start.5) | collective-permute-done | bytes 69664 | tf_op jit(solution)/shard_map/ppermute | solution.py:214
  24.3 1.4 %collective-permute-done.6.refs_2_ = bf16[272,128]{1,0:T(8,128)(2,1)S(1)} collective-permute-done((bf16[272,128]{1,0:T(8,128)(2,1)S(1)}, bf16[272,128]{1,0:T(8,128)(2,1)S(1)}, u32[]{:S(2)}, u32[]{:S(2)}) %collective-permute-start.6) | collective-permute-done | bytes 69664 | tf_op jit(solution)/shard_map/ppermute | solution.py:214
  25.7 1.3 %collective-permute-done.7.refs_3_ = bf16[272,128]{1,0:T(8,128)(2,1)S(1)} collective-permute-done((bf16[272,128]{1,0:T(8,128)(2,1)S(1)}, bf16[272,128]{1,0:T(8,128)(2,1)S(1)}, u32[]{:S(2)}, u32[]{:S(2)}) %collective-permute-start.7) | collective-permute-done | bytes 69664 | tf_op jit(solution)/shard_map/ppermute | solution.py:214
  27.0 0.3 shard_map.156
  27.3 1.1 %collective-permute-done.8 = f32[1,128]{1,0:T(1,128)S(1)} collective-permute-done((f32[1,128]{1,0:T(1,128)S(1)}, f32[1,128]{1,0:T(1,128)S(1)}, u32[]{:S(2)}, u32[]{:S(2)}) %collective-permute-start.8) | collective-permute-done | bytes 544 | tf_op jit(solution)/shard_map/ppermute | solution.py:214
  28.4 1.3 %collective-permute-start.9 = (f32[1,128]{1,0:T(1,128)S(1)}, f32[1,128]{1,0:T(1,128)S(1)}, u32[]{:S(2)}, u32[]{:S(2)}) collective-permute-start(f32[1,128]{1,0:T(1,128)S(1)} %add.7.norms_ref), channel_id=1, source_target_pairs={{0,3},{1,2},{2,1},{3,0},{4,7},{5,6},{6,5},{7,4},{8,11},{9,10},{10,... | collective-permute-start | bytes 1544 | tf_op jit(solution)/shard_map/ppermute | solution.py:214
  29.7 0.7 %collective-permute-start.11 = (f32[1,128]{1,0:T(1,128)S(1)}, f32[1,128]{1,0:T(1,128)S(1)}, u32[]{:S(2)}, u32[]{:S(2)}) collective-permute-start(f32[1,128]{1,0:T(1,128)S(1)} %add.7.norms_ref), channel_id=1, source_target_pairs={{0,7},{1,6},{2,5},{3,4},{4,3},{5,2},{6,1},{7,0},{8,15},{9,14},{10,... | collective-permute-start | bytes 1544 | tf_op jit(solution)/shard_map/ppermute | solution.py:214
  30.4 1.1 %collective-permute-start.10 = (f32[1,128]{1,0:T(1,128)S(1)}, f32[1,128]{1,0:T(1,128)S(1)}, u32[]{:S(2)}, u32[]{:S(2)}) collective-permute-start(f32[1,128]{1,0:T(1,128)S(1)} %add.7.norms_ref), channel_id=1, source_target_pairs={{0,5},{1,4},{2,7},{3,6},{4,1},{5,0},{6,3},{7,2},{8,13},{9,12},{10,... | collective-permute-start | bytes 1544 | tf_op jit(solution)/shard_map/ppermute | solution.py:214
  31.5 0.8 %shard_map.157 = (f32[8,2,1024]{2,1,0:T(2,128)}, f32[8,2,1024]{2,1,0:T(2,128)}, f32[8,2,512]{2,1,0:T(2,128)}, f32[8,2,1024]{2,1,0:T(2,128)}, f32[1,128]{1,0:T(1,128)S(1)}) custom-call(f32[1,128]{1,0:T(1,128)S(1)} %add.7.norms_ref, f32[1,128]{1,0:T(1,128)S(1)} %collective-permute-done.9.got_ref, f32[1,128]{1,0:T(1,128)S(1)} %get-tuple-element.34.beta_ref, ...), custom_call_target="tpu_custom_call" | custom-call | flops 1000000000 | bytes 8388608 | tf_op jit(solution)/shard_map/pallas_call | solution.py:18
  32.3 1.3 %collective-permute-done.11.refs_2_ = f32[1,128]{1,0:T(1,128)S(1)} collective-permute-done((f32[1,128]{1,0:T(1,128)S(1)}, f32[1,128]{1,0:T(1,128)S(1)}, u32[]{:S(2)}, u32[]{:S(2)}) %collective-permute-start.11) | collective-permute-done | bytes 544 | tf_op jit(solution)/shard_map/ppermute | solution.py:214
  33.6 0.5 %shard_map.158 = (f32[1,32]{1,0:T(1,128)}, f32[1,32]{1,0:T(1,128)}, f32[1,32]{1,0:T(1,128)}) custom-call(f32[1,128]{1,0:T(1,128)S(1)} %get-tuple-element.34.beta_ref, f32[3,32]{1,0:T(4,128)S(1)} %pad_maximum_fusion.alpha_ref.scalars_ref, f32[1,128]{1,0:T(1,128)S(1)} %get-tuple-element.41.refs_0_, f32[1,128]{1,0:T(1,128)S(1)} %collective-permute-done.10.refs_1_, ...), custom_call_target="tpu_custom_call" | custom-call | tf_op jit(solution)/shard_map/pallas_call | solution.py:18
  (30 shorter events, 0.6 us)
Async XLA Ops:
  0.6 10.8 %copy-start.1 = (bf16[1,2,2,128,512]{4,3,2,1,0:T(8,128)(2,1)S(1)}, bf16[1,2,2,128,512]{4,3,2,1,0:T(8,128)(2,1)}, u32[]{:S(2)}) copy-start(bf16[1,2,2,128,512]{4,3,2,1,0:T(8,128)(2,1)} %v_bases.3) | copy-start | bytes 1572868
  0.6 10.8 %copy-start = (bf16[1,2,2,128,512]{4,3,2,1,0:T(8,128)(2,1)S(1)}, bf16[1,2,2,128,512]{4,3,2,1,0:T(8,128)(2,1)}, u32[]{:S(2)}) copy-start(bf16[1,2,2,128,512]{4,3,2,1,0:T(8,128)(2,1)} %u_bases.3) | copy-start | bytes 1572868
  0.7 0.9 %copy-start.2 = (f32[8,2,1024]{2,1,0:T(2,128)S(1)}, f32[8,2,1024]{2,1,0:T(2,128)}, u32[]{:S(2)}) copy-start(f32[8,2,1024]{2,1,0:T(2,128)} %v_ref.3) | copy-start | bytes 196612
  1.6 9.9 %copy-start.3 = (f32[8,2,512]{2,1,0:T(2,128)S(1)}, f32[8,2,512]{2,1,0:T(2,128)}, u32[]{:S(2)}) copy-start(f32[8,2,512]{2,1,0:T(2,128)} %u_ref.1) | copy-start | bytes 98308
  1.6 5.7 %copy-start.9 = (s32[1,2]{1,0:T(1,128)S(1)}, s32[1,2]{1,0:T(1,128)}, u32[]{:S(2)}) copy-start(s32[1,2]{1,0:T(1,128)} %param.12) | copy-start | bytes 28
  1.6 6.5 %collective-permute-start.2 = (bf16[16,1024]{1,0:T(8,128)(2,1)S(1)}, bf16[16,1024]{1,0:T(8,128)(2,1)S(1)}, u32[]{:S(2)}, u32[]{:S(2)}) collective-permute-start(bf16[16,1024]{1,0:T(8,128)(2,1)S(1)} %shard_map.153.refs_0_), channel_id=1, source_target_pairs={{0,8},{4,12},{8,0},{12,4},{1,9},{5,13},{9,1},{13,5},{2,10},{6,14},... | collective-permute-start | bytes 98312 | tf_op jit(solution)/shard_map/ppermute | solution.py:214
  5.7 5.7 %collective-permute-start.1 = (bf16[16,1024]{1,0:T(8,128)(2,1)S(1)}, bf16[16,1024]{1,0:T(8,128)(2,1)S(1)}, u32[]{:S(2)}, u32[]{:S(2)}) collective-permute-start(bf16[16,1024]{1,0:T(8,128)(2,1)S(1)} %shard_map.153.refs_0_), channel_id=1, source_target_pairs={{0,12},{4,8},{8,4},{12,0},{1,13},{5,9},{9,5},{13,1},{2,14},{6,10},... | collective-permute-start | bytes 98312 | tf_op jit(solution)/shard_map/ppermute | solution.py:214
  7.1 4.4 %collective-permute-start = (bf16[16,1024]{1,0:T(8,128)(2,1)S(1)}, bf16[16,1024]{1,0:T(8,128)(2,1)S(1)}, u32[]{:S(2)}, u32[]{:S(2)}) collective-permute-start(bf16[16,1024]{1,0:T(8,128)(2,1)S(1)} %shard_map.153.refs_0_), channel_id=1, source_target_pairs={{0,4},{4,0},{8,12},{12,8},{1,5},{5,1},{9,13},{13,9},{2,6},{6,2},{1... | collective-permute-start | bytes 98312 | tf_op jit(solution)/shard_map/ppermute | solution.py:214
  7.4 0.7 %copy-start.6 = (f32[32]{0:T(128)S(1)}, f32[32]{0:T(128)}, u32[]{:S(2)}) copy-start(f32[32]{0:T(128)} %param.19) | copy-start | bytes 388
  7.4 0.7 %copy-start.7 = (f32[32]{0:T(128)S(1)}, f32[32]{0:T(128)}, u32[]{:S(2)}) copy-start(f32[32]{0:T(128)} %param.18) | copy-start | bytes 388
  7.4 0.7 %copy-start.8 = (f32[32]{0:T(128)S(1)}, f32[32]{0:T(128)}, u32[]{:S(2)}) copy-start(f32[32]{0:T(128)} %param.17) | copy-start | bytes 388
  11.9 1.3 %collective-permute-start.3 = (bf16[64,512]{1,0:T(8,128)(2,1)S(1)}, bf16[64,512]{1,0:T(8,128)(2,1)S(1)}, u32[]{:S(2)}, u32[]{:S(2)}) collective-permute-start(bf16[64,512]{1,0:T(8,128)(2,1)S(1)} %get-tuple-element.28), channel_id=1, source_target_pairs={{0,1},{1,0},{2,3},{3,2},{4,5},{5,4},{6,7},{7,6},{8,9},{9,8},{10,11... | collective-permute-start | bytes 196616 | tf_op jit(solution)/shard_map/ppermute | solution.py:214
  13.3 4.1 %collective-permute-start.4 = (bf16[64,512]{1,0:T(8,128)(2,1)S(1)}, bf16[64,512]{1,0:T(8,128)(2,1)S(1)}, u32[]{:S(2)}, u32[]{:S(2)}) collective-permute-start(bf16[64,512]{1,0:T(8,128)(2,1)S(1)} %add_convert_fusion.sum_ref), channel_id=1, source_target_pairs={{0,3},{1,2},{2,1},{3,0},{4,7},{5,6},{6,5},{7,4},{8,11},{9,10},{10,... | collective-permute-start | bytes 196616 | tf_op jit(solution)/shard_map/ppermute | solution.py:214
  18.1 6.2 %collective-permute-start.5 = (bf16[272,128]{1,0:T(8,128)(2,1)S(1)}, bf16[272,128]{1,0:T(8,128)(2,1)S(1)}, u32[]{:S(2)}, u32[]{:S(2)}) collective-permute-start(bf16[272,128]{1,0:T(8,128)(2,1)S(1)} %get-tuple-element.30), channel_id=1, source_target_pairs={{0,8},{4,12},{8,0},{12,4},{1,9},{5,13},{9,1},{13,5},{2,10},{6,14},... | collective-permute-start | bytes 208904 | tf_op jit(solution)/shard_map/ppermute | solution.py:214
  19.4 6.3 %collective-permute-start.6 = (bf16[272,128]{1,0:T(8,128)(2,1)S(1)}, bf16[272,128]{1,0:T(8,128)(2,1)S(1)}, u32[]{:S(2)}, u32[]{:S(2)}) collective-permute-start(bf16[272,128]{1,0:T(8,128)(2,1)S(1)} %get-tuple-element.31), channel_id=1, source_target_pairs={{0,4},{4,0},{8,12},{12,8},{1,5},{5,1},{9,13},{13,9},{2,6},{6,2},{1... | collective-permute-start | bytes 208904 | tf_op jit(solution)/shard_map/ppermute | solution.py:214
  20.8 6.2 %collective-permute-start.7 = (bf16[272,128]{1,0:T(8,128)(2,1)S(1)}, bf16[272,128]{1,0:T(8,128)(2,1)S(1)}, u32[]{:S(2)}, u32[]{:S(2)}) collective-permute-start(bf16[272,128]{1,0:T(8,128)(2,1)S(1)} %get-tuple-element.32), channel_id=1, source_target_pairs={{0,12},{4,8},{8,4},{12,0},{1,13},{5,9},{9,5},{13,1},{2,14},{6,10},... | collective-permute-start | bytes 208904 | tf_op jit(solution)/shard_map/ppermute | solution.py:214
  27.0 4.5 %copy-start.4 = (f32[8,2,1024]{2,1,0:T(2,128)S(1)}, f32[8,2,1024]{2,1,0:T(2,128)}, u32[]{:S(2)}) copy-start(f32[8,2,1024]{2,1,0:T(2,128)} %x_ref.1) | copy-start | bytes 196612
  27.0 4.5 %copy-start.5 = (f32[8,2,1024]{2,1,0:T(2,128)S(1)}, f32[8,2,1024]{2,1,0:T(2,128)}, u32[]{:S(2)}) copy-start(f32[8,2,1024]{2,1,0:T(2,128)} %w_ref.1) | copy-start | bytes 196612
  27.3 1.2 %collective-permute-start.8 = (f32[1,128]{1,0:T(1,128)S(1)}, f32[1,128]{1,0:T(1,128)S(1)}, u32[]{:S(2)}, u32[]{:S(2)}) collective-permute-start(f32[1,128]{1,0:T(1,128)S(1)} %get-tuple-element.33), channel_id=1, source_target_pairs={{0,1},{1,0},{2,3},{3,2},{4,5},{5,4},{6,7},{7,6},{8,9},{9,8},{10,11... | collective-permute-start | bytes 1544 | tf_op jit(solution)/shard_map/ppermute | solution.py:214
  28.4 3.0 %collective-permute-start.9 = (f32[1,128]{1,0:T(1,128)S(1)}, f32[1,128]{1,0:T(1,128)S(1)}, u32[]{:S(2)}, u32[]{:S(2)}) collective-permute-start(f32[1,128]{1,0:T(1,128)S(1)} %add.7.norms_ref), channel_id=1, source_target_pairs={{0,3},{1,2},{2,1},{3,0},{4,7},{5,6},{6,5},{7,4},{8,11},{9,10},{10,... | collective-permute-start | bytes 1544 | tf_op jit(solution)/shard_map/ppermute | solution.py:214
  29.7 3.9 %collective-permute-start.11 = (f32[1,128]{1,0:T(1,128)S(1)}, f32[1,128]{1,0:T(1,128)S(1)}, u32[]{:S(2)}, u32[]{:S(2)}) collective-permute-start(f32[1,128]{1,0:T(1,128)S(1)} %add.7.norms_ref), channel_id=1, source_target_pairs={{0,7},{1,6},{2,5},{3,4},{4,3},{5,2},{6,1},{7,0},{8,15},{9,14},{10,... | collective-permute-start | bytes 1544 | tf_op jit(solution)/shard_map/ppermute | solution.py:214
  30.4 3.2 %collective-permute-start.10 = (f32[1,128]{1,0:T(1,128)S(1)}, f32[1,128]{1,0:T(1,128)S(1)}, u32[]{:S(2)}, u32[]{:S(2)}) collective-permute-start(f32[1,128]{1,0:T(1,128)S(1)} %add.7.norms_ref), channel_id=1, source_target_pairs={{0,5},{1,4},{2,7},{3,6},{4,1},{5,0},{6,3},{7,2},{8,13},{9,12},{10,... | collective-permute-start | bytes 1544 | tf_op jit(solution)/shard_map/ppermute | solution.py:214

commit v5 on v4

--- a/solution.py
+++ b/solution.py
@@ -47,28 +47,30 @@
 
 
 def through(inner, outer, live_ref, x, own):
-    total = []
     tiles, _, ranks, size = inner.shape[1:]
-    for q in range(tiles):
-        g = dot(x(q), inner[0, q].reshape(2 * ranks, size), True)
+    mids = []
+    gs = [dot(x(q), inner[0, q].reshape(2 * ranks, size), True) for q in range(tiles)]
+    for q, g in enumerate(gs):
         rows = g.shape[0]
         g = g.reshape(rows // (2 * own), 2, own, 2 * ranks)
         live = live_ref[q : q + 1, :]
         re = (g[:, 0, :, :ranks] + g[:, 1, :, ranks:]) * live
         im = (g[:, 1, :, :ranks] - g[:, 0, :, ranks:]) * live
         both = jnp.stack([jnp.concatenate([re, -im], 2), jnp.concatenate([im, re], 2)], 1)
-        both = both.reshape(rows, 2 * ranks).astype(bf16)
-        total.append(dot(both, outer[0, q].reshape(2 * ranks, size), False))
-    return total
+        mids.append(both.reshape(rows, 2 * ranks).astype(bf16))
+    return [dot(both, outer[0, q].reshape(2 * ranks, size), False) for q, both in enumerate(mids)]
 
 
 def in_order(blocks, order):
     return [blocks[0]] + [blocks[1 + order.index(k)] for k in range(1, len(blocks))]
 
 
-def pack_kernel(v_ref, out_ref):
-    own = v_ref.shape[0]
-    out_ref[...] = jnp.concatenate([v_ref[:, 0, :], v_ref[:, 1, :]], 0).astype(bf16)
+def prepare_kernel(ranks_ref, alpha_ref, rhobar_ref, phibar_ref, live_ref, scalars_ref):
+    for q in range(live_ref.shape[0]):
+        here = iota((1, live_ref.shape[1]), 1) < ranks_ref[0:1, q : q + 1]
+        live_ref[q : q + 1, :] = here.astype(f32)
+    for i, ref in enumerate((alpha_ref, rhobar_ref, phibar_ref)):
+        scalars_ref[i : i + 1, :] = ref[...]
 
 
 def forward_kernel(n_row, order, own_v, own_u, live_ref, u_bases, v_bases, u_ref, alpha_ref, *refs):
@@ -237,13 +239,22 @@
     rhs = own_v * n_row
     lanes = -(-rhs // 128) * 128
     block = 2 * own_v
-    live = (jnp.arange(u_bases.shape[3], dtype=jnp.int32)[None] < tile_ranks[0][:, None]).astype(f32)
-
     vmem = 8 + rhs // 16
     first = [1, *range(n_row - 1, 1, -1)]
-    second = [2, 1, *range(3, n_row)]
+    second = [*range(2, n_row), 1]
+    live, scalars = call(
+        prepare_kernel,
+        [((u_bases.shape[1], u_bases.shape[3]), f32), ((3, rhs), f32)],
+        tile_ranks,
+        alpha_prev[None],
+        rhobar_prev[None],
+        phibar_prev[None],
+        cost=pl.CostEstimate(flops=10**10, bytes_accessed=2**26, transcendentals=0),
+    )
+    first = [1, *range(n_row - 1, 1, -1)]
+    second = [*range(2, n_row), 1]
     scalars = jnp.stack([alpha_prev, rhobar_prev, phibar_prev])
-    (v_low,) = call(pack_kernel, [((block, wide), bf16)], v_unit, cost=pl.CostEstimate(flops=10**10, bytes_accessed=2**26, transcendentals=0))
+    v_low = jnp.swapaxes(v_unit, 0, 1).reshape(block, wide).astype(bf16)
     blocks = [v_low] + [flip(v_low, "row", k) for k in first]
     low, own, kept = call(
         partial(forward_kernel, n_row, first, own_v, own_u),

time: 34.3 us -> 34.1 us (level)
  starting transfers between devices: 14.6 us -> 13.7 us
  local copies, waits for them, and re-layouts: 1.63 us -> 0.73 us
  other arithmetic: 0.1 us -> 0.9 us
  waiting for transfers between devices: 14.2 us -> 14.8 us
    unnamed x20, local copies, waits for them, and re-layouts: 1.63 us -> 0.72 us
    ppermute x12, starting transfers between devices: 14.6 us -> 13.7 us  [flip(): lax.ppermute(x, axes, [(i, i ^ mask) for i in range(lax.axis_size(axes))])]
    convert_element_type x1, other arithmetic: 0.07 us -> 0.87 us  [body(): v_low = jnp.swapaxes(v_unit, 0, 1).reshape(block, wide).astype(bf16)]
    ppermute x12, waiting for transfers between devices: 14.2 us -> 14.8 us  [flip(): lax.ppermute(x, axes, [(i, i ^ mask) for i in range(lax.axis_size(axes))])]
  transfers between devices with their start and end apart: 12 -> 12, of which waited for: 8 -> 8; matrix products, arithmetic and copies ran while one was open for 0% -> 0% of each run, Pallas kernels for 2% -> 4%
where the time goes in v5:
time: 34.1 us; the launch traced here: 33.9 us
  waiting for transfers between devices  14.8 us (43%)
  starting transfers between devices  13.7 us (40%)
  Pallas kernels  3.12 us (9%)
  other arithmetic  0.9 us (3%)
  local copies, waits for them, and re-layouts  0.73 us (2%)
  between operations  0.73 us (2%)
    ppermute x12, waiting for transfers between devices, flip(): lax.ppermute(x, axes, [(i, i ^ mask) for i in range(lax.axis_size(axes))])  14.8 us
    ppermute x12, starting transfers between devices, flip(): lax.ppermute(x, axes, [(i, i ^ mask) for i in range(lax.axis_size(axes))])  13.7 us
    pallas_call x6, Pallas kernels, call(): pl.pallas_call(kernel, out_shape=[jax.ShapeDtypeStruct(s, d) for s, d in...  3.12 us
    convert_element_type x1, other arithmetic, body(): v_low = jnp.swapaxes(v_unit, 0, 1).reshape(block, wide).astype(bf16)  0.87 us
    unnamed x20, local copies, waits for them, and re-layouts  0.72 us
  transfers between devices with their start and end apart: 12, of which 8 were waited for; matrix products, arithmetic and copies ran while one was open for 0% of the time, Pallas kernels for 4%

profile of v5, /device:TPU:0, one launch (start us, length us, event | category | flops | bytes accessed | tf_op | source)
XLA Modules:
  0.0 33.9 jit_solution(990760602034231499)
XLA Ops:
  0.6 0.9 %convert_bitcast_fusion = bf16[2,8,1024]{2,0,1:T(2,128)(2,1)S(1)} fusion(f32[8,2,1024]{2,1,0:T(2,128)} %v_ref.1), kind=kLoop, calls=%fused_computation.2 | loop fusion | flops 16384 | bytes 98304 | tf_op jit(solution)/shard_map/convert_element_type | solution.py:257
  1.5 4.1 %collective-permute-start.2 = (bf16[16,1024]{1,0:T(8,128)(2,1)S(1)}, bf16[16,1024]{1,0:T(8,128)(2,1)S(1)}, u32[]{:S(2)}, u32[]{:S(2)}) collective-permute-start(bf16[16,1024]{1,0:T(8,128)(2,1)S(1)} %bitcast.11), channel_id=1, source_target_pairs={{0,8},{4,12},{8,0},{12,4},{1,9},{5,13},{9,1},{13,5},{2,10},{6,14},... | collective-permute-start | bytes 98312 | tf_op jit(solution)/shard_map/ppermute | solution.py:216
  5.6 1.3 %collective-permute-start.1 = (bf16[16,1024]{1,0:T(8,128)(2,1)S(1)}, bf16[16,1024]{1,0:T(8,128)(2,1)S(1)}, u32[]{:S(2)}, u32[]{:S(2)}) collective-permute-start(bf16[16,1024]{1,0:T(8,128)(2,1)S(1)} %bitcast.12), channel_id=1, source_target_pairs={{0,12},{4,8},{8,4},{12,0},{1,13},{5,9},{9,5},{13,1},{2,14},{6,10},... | collective-permute-start | bytes 98312 | tf_op jit(solution)/shard_map/ppermute | solution.py:216
  7.2 0.6 %copy-done.9 = s32[1,2]{1,0:T(1,128)S(1)} copy-done((s32[1,2]{1,0:T(1,128)S(1)}, s32[1,2]{1,0:T(1,128)}, u32[]{:S(2)}) %copy-start.9) | copy-done | bytes 32
  7.9 0.6 %shard_map.153 = (f32[2,128]{1,0:T(2,128)S(1)}, f32[3,32]{1,0:T(4,128)}) custom-call(s32[1,2]{1,0:T(1,128)S(1)} %copy-done.9, f32[1,32]{1,0:T(1,128)S(1)} %bitcast.15, f32[1,32]{1,0:T(1,128)S(1)} %bitcast.17, f32[1,32]{1,0:T(1,128)S(1)} %bitcast.19), custom_call_target="tpu_custom_call" | custom-call | flops 10000000000 | bytes 67108864 | tf_op jit(solution)/shard_map/pallas_call | solution.py:18
  8.5 2.8 %collective-permute-done.1.refs_2_ = bf16[16,1024]{1,0:T(8,128)(2,1)S(1)} collective-permute-done((bf16[16,1024]{1,0:T(8,128)(2,1)S(1)}, bf16[16,1024]{1,0:T(8,128)(2,1)S(1)}, u32[]{:S(2)}, u32[]{:S(2)}) %collective-permute-start.1) | collective-permute-done | bytes 32800 | tf_op jit(solution)/shard_map/ppermute | solution.py:216
  11.4 0.5 %shard_map.154 = (bf16[64,512]{1,0:T(8,128)(2,1)S(1)}, f32[16,512]{1,0:T(8,128)S(1)}, bf16[2,16,1024]{2,1,0:T(8,128)(2,1)S(1)}) custom-call(f32[2,128]{1,0:T(2,128)S(1)} %get-tuple-element.27.live_ref, bf16[1,2,2,128,512]{4,3,2,1,0:T(8,128)(2,1)S(1)} %copy-done, bf16[1,2,2,128,512]{4,3,2,1,0:T(8,128)(2,1)S(1)} %copy-done.1, f32[8,2,512]{2,1,0:T(2,128)S(1)} %copy-done.3, ...), custom_call_target="tpu_custom_call" | custom-call | tf_op jit(solution)/shard_map/pallas_call | solution.py:18
  11.9 1.2 %collective-permute-done.3.refs_0_ = bf16[64,512]{1,0:T(8,128)(2,1)S(1)} collective-permute-done((bf16[64,512]{1,0:T(8,128)(2,1)S(1)}, bf16[64,512]{1,0:T(8,128)(2,1)S(1)}, u32[]{:S(2)}, u32[]{:S(2)}) %collective-permute-start.3) | collective-permute-done | bytes 65568 | tf_op jit(solution)/shard_map/ppermute | solution.py:216
  13.2 1.3 %collective-permute-start.4 = (bf16[64,512]{1,0:T(8,128)(2,1)S(1)}, bf16[64,512]{1,0:T(8,128)(2,1)S(1)}, u32[]{:S(2)}, u32[]{:S(2)}) collective-permute-start(bf16[64,512]{1,0:T(8,128)(2,1)S(1)} %add_convert_fusion.sum_ref), channel_id=1, source_target_pairs={{0,3},{1,2},{2,1},{3,0},{4,7},{5,6},{6,5},{7,4},{8,11},{9,10},{10,... | collective-permute-start | bytes 196616 | tf_op jit(solution)/shard_map/ppermute | solution.py:216
  14.5 2.8 %collective-permute-done.4.refs_1_ = bf16[64,512]{1,0:T(8,128)(2,1)S(1)} collective-permute-done((bf16[64,512]{1,0:T(8,128)(2,1)S(1)}, bf16[64,512]{1,0:T(8,128)(2,1)S(1)}, u32[]{:S(2)}, u32[]{:S(2)}) %collective-permute-start.4) | collective-permute-done | bytes 65568 | tf_op jit(solution)/shard_map/ppermute | solution.py:216
  17.3 0.4 %shard_map.155 = (bf16[272,128]{1,0:T(8,128)(2,1)S(1)}, bf16[272,128]{1,0:T(8,128)(2,1)S(1)}, bf16[272,128]{1,0:T(8,128)(2,1)S(1)}, bf16[272,128]{1,0:T(8,128)(2,1)S(1)}, f32[16,512]{1,0:T(8,128)S(1)}) custom-call(f32[2,128]{1,0:T(2,128)S(1)} %get-tuple-element.27.live_ref, bf16[1,2,2,128,512]{4,3,2,1,0:T(8,128)(2,1)S(1)} %copy-done, ...), custom_call_target="tpu_custom_call" | custom-call | tf_op jit(solution)/shard_map/pallas_call | solution.py:18
  17.7 1.3 %collective-permute-start.5 = (bf16[272,128]{1,0:T(8,128)(2,1)S(1)}, bf16[272,128]{1,0:T(8,128)(2,1)S(1)}, u32[]{:S(2)}, u32[]{:S(2)}) collective-permute-start(bf16[272,128]{1,0:T(8,128)(2,1)S(1)} %get-tuple-element.32), channel_id=1, source_target_pairs={{0,8},{4,12},{8,0},{12,4},{1,9},{5,13},{9,1},{13,5},{2,10},{6,14},... | collective-permute-start | bytes 208904 | tf_op jit(solution)/shard_map/ppermute | solution.py:216
  19.0 1.0 %collective-permute-start.6 = (bf16[272,128]{1,0:T(8,128)(2,1)S(1)}, bf16[272,128]{1,0:T(8,128)(2,1)S(1)}, u32[]{:S(2)}, u32[]{:S(2)}) collective-permute-start(bf16[272,128]{1,0:T(8,128)(2,1)S(1)} %get-tuple-element.33), channel_id=1, source_target_pairs={{0,12},{4,8},{8,4},{12,0},{1,13},{5,9},{9,5},{13,1},{2,14},{6,10},... | collective-permute-start | bytes 208904 | tf_op jit(solution)/shard_map/ppermute | solution.py:216
  20.1 1.2 %collective-permute-start.7 = (bf16[272,128]{1,0:T(8,128)(2,1)S(1)}, bf16[272,128]{1,0:T(8,128)(2,1)S(1)}, u32[]{:S(2)}, u32[]{:S(2)}) collective-permute-start(bf16[272,128]{1,0:T(8,128)(2,1)S(1)} %get-tuple-element.34), channel_id=1, source_target_pairs={{0,4},{4,0},{8,12},{12,8},{1,5},{5,1},{9,13},{13,9},{2,6},{6,2},{1... | collective-permute-start | bytes 208904 | tf_op jit(solution)/shard_map/ppermute | solution.py:216
  21.3 3.7 %collective-permute-done.5.refs_1_ = bf16[272,128]{1,0:T(8,128)(2,1)S(1)} collective-permute-done((bf16[272,128]{1,0:T(8,128)(2,1)S(1)}, bf16[272,128]{1,0:T(8,128)(2,1)S(1)}, u32[]{:S(2)}, u32[]{:S(2)}) %collective-permute-start.5) | collective-permute-done | bytes 69664 | tf_op jit(solution)/shard_map/ppermute | solution.py:216
  25.0 0.6 %collective-permute-done.6.refs_2_ = bf16[272,128]{1,0:T(8,128)(2,1)S(1)} collective-permute-done((bf16[272,128]{1,0:T(8,128)(2,1)S(1)}, bf16[272,128]{1,0:T(8,128)(2,1)S(1)}, u32[]{:S(2)}, u32[]{:S(2)}) %collective-permute-start.6) | collective-permute-done | bytes 69664 | tf_op jit(solution)/shard_map/ppermute | solution.py:216
  25.6 1.2 %collective-permute-done.7.refs_3_ = bf16[272,128]{1,0:T(8,128)(2,1)S(1)} collective-permute-done((bf16[272,128]{1,0:T(8,128)(2,1)S(1)}, bf16[272,128]{1,0:T(8,128)(2,1)S(1)}, u32[]{:S(2)}, u32[]{:S(2)}) %collective-permute-start.7) | collective-permute-done | bytes 69664 | tf_op jit(solution)/shard_map/ppermute | solution.py:216
  27.1 1.1 %collective-permute-done.8 = f32[1,128]{1,0:T(1,128)S(1)} collective-permute-done((f32[1,128]{1,0:T(1,128)S(1)}, f32[1,128]{1,0:T(1,128)S(1)}, u32[]{:S(2)}, u32[]{:S(2)}) %collective-permute-start.8) | collective-permute-done | bytes 544 | tf_op jit(solution)/shard_map/ppermute | solution.py:216
  28.2 1.3 %collective-permute-start.9 = (f32[1,128]{1,0:T(1,128)S(1)}, f32[1,128]{1,0:T(1,128)S(1)}, u32[]{:S(2)}, u32[]{:S(2)}) collective-permute-start(f32[1,128]{1,0:T(1,128)S(1)} %add.7.norms_ref), channel_id=1, source_target_pairs={{0,3},{1,2},{2,1},{3,0},{4,7},{5,6},{6,5},{7,4},{8,11},{9,10},{10,... | collective-permute-start | bytes 1544 | tf_op jit(solution)/shard_map/ppermute | solution.py:216
  29.5 0.6 %collective-permute-start.11 = (f32[1,128]{1,0:T(1,128)S(1)}, f32[1,128]{1,0:T(1,128)S(1)}, u32[]{:S(2)}, u32[]{:S(2)}) collective-permute-start(f32[1,128]{1,0:T(1,128)S(1)} %add.7.norms_ref), channel_id=1, source_target_pairs={{0,7},{1,6},{2,5},{3,4},{4,3},{5,2},{6,1},{7,0},{8,15},{9,14},{10,... | collective-permute-start | bytes 1544 | tf_op jit(solution)/shard_map/ppermute | solution.py:216
  30.1 1.2 %collective-permute-start.10 = (f32[1,128]{1,0:T(1,128)S(1)}, f32[1,128]{1,0:T(1,128)S(1)}, u32[]{:S(2)}, u32[]{:S(2)}) collective-permute-start(f32[1,128]{1,0:T(1,128)S(1)} %add.7.norms_ref), channel_id=1, source_target_pairs={{0,5},{1,4},{2,7},{3,6},{4,1},{5,0},{6,3},{7,2},{8,13},{9,12},{10,... | collective-permute-start | bytes 1544 | tf_op jit(solution)/shard_map/ppermute | solution.py:216
  31.3 0.8 %shard_map.157 = (f32[8,2,1024]{2,1,0:T(2,128)}, f32[8,2,1024]{2,1,0:T(2,128)}, f32[8,2,512]{2,1,0:T(2,128)}, f32[8,2,1024]{2,1,0:T(2,128)}, f32[1,128]{1,0:T(1,128)S(1)}) custom-call(f32[1,128]{1,0:T(1,128)S(1)} %add.7.norms_ref, f32[1,128]{1,0:T(1,128)S(1)} %collective-permute-done.9.got_ref, f32[1,128]{1,0:T(1,128)S(1)} %get-tuple-element.36.beta_ref, ...), custom_call_target="tpu_custom_call" | custom-call | flops 1000000000 | bytes 8388608 | tf_op jit(solution)/shard_map/pallas_call | solution.py:18
  32.1 1.3 %collective-permute-done.11.refs_2_ = f32[1,128]{1,0:T(1,128)S(1)} collective-permute-done((f32[1,128]{1,0:T(1,128)S(1)}, f32[1,128]{1,0:T(1,128)S(1)}, u32[]{:S(2)}, u32[]{:S(2)}) %collective-permute-start.11) | collective-permute-done | bytes 544 | tf_op jit(solution)/shard_map/ppermute | solution.py:216
  33.4 0.5 %shard_map.158 = (f32[1,32]{1,0:T(1,128)}, f32[1,32]{1,0:T(1,128)}, f32[1,32]{1,0:T(1,128)}) custom-call(f32[1,128]{1,0:T(1,128)S(1)} %get-tuple-element.36.beta_ref, f32[3,32]{1,0:T(4,128)S(1)} %pad_maximum_fusion.alpha_ref.scalars_ref, f32[1,128]{1,0:T(1,128)S(1)} %get-tuple-element.43.refs_0_, f32[1,128]{1,0:T(1,128)S(1)} %collective-permute-done.10.refs_1_, ...), custom_call_target="tpu_custom_call" | custom-call | tf_op jit(solution)/shard_map/pallas_call | solution.py:18
  (31 shorter events, 0.8 us)
Async XLA Ops:
  1.5 7.0 %collective-permute-start.2 = (bf16[16,1024]{1,0:T(8,128)(2,1)S(1)}, bf16[16,1024]{1,0:T(8,128)(2,1)S(1)}, u32[]{:S(2)}, u32[]{:S(2)}) collective-permute-start(bf16[16,1024]{1,0:T(8,128)(2,1)S(1)} %bitcast.11), channel_id=1, source_target_pairs={{0,8},{4,12},{8,0},{12,4},{1,9},{5,13},{9,1},{13,5},{2,10},{6,14},... | collective-permute-start | bytes 98312 | tf_op jit(solution)/shard_map/ppermute | solution.py:216
  5.6 5.7 %collective-permute-start.1 = (bf16[16,1024]{1,0:T(8,128)(2,1)S(1)}, bf16[16,1024]{1,0:T(8,128)(2,1)S(1)}, u32[]{:S(2)}, u32[]{:S(2)}) collective-permute-start(bf16[16,1024]{1,0:T(8,128)(2,1)S(1)} %bitcast.12), channel_id=1, source_target_pairs={{0,12},{4,8},{8,4},{12,0},{1,13},{5,9},{9,5},{13,1},{2,14},{6,10},... | collective-permute-start | bytes 98312 | tf_op jit(solution)/shard_map/ppermute | solution.py:216
  7.0 4.4 %collective-permute-start = (bf16[16,1024]{1,0:T(8,128)(2,1)S(1)}, bf16[16,1024]{1,0:T(8,128)(2,1)S(1)}, u32[]{:S(2)}, u32[]{:S(2)}) collective-permute-start(bf16[16,1024]{1,0:T(8,128)(2,1)S(1)} %bitcast.13), channel_id=1, source_target_pairs={{0,4},{4,0},{8,12},{12,8},{1,5},{5,1},{9,13},{13,9},{2,6},{6,2},{1... | collective-permute-start | bytes 98312 | tf_op jit(solution)/shard_map/ppermute | solution.py:216
  7.2 0.7 %copy-start.9 = (s32[1,2]{1,0:T(1,128)S(1)}, s32[1,2]{1,0:T(1,128)}, u32[]{:S(2)}) copy-start(s32[1,2]{1,0:T(1,128)} %ranks_ref.1) | copy-start | bytes 28
  7.2 0.7 %copy-start.4 = (f32[32]{0:T(128)S(1)}, f32[32]{0:T(128)}, u32[]{:S(2)}) copy-start(f32[32]{0:T(128)} %param.17) | copy-start | bytes 388
  7.2 0.7 %copy-start.5 = (f32[32]{0:T(128)S(1)}, f32[32]{0:T(128)}, u32[]{:S(2)}) copy-start(f32[32]{0:T(128)} %param.18) | copy-start | bytes 388
  7.2 0.7 %copy-start.6 = (f32[32]{0:T(128)S(1)}, f32[32]{0:T(128)}, u32[]{:S(2)}) copy-start(f32[32]{0:T(128)} %param.19) | copy-start | bytes 388
  7.9 3.4 %copy-start = (bf16[1,2,2,128,512]{4,3,2,1,0:T(8,128)(2,1)S(1)}, bf16[1,2,2,128,512]{4,3,2,1,0:T(8,128)(2,1)}, u32[]{:S(2)}) copy-start(bf16[1,2,2,128,512]{4,3,2,1,0:T(8,128)(2,1)} %u_bases.3) | copy-start | bytes 1572868
  7.9 3.4 %copy-start.1 = (bf16[1,2,2,128,512]{4,3,2,1,0:T(8,128)(2,1)S(1)}, bf16[1,2,2,128,512]{4,3,2,1,0:T(8,128)(2,1)}, u32[]{:S(2)}) copy-start(bf16[1,2,2,128,512]{4,3,2,1,0:T(8,128)(2,1)} %v_bases.3) | copy-start | bytes 1572868
  7.9 3.4 %copy-start.3 = (f32[8,2,512]{2,1,0:T(2,128)S(1)}, f32[8,2,512]{2,1,0:T(2,128)}, u32[]{:S(2)}) copy-start(f32[8,2,512]{2,1,0:T(2,128)} %u_ref.1) | copy-start | bytes 98308
  11.8 1.3 %collective-permute-start.3 = (bf16[64,512]{1,0:T(8,128)(2,1)S(1)}, bf16[64,512]{1,0:T(8,128)(2,1)S(1)}, u32[]{:S(2)}, u32[]{:S(2)}) collective-permute-start(bf16[64,512]{1,0:T(8,128)(2,1)S(1)} %get-tuple-element.30), channel_id=1, source_target_pairs={{0,1},{1,0},{2,3},{3,2},{4,5},{5,4},{6,7},{7,6},{8,9},{9,8},{10,11... | collective-permute-start | bytes 196616 | tf_op jit(solution)/shard_map/ppermute | solution.py:216
  13.2 4.1 %collective-permute-start.4 = (bf16[64,512]{1,0:T(8,128)(2,1)S(1)}, bf16[64,512]{1,0:T(8,128)(2,1)S(1)}, u32[]{:S(2)}, u32[]{:S(2)}) collective-permute-start(bf16[64,512]{1,0:T(8,128)(2,1)S(1)} %add_convert_fusion.sum_ref), channel_id=1, source_target_pairs={{0,3},{1,2},{2,1},{3,0},{4,7},{5,6},{6,5},{7,4},{8,11},{9,10},{10,... | collective-permute-start | bytes 196616 | tf_op jit(solution)/shard_map/ppermute | solution.py:216
  17.3 9.5 %copy-start.2 = (f32[8,2,1024]{2,1,0:T(2,128)S(1)}, f32[8,2,1024]{2,1,0:T(2,128)}, u32[]{:S(2)}) copy-start(f32[8,2,1024]{2,1,0:T(2,128)} %v_ref.1) | copy-start | bytes 196612
  17.7 7.2 %collective-permute-start.5 = (bf16[272,128]{1,0:T(8,128)(2,1)S(1)}, bf16[272,128]{1,0:T(8,128)(2,1)S(1)}, u32[]{:S(2)}, u32[]{:S(2)}) collective-permute-start(bf16[272,128]{1,0:T(8,128)(2,1)S(1)} %get-tuple-element.32), channel_id=1, source_target_pairs={{0,8},{4,12},{8,0},{12,4},{1,9},{5,13},{9,1},{13,5},{2,10},{6,14},... | collective-permute-start | bytes 208904 | tf_op jit(solution)/shard_map/ppermute | solution.py:216
  19.0 6.6 %collective-permute-start.6 = (bf16[272,128]{1,0:T(8,128)(2,1)S(1)}, bf16[272,128]{1,0:T(8,128)(2,1)S(1)}, u32[]{:S(2)}, u32[]{:S(2)}) collective-permute-start(bf16[272,128]{1,0:T(8,128)(2,1)S(1)} %get-tuple-element.33), channel_id=1, source_target_pairs={{0,12},{4,8},{8,4},{12,0},{1,13},{5,9},{9,5},{13,1},{2,14},{6,10},... | collective-permute-start | bytes 208904 | tf_op jit(solution)/shard_map/ppermute | solution.py:216
  20.1 6.7 %collective-permute-start.7 = (bf16[272,128]{1,0:T(8,128)(2,1)S(1)}, bf16[272,128]{1,0:T(8,128)(2,1)S(1)}, u32[]{:S(2)}, u32[]{:S(2)}) collective-permute-start(bf16[272,128]{1,0:T(8,128)(2,1)S(1)} %get-tuple-element.34), channel_id=1, source_target_pairs={{0,4},{4,0},{8,12},{12,8},{1,5},{5,1},{9,13},{13,9},{2,6},{6,2},{1... | collective-permute-start | bytes 208904 | tf_op jit(solution)/shard_map/ppermute | solution.py:216
  26.8 4.5 %copy-start.7 = (f32[8,2,1024]{2,1,0:T(2,128)S(1)}, f32[8,2,1024]{2,1,0:T(2,128)}, u32[]{:S(2)}) copy-start(f32[8,2,1024]{2,1,0:T(2,128)} %x_ref.1) | copy-start | bytes 196612
  26.8 4.5 %copy-start.8 = (f32[8,2,1024]{2,1,0:T(2,128)S(1)}, f32[8,2,1024]{2,1,0:T(2,128)}, u32[]{:S(2)}) copy-start(f32[8,2,1024]{2,1,0:T(2,128)} %w_ref.1) | copy-start | bytes 196612
  27.1 1.2 %collective-permute-start.8 = (f32[1,128]{1,0:T(1,128)S(1)}, f32[1,128]{1,0:T(1,128)S(1)}, u32[]{:S(2)}, u32[]{:S(2)}) collective-permute-start(f32[1,128]{1,0:T(1,128)S(1)} %get-tuple-element.35), channel_id=1, source_target_pairs={{0,1},{1,0},{2,3},{3,2},{4,5},{5,4},{6,7},{7,6},{8,9},{9,8},{10,11... | collective-permute-start | bytes 1544 | tf_op jit(solution)/shard_map/ppermute | solution.py:216
  28.2 3.0 %collective-permute-start.9 = (f32[1,128]{1,0:T(1,128)S(1)}, f32[1,128]{1,0:T(1,128)S(1)}, u32[]{:S(2)}, u32[]{:S(2)}) collective-permute-start(f32[1,128]{1,0:T(1,128)S(1)} %add.7.norms_ref), channel_id=1, source_target_pairs={{0,3},{1,2},{2,1},{3,0},{4,7},{5,6},{6,5},{7,4},{8,11},{9,10},{10,... | collective-permute-start | bytes 1544 | tf_op jit(solution)/shard_map/ppermute | solution.py:216
  29.5 3.9 %collective-permute-start.11 = (f32[1,128]{1,0:T(1,128)S(1)}, f32[1,128]{1,0:T(1,128)S(1)}, u32[]{:S(2)}, u32[]{:S(2)}) collective-permute-start(f32[1,128]{1,0:T(1,128)S(1)} %add.7.norms_ref), channel_id=1, source_target_pairs={{0,7},{1,6},{2,5},{3,4},{4,3},{5,2},{6,1},{7,0},{8,15},{9,14},{10,... | collective-permute-start | bytes 1544 | tf_op jit(solution)/shard_map/ppermute | solution.py:216
  30.1 3.3 %collective-permute-start.10 = (f32[1,128]{1,0:T(1,128)S(1)}, f32[1,128]{1,0:T(1,128)S(1)}, u32[]{:S(2)}, u32[]{:S(2)}) collective-permute-start(f32[1,128]{1,0:T(1,128)S(1)} %add.7.norms_ref), channel_id=1, source_target_pairs={{0,5},{1,4},{2,7},{3,6},{4,1},{5,0},{6,3},{7,2},{8,13},{9,12},{10,... | collective-permute-start | bytes 1544 | tf_op jit(solution)/shard_map/ppermute | solution.py:216

commit v6 on v5

--- a/solution.py
+++ b/solution.py
@@ -272,7 +272,7 @@
     mask = n_cplx
     while mask < n_cols:
         low = (low.astype(f32) + got[-1].astype(f32)).astype(bf16)
-        got.append(flip(low, ("col", "cplx"), mask + 1))
+        got.append(flip(low, ("col", "cplx"), mask))
         mask *= 2
     *outs, own = call(
         partial(adjoint_kernel, n_row, len(got), own_v, own_u, lanes),

time: 34.1 us -> 33.2 us (0.974)
  waiting for transfers between devices: 14.8 us -> 13.6 us
    ppermute x12, waiting for transfers between devices: 14.8 us -> 13.6 us  [flip(): lax.ppermute(x, axes, [(i, i ^ mask) for i in range(lax.axis_size(axes))])]
where the time goes in v6:
time: 33.2 us; the launch traced here: 33.1 us
  starting transfers between devices  13.9 us (42%)
  waiting for transfers between devices  13.6 us (41%)
  Pallas kernels  3.12 us (9%)
  other arithmetic  0.9 us (3%)
  local copies, waits for them, and re-layouts  0.73 us (2%)
  between operations  0.73 us (2%)
    ppermute x12, starting transfers between devices, flip(): lax.ppermute(x, axes, [(i, i ^ mask) for i in range(lax.axis_size(axes))])  13.9 us
    ppermute x12, waiting for transfers between devices, flip(): lax.ppermute(x, axes, [(i, i ^ mask) for i in range(lax.axis_size(axes))])  13.6 us
    pallas_call x6, Pallas kernels, call(): pl.pallas_call(kernel, out_shape=[jax.ShapeDtypeStruct(s, d) for s, d in...  3.12 us
    convert_element_type x1, other arithmetic, body(): v_low = jnp.swapaxes(v_unit, 0, 1).reshape(block, wide).astype(bf16)  0.87 us
    unnamed x20, local copies, waits for them, and re-layouts  0.72 us
  transfers between devices with their start and end apart: 12, of which 8 were waited for; matrix products, arithmetic and copies ran while one was open for 0% of the time, Pallas kernels for 4%

profile of v6, /device:TPU:0, one launch (start us, length us, event | category | flops | bytes accessed | tf_op | source)
XLA Modules:
  0.0 33.1 jit_solution(2156998248715129116)
XLA Ops:
  0.6 0.9 %convert_bitcast_fusion = bf16[2,8,1024]{2,0,1:T(2,128)(2,1)S(1)} fusion(f32[8,2,1024]{2,1,0:T(2,128)} %v_ref.1), kind=kLoop, calls=%fused_computation.2 | loop fusion | flops 16384 | bytes 98304 | tf_op jit(solution)/shard_map/convert_element_type | solution.py:257
  1.5 4.1 %collective-permute-start.2 = (bf16[16,1024]{1,0:T(8,128)(2,1)S(1)}, bf16[16,1024]{1,0:T(8,128)(2,1)S(1)}, u32[]{:S(2)}, u32[]{:S(2)}) collective-permute-start(bf16[16,1024]{1,0:T(8,128)(2,1)S(1)} %bitcast.11), channel_id=1, source_target_pairs={{0,8},{4,12},{8,0},{12,4},{1,9},{5,13},{9,1},{13,5},{2,10},{6,14},... | collective-permute-start | bytes 98312 | tf_op jit(solution)/shard_map/ppermute | solution.py:216
  5.6 1.3 %collective-permute-start.1 = (bf16[16,1024]{1,0:T(8,128)(2,1)S(1)}, bf16[16,1024]{1,0:T(8,128)(2,1)S(1)}, u32[]{:S(2)}, u32[]{:S(2)}) collective-permute-start(bf16[16,1024]{1,0:T(8,128)(2,1)S(1)} %bitcast.12), channel_id=1, source_target_pairs={{0,12},{4,8},{8,4},{12,0},{1,13},{5,9},{9,5},{13,1},{2,14},{6,10},... | collective-permute-start | bytes 98312 | tf_op jit(solution)/shard_map/ppermute | solution.py:216
  7.2 0.6 %copy-done.9 = s32[1,2]{1,0:T(1,128)S(1)} copy-done((s32[1,2]{1,0:T(1,128)S(1)}, s32[1,2]{1,0:T(1,128)}, u32[]{:S(2)}) %copy-start.9) | copy-done | bytes 32
  7.9 0.6 %shard_map.153 = (f32[2,128]{1,0:T(2,128)S(1)}, f32[3,32]{1,0:T(4,128)}) custom-call(s32[1,2]{1,0:T(1,128)S(1)} %copy-done.9, f32[1,32]{1,0:T(1,128)S(1)} %bitcast.15, f32[1,32]{1,0:T(1,128)S(1)} %bitcast.17, f32[1,32]{1,0:T(1,128)S(1)} %bitcast.19), custom_call_target="tpu_custom_call" | custom-call | flops 10000000000 | bytes 67108864 | tf_op jit(solution)/shard_map/pallas_call | solution.py:18
  8.5 2.8 %collective-permute-done.1.refs_2_ = bf16[16,1024]{1,0:T(8,128)(2,1)S(1)} collective-permute-done((bf16[16,1024]{1,0:T(8,128)(2,1)S(1)}, bf16[16,1024]{1,0:T(8,128)(2,1)S(1)}, u32[]{:S(2)}, u32[]{:S(2)}) %collective-permute-start.1) | collective-permute-done | bytes 32800 | tf_op jit(solution)/shard_map/ppermute | solution.py:216
  11.4 0.5 %shard_map.154 = (bf16[64,512]{1,0:T(8,128)(2,1)S(1)}, f32[16,512]{1,0:T(8,128)S(1)}, bf16[2,16,1024]{2,1,0:T(8,128)(2,1)S(1)}) custom-call(f32[2,128]{1,0:T(2,128)S(1)} %get-tuple-element.27.live_ref, bf16[1,2,2,128,512]{4,3,2,1,0:T(8,128)(2,1)S(1)} %copy-done, bf16[1,2,2,128,512]{4,3,2,1,0:T(8,128)(2,1)S(1)} %copy-done.1, f32[8,2,512]{2,1,0:T(2,128)S(1)} %copy-done.3, ...), custom_call_target="tpu_custom_call" | custom-call | tf_op jit(solution)/shard_map/pallas_call | solution.py:18
  11.9 1.2 %collective-permute-done.3.refs_0_ = bf16[64,512]{1,0:T(8,128)(2,1)S(1)} collective-permute-done((bf16[64,512]{1,0:T(8,128)(2,1)S(1)}, bf16[64,512]{1,0:T(8,128)(2,1)S(1)}, u32[]{:S(2)}, u32[]{:S(2)}) %collective-permute-start.3) | collective-permute-done | bytes 65568 | tf_op jit(solution)/shard_map/ppermute | solution.py:216
  13.2 1.6 %collective-permute-start.4 = (bf16[64,512]{1,0:T(8,128)(2,1)S(1)}, bf16[64,512]{1,0:T(8,128)(2,1)S(1)}, u32[]{:S(2)}, u32[]{:S(2)}) collective-permute-start(bf16[64,512]{1,0:T(8,128)(2,1)S(1)} %add_convert_fusion.sum_ref), channel_id=1, source_target_pairs={{0,2},{1,3},{2,0},{3,1},{4,6},{5,7},{6,4},{7,5},{8,10},{9,11},{10,... | collective-permute-start | bytes 196616 | tf_op jit(solution)/shard_map/ppermute | solution.py:216
  14.7 2.8 %collective-permute-done.4.refs_1_ = bf16[64,512]{1,0:T(8,128)(2,1)S(1)} collective-permute-done((bf16[64,512]{1,0:T(8,128)(2,1)S(1)}, bf16[64,512]{1,0:T(8,128)(2,1)S(1)}, u32[]{:S(2)}, u32[]{:S(2)}) %collective-permute-start.4) | collective-permute-done | bytes 65568 | tf_op jit(solution)/shard_map/ppermute | solution.py:216
  17.5 0.5 %shard_map.155 = (bf16[272,128]{1,0:T(8,128)(2,1)S(1)}, bf16[272,128]{1,0:T(8,128)(2,1)S(1)}, bf16[272,128]{1,0:T(8,128)(2,1)S(1)}, bf16[272,128]{1,0:T(8,128)(2,1)S(1)}, f32[16,512]{1,0:T(8,128)S(1)}) custom-call(f32[2,128]{1,0:T(2,128)S(1)} %get-tuple-element.27.live_ref, bf16[1,2,2,128,512]{4,3,2,1,0:T(8,128)(2,1)S(1)} %copy-done, ...), custom_call_target="tpu_custom_call" | custom-call | tf_op jit(solution)/shard_map/pallas_call | solution.py:18
  18.0 1.3 %collective-permute-start.5 = (bf16[272,128]{1,0:T(8,128)(2,1)S(1)}, bf16[272,128]{1,0:T(8,128)(2,1)S(1)}, u32[]{:S(2)}, u32[]{:S(2)}) collective-permute-start(bf16[272,128]{1,0:T(8,128)(2,1)S(1)} %get-tuple-element.32), channel_id=1, source_target_pairs={{0,8},{4,12},{8,0},{12,4},{1,9},{5,13},{9,1},{13,5},{2,10},{6,14},... | collective-permute-start | bytes 208904 | tf_op jit(solution)/shard_map/ppermute | solution.py:216
  19.3 1.0 %collective-permute-start.6 = (bf16[272,128]{1,0:T(8,128)(2,1)S(1)}, bf16[272,128]{1,0:T(8,128)(2,1)S(1)}, u32[]{:S(2)}, u32[]{:S(2)}) collective-permute-start(bf16[272,128]{1,0:T(8,128)(2,1)S(1)} %get-tuple-element.33), channel_id=1, source_target_pairs={{0,12},{4,8},{8,4},{12,0},{1,13},{5,9},{9,5},{13,1},{2,14},{6,10},... | collective-permute-start | bytes 208904 | tf_op jit(solution)/shard_map/ppermute | solution.py:216
  20.3 1.2 %collective-permute-start.7 = (bf16[272,128]{1,0:T(8,128)(2,1)S(1)}, bf16[272,128]{1,0:T(8,128)(2,1)S(1)}, u32[]{:S(2)}, u32[]{:S(2)}) collective-permute-start(bf16[272,128]{1,0:T(8,128)(2,1)S(1)} %get-tuple-element.34), channel_id=1, source_target_pairs={{0,4},{4,0},{8,12},{12,8},{1,5},{5,1},{9,13},{13,9},{2,6},{6,2},{1... | collective-permute-start | bytes 208904 | tf_op jit(solution)/shard_map/ppermute | solution.py:216
  21.5 2.9 %collective-permute-done.5.refs_1_ = bf16[272,128]{1,0:T(8,128)(2,1)S(1)} collective-permute-done((bf16[272,128]{1,0:T(8,128)(2,1)S(1)}, bf16[272,128]{1,0:T(8,128)(2,1)S(1)}, u32[]{:S(2)}, u32[]{:S(2)}) %collective-permute-start.5) | collective-permute-done | bytes 69664 | tf_op jit(solution)/shard_map/ppermute | solution.py:216
  24.4 1.1 %collective-permute-done.6.refs_2_ = bf16[272,128]{1,0:T(8,128)(2,1)S(1)} collective-permute-done((bf16[272,128]{1,0:T(8,128)(2,1)S(1)}, bf16[272,128]{1,0:T(8,128)(2,1)S(1)}, u32[]{:S(2)}, u32[]{:S(2)}) %collective-permute-start.6) | collective-permute-done | bytes 69664 | tf_op jit(solution)/shard_map/ppermute | solution.py:216
  25.5 0.4 %collective-permute-done.7.refs_3_ = bf16[272,128]{1,0:T(8,128)(2,1)S(1)} collective-permute-done((bf16[272,128]{1,0:T(8,128)(2,1)S(1)}, bf16[272,128]{1,0:T(8,128)(2,1)S(1)}, u32[]{:S(2)}, u32[]{:S(2)}) %collective-permute-start.7) | collective-permute-done | bytes 69664 | tf_op jit(solution)/shard_map/ppermute | solution.py:216
  26.2 1.1 %collective-permute-done.8 = f32[1,128]{1,0:T(1,128)S(1)} collective-permute-done((f32[1,128]{1,0:T(1,128)S(1)}, f32[1,128]{1,0:T(1,128)S(1)}, u32[]{:S(2)}, u32[]{:S(2)}) %collective-permute-start.8) | collective-permute-done | bytes 544 | tf_op jit(solution)/shard_map/ppermute | solution.py:216
  27.3 1.3 %collective-permute-start.9 = (f32[1,128]{1,0:T(1,128)S(1)}, f32[1,128]{1,0:T(1,128)S(1)}, u32[]{:S(2)}, u32[]{:S(2)}) collective-permute-start(f32[1,128]{1,0:T(1,128)S(1)} %add.7.norms_ref), channel_id=1, source_target_pairs={{0,3},{1,2},{2,1},{3,0},{4,7},{5,6},{6,5},{7,4},{8,11},{9,10},{10,... | collective-permute-start | bytes 1544 | tf_op jit(solution)/shard_map/ppermute | solution.py:216
  28.6 0.5 %collective-permute-start.11 = (f32[1,128]{1,0:T(1,128)S(1)}, f32[1,128]{1,0:T(1,128)S(1)}, u32[]{:S(2)}, u32[]{:S(2)}) collective-permute-start(f32[1,128]{1,0:T(1,128)S(1)} %add.7.norms_ref), channel_id=1, source_target_pairs={{0,7},{1,6},{2,5},{3,4},{4,3},{5,2},{6,1},{7,0},{8,15},{9,14},{10,... | collective-permute-start | bytes 1544 | tf_op jit(solution)/shard_map/ppermute | solution.py:216
  29.1 1.3 %collective-permute-start.10 = (f32[1,128]{1,0:T(1,128)S(1)}, f32[1,128]{1,0:T(1,128)S(1)}, u32[]{:S(2)}, u32[]{:S(2)}) collective-permute-start(f32[1,128]{1,0:T(1,128)S(1)} %add.7.norms_ref), channel_id=1, source_target_pairs={{0,5},{1,4},{2,7},{3,6},{4,1},{5,0},{6,3},{7,2},{8,13},{9,12},{10,... | collective-permute-start | bytes 1544 | tf_op jit(solution)/shard_map/ppermute | solution.py:216
  30.4 0.8 %shard_map.157 = (f32[8,2,1024]{2,1,0:T(2,128)}, f32[8,2,1024]{2,1,0:T(2,128)}, f32[8,2,512]{2,1,0:T(2,128)}, f32[8,2,1024]{2,1,0:T(2,128)}, f32[1,128]{1,0:T(1,128)S(1)}) custom-call(f32[1,128]{1,0:T(1,128)S(1)} %add.7.norms_ref, f32[1,128]{1,0:T(1,128)S(1)} %collective-permute-done.9.got_ref, f32[1,128]{1,0:T(1,128)S(1)} %get-tuple-element.36.beta_ref, ...), custom_call_target="tpu_custom_call" | custom-call | flops 1000000000 | bytes 8388608 | tf_op jit(solution)/shard_map/pallas_call | solution.py:18
  31.2 1.3 %collective-permute-done.11.refs_2_ = f32[1,128]{1,0:T(1,128)S(1)} collective-permute-done((f32[1,128]{1,0:T(1,128)S(1)}, f32[1,128]{1,0:T(1,128)S(1)}, u32[]{:S(2)}, u32[]{:S(2)}) %collective-permute-start.11) | collective-permute-done | bytes 544 | tf_op jit(solution)/shard_map/ppermute | solution.py:216
  32.5 0.5 %shard_map.158 = (f32[1,32]{1,0:T(1,128)}, f32[1,32]{1,0:T(1,128)}, f32[1,32]{1,0:T(1,128)}) custom-call(f32[1,128]{1,0:T(1,128)S(1)} %get-tuple-element.36.beta_ref, f32[3,32]{1,0:T(4,128)S(1)} %pad_maximum_fusion.alpha_ref.scalars_ref, f32[1,128]{1,0:T(1,128)S(1)} %get-tuple-element.43.refs_0_, f32[1,128]{1,0:T(1,128)S(1)} %collective-permute-done.10.refs_1_, ...), custom_call_target="tpu_custom_call" | custom-call | tf_op jit(solution)/shard_map/pallas_call | solution.py:18
  (31 shorter events, 0.8 us)
Async XLA Ops:
  1.5 7.0 %collective-permute-start.2 = (bf16[16,1024]{1,0:T(8,128)(2,1)S(1)}, bf16[16,1024]{1,0:T(8,128)(2,1)S(1)}, u32[]{:S(2)}, u32[]{:S(2)}) collective-permute-start(bf16[16,1024]{1,0:T(8,128)(2,1)S(1)} %bitcast.11), channel_id=1, source_target_pairs={{0,8},{4,12},{8,0},{12,4},{1,9},{5,13},{9,1},{13,5},{2,10},{6,14},... | collective-permute-start | bytes 98312 | tf_op jit(solution)/shard_map/ppermute | solution.py:216
  5.6 5.7 %collective-permute-start.1 = (bf16[16,1024]{1,0:T(8,128)(2,1)S(1)}, bf16[16,1024]{1,0:T(8,128)(2,1)S(1)}, u32[]{:S(2)}, u32[]{:S(2)}) collective-permute-start(bf16[16,1024]{1,0:T(8,128)(2,1)S(1)} %bitcast.12), channel_id=1, source_target_pairs={{0,12},{4,8},{8,4},{12,0},{1,13},{5,9},{9,5},{13,1},{2,14},{6,10},... | collective-permute-start | bytes 98312 | tf_op jit(solution)/shard_map/ppermute | solution.py:216
  7.0 4.4 %collective-permute-start = (bf16[16,1024]{1,0:T(8,128)(2,1)S(1)}, bf16[16,1024]{1,0:T(8,128)(2,1)S(1)}, u32[]{:S(2)}, u32[]{:S(2)}) collective-permute-start(bf16[16,1024]{1,0:T(8,128)(2,1)S(1)} %bitcast.13), channel_id=1, source_target_pairs={{0,4},{4,0},{8,12},{12,8},{1,5},{5,1},{9,13},{13,9},{2,6},{6,2},{1... | collective-permute-start | bytes 98312 | tf_op jit(solution)/shard_map/ppermute | solution.py:216
  7.2 0.7 %copy-start.9 = (s32[1,2]{1,0:T(1,128)S(1)}, s32[1,2]{1,0:T(1,128)}, u32[]{:S(2)}) copy-start(s32[1,2]{1,0:T(1,128)} %ranks_ref.1) | copy-start | bytes 28
  7.2 0.7 %copy-start.4 = (f32[32]{0:T(128)S(1)}, f32[32]{0:T(128)}, u32[]{:S(2)}) copy-start(f32[32]{0:T(128)} %param.17) | copy-start | bytes 388
  7.2 0.7 %copy-start.5 = (f32[32]{0:T(128)S(1)}, f32[32]{0:T(128)}, u32[]{:S(2)}) copy-start(f32[32]{0:T(128)} %param.18) | copy-start | bytes 388
  7.2 0.7 %copy-start.6 = (f32[32]{0:T(128)S(1)}, f32[32]{0:T(128)}, u32[]{:S(2)}) copy-start(f32[32]{0:T(128)} %param.19) | copy-start | bytes 388
  7.9 3.4 %copy-start = (bf16[1,2,2,128,512]{4,3,2,1,0:T(8,128)(2,1)S(1)}, bf16[1,2,2,128,512]{4,3,2,1,0:T(8,128)(2,1)}, u32[]{:S(2)}) copy-start(bf16[1,2,2,128,512]{4,3,2,1,0:T(8,128)(2,1)} %u_bases.3) | copy-start | bytes 1572868
  7.9 3.4 %copy-start.1 = (bf16[1,2,2,128,512]{4,3,2,1,0:T(8,128)(2,1)S(1)}, bf16[1,2,2,128,512]{4,3,2,1,0:T(8,128)(2,1)}, u32[]{:S(2)}) copy-start(bf16[1,2,2,128,512]{4,3,2,1,0:T(8,128)(2,1)} %v_bases.3) | copy-start | bytes 1572868
  7.9 3.4 %copy-start.3 = (f32[8,2,512]{2,1,0:T(2,128)S(1)}, f32[8,2,512]{2,1,0:T(2,128)}, u32[]{:S(2)}) copy-start(f32[8,2,512]{2,1,0:T(2,128)} %u_ref.1) | copy-start | bytes 98308
  11.8 1.3 %collective-permute-start.3 = (bf16[64,512]{1,0:T(8,128)(2,1)S(1)}, bf16[64,512]{1,0:T(8,128)(2,1)S(1)}, u32[]{:S(2)}, u32[]{:S(2)}) collective-permute-start(bf16[64,512]{1,0:T(8,128)(2,1)S(1)} %get-tuple-element.30), channel_id=1, source_target_pairs={{0,1},{1,0},{2,3},{3,2},{4,5},{5,4},{6,7},{7,6},{8,9},{9,8},{10,11... | collective-permute-start | bytes 196616 | tf_op jit(solution)/shard_map/ppermute | solution.py:216
  13.2 4.3 %collective-permute-start.4 = (bf16[64,512]{1,0:T(8,128)(2,1)S(1)}, bf16[64,512]{1,0:T(8,128)(2,1)S(1)}, u32[]{:S(2)}, u32[]{:S(2)}) collective-permute-start(bf16[64,512]{1,0:T(8,128)(2,1)S(1)} %add_convert_fusion.sum_ref), channel_id=1, source_target_pairs={{0,2},{1,3},{2,0},{3,1},{4,6},{5,7},{6,4},{7,5},{8,10},{9,11},{10,... | collective-permute-start | bytes 196616 | tf_op jit(solution)/shard_map/ppermute | solution.py:216
  17.5 8.4 %copy-start.2 = (f32[8,2,1024]{2,1,0:T(2,128)S(1)}, f32[8,2,1024]{2,1,0:T(2,128)}, u32[]{:S(2)}) copy-start(f32[8,2,1024]{2,1,0:T(2,128)} %v_ref.1) | copy-start | bytes 196612
  18.0 6.5 %collective-permute-start.5 = (bf16[272,128]{1,0:T(8,128)(2,1)S(1)}, bf16[272,128]{1,0:T(8,128)(2,1)S(1)}, u32[]{:S(2)}, u32[]{:S(2)}) collective-permute-start(bf16[272,128]{1,0:T(8,128)(2,1)S(1)} %get-tuple-element.32), channel_id=1, source_target_pairs={{0,8},{4,12},{8,0},{12,4},{1,9},{5,13},{9,1},{13,5},{2,10},{6,14},... | collective-permute-start | bytes 208904 | tf_op jit(solution)/shard_map/ppermute | solution.py:216
  19.3 6.3 %collective-permute-start.6 = (bf16[272,128]{1,0:T(8,128)(2,1)S(1)}, bf16[272,128]{1,0:T(8,128)(2,1)S(1)}, u32[]{:S(2)}, u32[]{:S(2)}) collective-permute-start(bf16[272,128]{1,0:T(8,128)(2,1)S(1)} %get-tuple-element.33), channel_id=1, source_target_pairs={{0,12},{4,8},{8,4},{12,0},{1,13},{5,9},{9,5},{13,1},{2,14},{6,10},... | collective-permute-start | bytes 208904 | tf_op jit(solution)/shard_map/ppermute | solution.py:216
  20.3 5.6 %collective-permute-start.7 = (bf16[272,128]{1,0:T(8,128)(2,1)S(1)}, bf16[272,128]{1,0:T(8,128)(2,1)S(1)}, u32[]{:S(2)}, u32[]{:S(2)}) collective-permute-start(bf16[272,128]{1,0:T(8,128)(2,1)S(1)} %get-tuple-element.34), channel_id=1, source_target_pairs={{0,4},{4,0},{8,12},{12,8},{1,5},{5,1},{9,13},{13,9},{2,6},{6,2},{1... | collective-permute-start | bytes 208904 | tf_op jit(solution)/shard_map/ppermute | solution.py:216
  25.9 4.5 %copy-start.7 = (f32[8,2,1024]{2,1,0:T(2,128)S(1)}, f32[8,2,1024]{2,1,0:T(2,128)}, u32[]{:S(2)}) copy-start(f32[8,2,1024]{2,1,0:T(2,128)} %x_ref.1) | copy-start | bytes 196612
  25.9 4.5 %copy-start.8 = (f32[8,2,1024]{2,1,0:T(2,128)S(1)}, f32[8,2,1024]{2,1,0:T(2,128)}, u32[]{:S(2)}) copy-start(f32[8,2,1024]{2,1,0:T(2,128)} %w_ref.1) | copy-start | bytes 196612
  26.2 1.2 %collective-permute-start.8 = (f32[1,128]{1,0:T(1,128)S(1)}, f32[1,128]{1,0:T(1,128)S(1)}, u32[]{:S(2)}, u32[]{:S(2)}) collective-permute-start(f32[1,128]{1,0:T(1,128)S(1)} %get-tuple-element.35), channel_id=1, source_target_pairs={{0,1},{1,0},{2,3},{3,2},{4,5},{5,4},{6,7},{7,6},{8,9},{9,8},{10,11... | collective-permute-start | bytes 1544 | tf_op jit(solution)/shard_map/ppermute | solution.py:216
  27.3 3.0 %collective-permute-start.9 = (f32[1,128]{1,0:T(1,128)S(1)}, f32[1,128]{1,0:T(1,128)S(1)}, u32[]{:S(2)}, u32[]{:S(2)}) collective-permute-start(f32[1,128]{1,0:T(1,128)S(1)} %add.7.norms_ref), channel_id=1, source_target_pairs={{0,3},{1,2},{2,1},{3,0},{4,7},{5,6},{6,5},{7,4},{8,11},{9,10},{10,... | collective-permute-start | bytes 1544 | tf_op jit(solution)/shard_map/ppermute | solution.py:216
  28.6 3.9 %collective-permute-start.11 = (f32[1,128]{1,0:T(1,128)S(1)}, f32[1,128]{1,0:T(1,128)S(1)}, u32[]{:S(2)}, u32[]{:S(2)}) collective-permute-start(f32[1,128]{1,0:T(1,128)S(1)} %add.7.norms_ref), channel_id=1, source_target_pairs={{0,7},{1,6},{2,5},{3,4},{4,3},{5,2},{6,1},{7,0},{8,15},{9,14},{10,... | collective-permute-start | bytes 1544 | tf_op jit(solution)/shard_map/ppermute | solution.py:216
  29.1 3.4 %collective-permute-start.10 = (f32[1,128]{1,0:T(1,128)S(1)}, f32[1,128]{1,0:T(1,128)S(1)}, u32[]{:S(2)}, u32[]{:S(2)}) collective-permute-start(f32[1,128]{1,0:T(1,128)S(1)} %add.7.norms_ref), channel_id=1, source_target_pairs={{0,5},{1,4},{2,7},{3,6},{4,1},{5,0},{6,3},{7,2},{8,13},{9,12},{10,... | collective-permute-start | bytes 1544 | tf_op jit(solution)/shard_map/ppermute | solution.py:216

commit v7 on v6

--- a/solution.py
+++ b/solution.py
@@ -141,27 +141,29 @@
     beta2 = pairs([b[end : end + 1, :].astype(f32) + b[end + 1 : end + 2, :].astype(f32) for b in blocks])
     beta = jnp.sqrt(beta2 / (2 * rows_total) + epsilon)
     beta_ref[...] = beta
-    norms = jnp.zeros((1, lanes), f32)
-    for h, row in enumerate((p, p ^ (n_row // 2))):
-        beta_here = to_column(beta, row * own_v, own_v)
-        beta_here = jnp.concatenate([beta_here, beta_here], 0)
-        scale = rows_total / cols_total / shrink / beta_here
-        squares = jnp.zeros((own_v, lanes), f32)
+    rows = (p, p ^ (n_row // 2))
+    first = jnp.where(iota((4 * own_v, 1), 0) < 2 * own_v, rows[0], rows[1]) * own_v + iota((4 * own_v, 1), 0) % own_v
+    here = iota((4 * own_v, lanes), 1) == first
+    betas = jnp.sum(jnp.where(here, beta, 0.0), axis=1, keepdims=True)
+    scales = rows_total / cols_total / shrink / betas
+    squares = []
+    for h in range(2):
+        both = slice(h * 2 * own_v, (h + 1) * 2 * own_v)
+        beta_here, scale = betas[both], scales[both]
+        total = jnp.zeros((2 * own_v, lanes), f32)
         for t in range(strips):
             at = (h * strips + t) * 2 * own_v
             back = scale * pairs([b[at : at + 2 * own_v, :].astype(f32) for b in blocks])
             strip = slice(t * lanes, (t + 1) * lanes)
-            low = beta_here * kept_ref[h, :, strip].astype(f32)
-            for i in range(2):
-                half = slice(i * own_v, (i + 1) * own_v)
-                if h == 0:
+            if h == 0:
+                for i in range(2):
+                    half = slice(i * own_v, (i + 1) * own_v)
                     res_ref[half, strip] = back[half] - beta_here[half] * v_ref[:, i, strip]
-                res = back[half] - low[half]
-                squares = squares + res * res
-        squares = jnp.sum(squares, axis=1, keepdims=True)
-        place = iota((own_v, 1), 0) + row * own_v
-        norms = norms + to_lanes(squares, place, lanes)
-    norm_ref[...] = norms
+            res = back - beta_here * kept_ref[h, :, strip].astype(f32)
+            total = total + res * res
+        squares.append(total)
+    squares = jnp.sum(jnp.concatenate(squares, 0), axis=1, keepdims=True)
+    norm_ref[...] = jnp.sum(jnp.where(here, squares, 0.0), axis=0, keepdims=True)
 
 
 def turn(beta, scalars_ref):
@@ -206,10 +208,6 @@
     alpha_out[...] = alpha
     rhobar_out[...] = -cosine * alpha
     phibar_out[...] = sine * phibar
-
-
-def third_of(x):
-    return x
 
 
 def flip(x, axes, mask):
@@ -253,7 +251,6 @@
     )
     first = [1, *range(n_row - 1, 1, -1)]
     second = [*range(2, n_row), 1]
-    scalars = jnp.stack([alpha_prev, rhobar_prev, phibar_prev])
     v_low = jnp.swapaxes(v_unit, 0, 1).reshape(block, wide).astype(bf16)
     blocks = [v_low] + [flip(v_low, "row", k) for k in first]
     low, own, kept = call(
@@ -314,7 +311,7 @@
         cost=pl.CostEstimate(flops=10**9, bytes_accessed=2**23, transcendentals=0),
     )
     alpha, rhobar, phibar = call(
-        partial(scalars_kernel, cols_total), [((1, rhs), f32)] * 3, beta, scalars, norms, *third_of(got[1:])
+        partial(scalars_kernel, cols_total), [((1, rhs), f32)] * 3, beta, scalars, norms, *got[1:]
     )
     return (x_next, w_next, u_next, v_next, alpha[0], rhobar[0], phibar[0])
 

time: 33.2 us -> 33.1 us (level)
  waiting for transfers between devices: 13.6 us -> 14.2 us
  Pallas kernels: 3.12 us -> 2.54 us
    pallas_call x6, Pallas kernels: 3.12 us -> 2.54 us  [call(): pl.pallas_call(kernel, out_shape=[jax.ShapeDtypeStruct(s, d) for s, d in...]
    ppermute x12, waiting for transfers between devices: 13.6 us -> 14.2 us  [flip(): lax.ppermute(x, axes, [(i, i ^ mask) for i in range(lax.axis_size(axes))])]
  transfers between devices with their start and end apart: 12 -> 12, of which waited for: 8 -> 8; matrix products, arithmetic and copies ran while one was open for 0% -> 0% of each run, Pallas kernels for 4% -> 3%
where the time goes in v7:
time: 33.1 us; the launch traced here: 33 us
  waiting for transfers between devices  14.2 us (43%)
  starting transfers between devices  13.9 us (42%)
  Pallas kernels  2.54 us (8%)
  other arithmetic  0.89 us (3%)
  local copies, waits for them, and re-layouts  0.73 us (2%)
  between operations  0.72 us (2%)
    ppermute x12, waiting for transfers between devices, flip(): lax.ppermute(x, axes, [(i, i ^ mask) for i in range(lax.axis_size(axes))])  14.2 us
    ppermute x12, starting transfers between devices, flip(): lax.ppermute(x, axes, [(i, i ^ mask) for i in range(lax.axis_size(axes))])  13.9 us
    pallas_call x6, Pallas kernels, call(): pl.pallas_call(kernel, out_shape=[jax.ShapeDtypeStruct(s, d) for s, d in...  2.54 us
    convert_element_type x1, other arithmetic, body(): v_low = jnp.swapaxes(v_unit, 0, 1).reshape(block, wide).astype(bf16)  0.87 us
    unnamed x20, local copies, waits for them, and re-layouts  0.72 us
  transfers between devices with their start and end apart: 12, of which 8 were waited for; matrix products, arithmetic and copies ran while one was open for 0% of the time, Pallas kernels for 3%

profile of v7, /device:TPU:0, one launch (start us, length us, event | category | flops | bytes accessed | tf_op | source)
XLA Modules:
  0.0 33.0 jit_solution(17997112731466731263)
XLA Ops:
  0.6 0.9 %convert_bitcast_fusion = bf16[2,8,1024]{2,0,1:T(2,128)(2,1)S(1)} fusion(f32[8,2,1024]{2,1,0:T(2,128)} %v_ref.1), kind=kLoop, calls=%fused_computation.2 | loop fusion | flops 16384 | bytes 98304 | tf_op jit(solution)/shard_map/convert_element_type | solution.py:254
  1.5 4.1 %collective-permute-start.2 = (bf16[16,1024]{1,0:T(8,128)(2,1)S(1)}, bf16[16,1024]{1,0:T(8,128)(2,1)S(1)}, u32[]{:S(2)}, u32[]{:S(2)}) collective-permute-start(bf16[16,1024]{1,0:T(8,128)(2,1)S(1)} %bitcast.11), channel_id=1, source_target_pairs={{0,8},{4,12},{8,0},{12,4},{1,9},{5,13},{9,1},{13,5},{2,10},{6,14},... | collective-permute-start | bytes 98312 | tf_op jit(solution)/shard_map/ppermute | solution.py:214
  5.6 1.3 %collective-permute-start.1 = (bf16[16,1024]{1,0:T(8,128)(2,1)S(1)}, bf16[16,1024]{1,0:T(8,128)(2,1)S(1)}, u32[]{:S(2)}, u32[]{:S(2)}) collective-permute-start(bf16[16,1024]{1,0:T(8,128)(2,1)S(1)} %bitcast.12), channel_id=1, source_target_pairs={{0,12},{4,8},{8,4},{12,0},{1,13},{5,9},{9,5},{13,1},{2,14},{6,10},... | collective-permute-start | bytes 98312 | tf_op jit(solution)/shard_map/ppermute | solution.py:214
  7.0 0.2 collective-permute-start
  7.2 0.6 %copy-done.9 = f32[32]{0:T(128)S(1)} copy-done((f32[32]{0:T(128)S(1)}, f32[32]{0:T(128)}, u32[]{:S(2)}) %copy-start.9) | copy-done | bytes 152
  8.0 3.3 %collective-permute-done.1.refs_2_ = bf16[16,1024]{1,0:T(8,128)(2,1)S(1)} collective-permute-done((bf16[16,1024]{1,0:T(8,128)(2,1)S(1)}, bf16[16,1024]{1,0:T(8,128)(2,1)S(1)}, u32[]{:S(2)}, u32[]{:S(2)}) %collective-permute-start.1) | collective-permute-done | bytes 32800 | tf_op jit(solution)/shard_map/ppermute | solution.py:214
  11.4 0.5 %shard_map.154 = (bf16[64,512]{1,0:T(8,128)(2,1)S(1)}, f32[16,512]{1,0:T(8,128)S(1)}, bf16[2,16,1024]{2,1,0:T(8,128)(2,1)S(1)}) custom-call(f32[2,128]{1,0:T(2,128)S(1)} %get-tuple-element.28.live_ref, bf16[1,2,2,128,512]{4,3,2,1,0:T(8,128)(2,1)S(1)} %copy-done, bf16[1,2,2,128,512]{4,3,2,1,0:T(8,128)(2,1)S(1)} %copy-done.1, f32[8,2,512]{2,1,0:T(2,128)S(1)} %copy-done.3, ...), custom_call_target="tpu_custom_call" | custom-call | tf_op jit(solution)/shard_map/pallas_call | solution.py:18
  11.9 1.2 %collective-permute-done.3.refs_0_ = bf16[64,512]{1,0:T(8,128)(2,1)S(1)} collective-permute-done((bf16[64,512]{1,0:T(8,128)(2,1)S(1)}, bf16[64,512]{1,0:T(8,128)(2,1)S(1)}, u32[]{:S(2)}, u32[]{:S(2)}) %collective-permute-start.3) | collective-permute-done | bytes 65568 | tf_op jit(solution)/shard_map/ppermute | solution.py:214
  13.2 1.6 %collective-permute-start.4 = (bf16[64,512]{1,0:T(8,128)(2,1)S(1)}, bf16[64,512]{1,0:T(8,128)(2,1)S(1)}, u32[]{:S(2)}, u32[]{:S(2)}) collective-permute-start(bf16[64,512]{1,0:T(8,128)(2,1)S(1)} %add_convert_fusion.sum_ref), channel_id=1, source_target_pairs={{0,2},{1,3},{2,0},{3,1},{4,6},{5,7},{6,4},{7,5},{8,10},{9,11},{10,... | collective-permute-start | bytes 196616 | tf_op jit(solution)/shard_map/ppermute | solution.py:214
  14.7 2.8 %collective-permute-done.4.refs_1_ = bf16[64,512]{1,0:T(8,128)(2,1)S(1)} collective-permute-done((bf16[64,512]{1,0:T(8,128)(2,1)S(1)}, bf16[64,512]{1,0:T(8,128)(2,1)S(1)}, u32[]{:S(2)}, u32[]{:S(2)}) %collective-permute-start.4) | collective-permute-done | bytes 65568 | tf_op jit(solution)/shard_map/ppermute | solution.py:214
  17.5 0.5 %shard_map.155 = (bf16[272,128]{1,0:T(8,128)(2,1)S(1)}, bf16[272,128]{1,0:T(8,128)(2,1)S(1)}, bf16[272,128]{1,0:T(8,128)(2,1)S(1)}, bf16[272,128]{1,0:T(8,128)(2,1)S(1)}, f32[16,512]{1,0:T(8,128)S(1)}) custom-call(f32[2,128]{1,0:T(2,128)S(1)} %get-tuple-element.28.live_ref, bf16[1,2,2,128,512]{4,3,2,1,0:T(8,128)(2,1)S(1)} %copy-done, ...), custom_call_target="tpu_custom_call" | custom-call | tf_op jit(solution)/shard_map/pallas_call | solution.py:18
  18.0 1.3 %collective-permute-start.5 = (bf16[272,128]{1,0:T(8,128)(2,1)S(1)}, bf16[272,128]{1,0:T(8,128)(2,1)S(1)}, u32[]{:S(2)}, u32[]{:S(2)}) collective-permute-start(bf16[272,128]{1,0:T(8,128)(2,1)S(1)} %get-tuple-element.34), channel_id=1, source_target_pairs={{0,8},{4,12},{8,0},{12,4},{1,9},{5,13},{9,1},{13,5},{2,10},{6,14},... | collective-permute-start | bytes 208904 | tf_op jit(solution)/shard_map/ppermute | solution.py:214
  19.3 1.0 %collective-permute-start.6 = (bf16[272,128]{1,0:T(8,128)(2,1)S(1)}, bf16[272,128]{1,0:T(8,128)(2,1)S(1)}, u32[]{:S(2)}, u32[]{:S(2)}) collective-permute-start(bf16[272,128]{1,0:T(8,128)(2,1)S(1)} %get-tuple-element.35), channel_id=1, source_target_pairs={{0,12},{4,8},{8,4},{12,0},{1,13},{5,9},{9,5},{13,1},{2,14},{6,10},... | collective-permute-start | bytes 208904 | tf_op jit(solution)/shard_map/ppermute | solution.py:214
  20.3 1.2 %collective-permute-start.7 = (bf16[272,128]{1,0:T(8,128)(2,1)S(1)}, bf16[272,128]{1,0:T(8,128)(2,1)S(1)}, u32[]{:S(2)}, u32[]{:S(2)}) collective-permute-start(bf16[272,128]{1,0:T(8,128)(2,1)S(1)} %get-tuple-element.36), channel_id=1, source_target_pairs={{0,4},{4,0},{8,12},{12,8},{1,5},{5,1},{9,13},{13,9},{2,6},{6,2},{1... | collective-permute-start | bytes 208904 | tf_op jit(solution)/shard_map/ppermute | solution.py:214
  21.5 2.9 %collective-permute-done.5.refs_1_ = bf16[272,128]{1,0:T(8,128)(2,1)S(1)} collective-permute-done((bf16[272,128]{1,0:T(8,128)(2,1)S(1)}, bf16[272,128]{1,0:T(8,128)(2,1)S(1)}, u32[]{:S(2)}, u32[]{:S(2)}) %collective-permute-start.5) | collective-permute-done | bytes 69664 | tf_op jit(solution)/shard_map/ppermute | solution.py:214
  24.4 1.1 %collective-permute-done.6.refs_2_ = bf16[272,128]{1,0:T(8,128)(2,1)S(1)} collective-permute-done((bf16[272,128]{1,0:T(8,128)(2,1)S(1)}, bf16[272,128]{1,0:T(8,128)(2,1)S(1)}, u32[]{:S(2)}, u32[]{:S(2)}) %collective-permute-start.6) | collective-permute-done | bytes 69664 | tf_op jit(solution)/shard_map/ppermute | solution.py:214
  25.5 0.4 %collective-permute-done.7.refs_3_ = bf16[272,128]{1,0:T(8,128)(2,1)S(1)} collective-permute-done((bf16[272,128]{1,0:T(8,128)(2,1)S(1)}, bf16[272,128]{1,0:T(8,128)(2,1)S(1)}, u32[]{:S(2)}, u32[]{:S(2)}) %collective-permute-start.7) | collective-permute-done | bytes 69664 | tf_op jit(solution)/shard_map/ppermute | solution.py:214
  26.2 1.1 %collective-permute-done.8 = f32[1,128]{1,0:T(1,128)S(1)} collective-permute-done((f32[1,128]{1,0:T(1,128)S(1)}, f32[1,128]{1,0:T(1,128)S(1)}, u32[]{:S(2)}, u32[]{:S(2)}) %collective-permute-start.8) | collective-permute-done | bytes 544 | tf_op jit(solution)/shard_map/ppermute | solution.py:214
  27.3 1.3 %collective-permute-start.9 = (f32[1,128]{1,0:T(1,128)S(1)}, f32[1,128]{1,0:T(1,128)S(1)}, u32[]{:S(2)}, u32[]{:S(2)}) collective-permute-start(f32[1,128]{1,0:T(1,128)S(1)} %add.7.norms_ref), channel_id=1, source_target_pairs={{0,3},{1,2},{2,1},{3,0},{4,7},{5,6},{6,5},{7,4},{8,11},{9,10},{10,... | collective-permute-start | bytes 1544 | tf_op jit(solution)/shard_map/ppermute | solution.py:214
  28.6 0.5 %collective-permute-start.11 = (f32[1,128]{1,0:T(1,128)S(1)}, f32[1,128]{1,0:T(1,128)S(1)}, u32[]{:S(2)}, u32[]{:S(2)}) collective-permute-start(f32[1,128]{1,0:T(1,128)S(1)} %add.7.norms_ref), channel_id=1, source_target_pairs={{0,7},{1,6},{2,5},{3,4},{4,3},{5,2},{6,1},{7,0},{8,15},{9,14},{10,... | collective-permute-start | bytes 1544 | tf_op jit(solution)/shard_map/ppermute | solution.py:214
  29.0 1.3 %collective-permute-start.10 = (f32[1,128]{1,0:T(1,128)S(1)}, f32[1,128]{1,0:T(1,128)S(1)}, u32[]{:S(2)}, u32[]{:S(2)}) collective-permute-start(f32[1,128]{1,0:T(1,128)S(1)} %add.7.norms_ref), channel_id=1, source_target_pairs={{0,5},{1,4},{2,7},{3,6},{4,1},{5,0},{6,3},{7,2},{8,13},{9,12},{10,... | collective-permute-start | bytes 1544 | tf_op jit(solution)/shard_map/ppermute | solution.py:214
  30.3 0.8 %shard_map.157 = (f32[8,2,1024]{2,1,0:T(2,128)}, f32[8,2,1024]{2,1,0:T(2,128)}, f32[8,2,512]{2,1,0:T(2,128)}, f32[8,2,1024]{2,1,0:T(2,128)}, f32[1,128]{1,0:T(1,128)S(1)}) custom-call(f32[1,128]{1,0:T(1,128)S(1)} %add.7.norms_ref, f32[1,128]{1,0:T(1,128)S(1)} %collective-permute-done.9.got_ref, f32[1,128]{1,0:T(1,128)S(1)} %get-tuple-element.38.beta_ref, ...), custom_call_target="tpu_custom_call" | custom-call | flops 1000000000 | bytes 8388608 | tf_op jit(solution)/shard_map/pallas_call | solution.py:18
  31.1 1.3 %collective-permute-done.11.refs_2_ = f32[1,128]{1,0:T(1,128)S(1)} collective-permute-done((f32[1,128]{1,0:T(1,128)S(1)}, f32[1,128]{1,0:T(1,128)S(1)}, u32[]{:S(2)}, u32[]{:S(2)}) %collective-permute-start.11) | collective-permute-done | bytes 544 | tf_op jit(solution)/shard_map/ppermute | solution.py:214
  32.4 0.5 %shard_map.158 = (f32[1,32]{1,0:T(1,128)}, f32[1,32]{1,0:T(1,128)}, f32[1,32]{1,0:T(1,128)}) custom-call(f32[1,128]{1,0:T(1,128)S(1)} %get-tuple-element.38.beta_ref, f32[3,32]{1,0:T(4,128)S(1)} %get-tuple-element.29.alpha_ref.scalars_ref, f32[1,128]{1,0:T(1,128)S(1)} %get-tuple-element.45.refs_0_, f32[1,128]{1,0:T(1,128)S(1)} %collective-permute-done.10.refs_1_, ...), custom_call_target="tpu_custom_call" | custom-call | tf_op jit(solution)/shard_map/pallas_call | solution.py:18
  (30 shorter events, 0.5 us)
Async XLA Ops:
  1.5 6.5 %collective-permute-start.2 = (bf16[16,1024]{1,0:T(8,128)(2,1)S(1)}, bf16[16,1024]{1,0:T(8,128)(2,1)S(1)}, u32[]{:S(2)}, u32[]{:S(2)}) collective-permute-start(bf16[16,1024]{1,0:T(8,128)(2,1)S(1)} %bitcast.11), channel_id=1, source_target_pairs={{0,8},{4,12},{8,0},{12,4},{1,9},{5,13},{9,1},{13,5},{2,10},{6,14},... | collective-permute-start | bytes 98312 | tf_op jit(solution)/shard_map/ppermute | solution.py:214
  5.6 5.7 %collective-permute-start.1 = (bf16[16,1024]{1,0:T(8,128)(2,1)S(1)}, bf16[16,1024]{1,0:T(8,128)(2,1)S(1)}, u32[]{:S(2)}, u32[]{:S(2)}) collective-permute-start(bf16[16,1024]{1,0:T(8,128)(2,1)S(1)} %bitcast.12), channel_id=1, source_target_pairs={{0,12},{4,8},{8,4},{12,0},{1,13},{5,9},{9,5},{13,1},{2,14},{6,10},... | collective-permute-start | bytes 98312 | tf_op jit(solution)/shard_map/ppermute | solution.py:214
  7.0 4.4 %collective-permute-start = (bf16[16,1024]{1,0:T(8,128)(2,1)S(1)}, bf16[16,1024]{1,0:T(8,128)(2,1)S(1)}, u32[]{:S(2)}, u32[]{:S(2)}) collective-permute-start(bf16[16,1024]{1,0:T(8,128)(2,1)S(1)} %bitcast.13), channel_id=1, source_target_pairs={{0,4},{4,0},{8,12},{12,8},{1,5},{5,1},{9,13},{13,9},{2,6},{6,2},{1... | collective-permute-start | bytes 98312 | tf_op jit(solution)/shard_map/ppermute | solution.py:214
  7.2 0.7 %copy-start.9 = (f32[32]{0:T(128)S(1)}, f32[32]{0:T(128)}, u32[]{:S(2)}) copy-start(f32[32]{0:T(128)} %param.19) | copy-start | bytes 388
  7.2 0.7 %copy-start.6 = (s32[1,2]{1,0:T(1,128)S(1)}, s32[1,2]{1,0:T(1,128)}, u32[]{:S(2)}) copy-start(s32[1,2]{1,0:T(1,128)} %ranks_ref.1) | copy-start | bytes 28
  7.2 0.7 %copy-start.7 = (f32[32]{0:T(128)S(1)}, f32[32]{0:T(128)}, u32[]{:S(2)}) copy-start(f32[32]{0:T(128)} %param.17) | copy-start | bytes 388
  7.2 0.7 %copy-start.8 = (f32[32]{0:T(128)S(1)}, f32[32]{0:T(128)}, u32[]{:S(2)}) copy-start(f32[32]{0:T(128)} %param.18) | copy-start | bytes 388
  7.9 3.4 %copy-start = (bf16[1,2,2,128,512]{4,3,2,1,0:T(8,128)(2,1)S(1)}, bf16[1,2,2,128,512]{4,3,2,1,0:T(8,128)(2,1)}, u32[]{:S(2)}) copy-start(bf16[1,2,2,128,512]{4,3,2,1,0:T(8,128)(2,1)} %u_bases.3) | copy-start | bytes 1572868
  7.9 3.4 %copy-start.1 = (bf16[1,2,2,128,512]{4,3,2,1,0:T(8,128)(2,1)S(1)}, bf16[1,2,2,128,512]{4,3,2,1,0:T(8,128)(2,1)}, u32[]{:S(2)}) copy-start(bf16[1,2,2,128,512]{4,3,2,1,0:T(8,128)(2,1)} %v_bases.3) | copy-start | bytes 1572868
  7.9 3.4 %copy-start.3 = (f32[8,2,512]{2,1,0:T(2,128)S(1)}, f32[8,2,512]{2,1,0:T(2,128)}, u32[]{:S(2)}) copy-start(f32[8,2,512]{2,1,0:T(2,128)} %u_ref.1) | copy-start | bytes 98308
  11.8 1.3 %collective-permute-start.3 = (bf16[64,512]{1,0:T(8,128)(2,1)S(1)}, bf16[64,512]{1,0:T(8,128)(2,1)S(1)}, u32[]{:S(2)}, u32[]{:S(2)}) collective-permute-start(bf16[64,512]{1,0:T(8,128)(2,1)S(1)} %get-tuple-element.32), channel_id=1, source_target_pairs={{0,1},{1,0},{2,3},{3,2},{4,5},{5,4},{6,7},{7,6},{8,9},{9,8},{10,11... | collective-permute-start | bytes 196616 | tf_op jit(solution)/shard_map/ppermute | solution.py:214
  13.2 4.3 %collective-permute-start.4 = (bf16[64,512]{1,0:T(8,128)(2,1)S(1)}, bf16[64,512]{1,0:T(8,128)(2,1)S(1)}, u32[]{:S(2)}, u32[]{:S(2)}) collective-permute-start(bf16[64,512]{1,0:T(8,128)(2,1)S(1)} %add_convert_fusion.sum_ref), channel_id=1, source_target_pairs={{0,2},{1,3},{2,0},{3,1},{4,6},{5,7},{6,4},{7,5},{8,10},{9,11},{10,... | collective-permute-start | bytes 196616 | tf_op jit(solution)/shard_map/ppermute | solution.py:214
  17.5 8.4 %copy-start.2 = (f32[8,2,1024]{2,1,0:T(2,128)S(1)}, f32[8,2,1024]{2,1,0:T(2,128)}, u32[]{:S(2)}) copy-start(f32[8,2,1024]{2,1,0:T(2,128)} %v_ref.1) | copy-start | bytes 196612
  18.0 6.5 %collective-permute-start.5 = (bf16[272,128]{1,0:T(8,128)(2,1)S(1)}, bf16[272,128]{1,0:T(8,128)(2,1)S(1)}, u32[]{:S(2)}, u32[]{:S(2)}) collective-permute-start(bf16[272,128]{1,0:T(8,128)(2,1)S(1)} %get-tuple-element.34), channel_id=1, source_target_pairs={{0,8},{4,12},{8,0},{12,4},{1,9},{5,13},{9,1},{13,5},{2,10},{6,14},... | collective-permute-start | bytes 208904 | tf_op jit(solution)/shard_map/ppermute | solution.py:214
  19.3 6.3 %collective-permute-start.6 = (bf16[272,128]{1,0:T(8,128)(2,1)S(1)}, bf16[272,128]{1,0:T(8,128)(2,1)S(1)}, u32[]{:S(2)}, u32[]{:S(2)}) collective-permute-start(bf16[272,128]{1,0:T(8,128)(2,1)S(1)} %get-tuple-element.35), channel_id=1, source_target_pairs={{0,12},{4,8},{8,4},{12,0},{1,13},{5,9},{9,5},{13,1},{2,14},{6,10},... | collective-permute-start | bytes 208904 | tf_op jit(solution)/shard_map/ppermute | solution.py:214
  20.3 5.6 %collective-permute-start.7 = (bf16[272,128]{1,0:T(8,128)(2,1)S(1)}, bf16[272,128]{1,0:T(8,128)(2,1)S(1)}, u32[]{:S(2)}, u32[]{:S(2)}) collective-permute-start(bf16[272,128]{1,0:T(8,128)(2,1)S(1)} %get-tuple-element.36), channel_id=1, source_target_pairs={{0,4},{4,0},{8,12},{12,8},{1,5},{5,1},{9,13},{13,9},{2,6},{6,2},{1... | collective-permute-start | bytes 208904 | tf_op jit(solution)/shard_map/ppermute | solution.py:214
  25.9 4.4 %copy-start.4 = (f32[8,2,1024]{2,1,0:T(2,128)S(1)}, f32[8,2,1024]{2,1,0:T(2,128)}, u32[]{:S(2)}) copy-start(f32[8,2,1024]{2,1,0:T(2,128)} %x_ref.1) | copy-start | bytes 196612
  25.9 4.4 %copy-start.5 = (f32[8,2,1024]{2,1,0:T(2,128)S(1)}, f32[8,2,1024]{2,1,0:T(2,128)}, u32[]{:S(2)}) copy-start(f32[8,2,1024]{2,1,0:T(2,128)} %w_ref.1) | copy-start | bytes 196612
  26.1 1.2 %collective-permute-start.8 = (f32[1,128]{1,0:T(1,128)S(1)}, f32[1,128]{1,0:T(1,128)S(1)}, u32[]{:S(2)}, u32[]{:S(2)}) collective-permute-start(f32[1,128]{1,0:T(1,128)S(1)} %get-tuple-element.37), channel_id=1, source_target_pairs={{0,1},{1,0},{2,3},{3,2},{4,5},{5,4},{6,7},{7,6},{8,9},{9,8},{10,11... | collective-permute-start | bytes 1544 | tf_op jit(solution)/shard_map/ppermute | solution.py:214
  27.3 3.0 %collective-permute-start.9 = (f32[1,128]{1,0:T(1,128)S(1)}, f32[1,128]{1,0:T(1,128)S(1)}, u32[]{:S(2)}, u32[]{:S(2)}) collective-permute-start(f32[1,128]{1,0:T(1,128)S(1)} %add.7.norms_ref), channel_id=1, source_target_pairs={{0,3},{1,2},{2,1},{3,0},{4,7},{5,6},{6,5},{7,4},{8,11},{9,10},{10,... | collective-permute-start | bytes 1544 | tf_op jit(solution)/shard_map/ppermute | solution.py:214
  28.6 3.9 %collective-permute-start.11 = (f32[1,128]{1,0:T(1,128)S(1)}, f32[1,128]{1,0:T(1,128)S(1)}, u32[]{:S(2)}, u32[]{:S(2)}) collective-permute-start(f32[1,128]{1,0:T(1,128)S(1)} %add.7.norms_ref), channel_id=1, source_target_pairs={{0,7},{1,6},{2,5},{3,4},{4,3},{5,2},{6,1},{7,0},{8,15},{9,14},{10,... | collective-permute-start | bytes 1544 | tf_op jit(solution)/shard_map/ppermute | solution.py:214
  29.0 3.4 %collective-permute-start.10 = (f32[1,128]{1,0:T(1,128)S(1)}, f32[1,128]{1,0:T(1,128)S(1)}, u32[]{:S(2)}, u32[]{:S(2)}) collective-permute-start(f32[1,128]{1,0:T(1,128)S(1)} %add.7.norms_ref), channel_id=1, source_target_pairs={{0,5},{1,4},{2,7},{3,6},{4,1},{5,0},{6,3},{7,2},{8,13},{9,12},{10,... | collective-permute-start | bytes 1544 | tf_op jit(solution)/shard_map/ppermute | solution.py:214

commit v8 on v7

--- a/solution.py
+++ b/solution.py
@@ -47,9 +47,12 @@
 
 
 def through(inner, outer, live_ref, x, own):
-    tiles, _, ranks, size = inner.shape[1:]
+    tiles, _, ranks, size = outer.shape[1:]
     mids = []
-    gs = [dot(x(q), inner[0, q].reshape(2 * ranks, size), True) for q in range(tiles)]
+    if len(inner.shape) == 3:
+        gs = [dot(x(q), inner[q], False) for q in range(tiles)]
+    else:
+        gs = [dot(x(q), inner[0, q].reshape(2 * ranks, size), True) for q in range(tiles)]
     for q, g in enumerate(gs):
         rows = g.shape[0]
         g = g.reshape(rows // (2 * own), 2, own, 2 * ranks)
@@ -76,7 +79,7 @@
 def forward_kernel(n_row, order, own_v, own_u, live_ref, u_bases, v_bases, u_ref, alpha_ref, *refs):
     blocks, (low_ref, own_ref, kept_ref, total) = in_order(refs[:n_row], order), refs[n_row:]
     p, c = lax.axis_index("row"), lax.axis_index(("col", "cplx"))
-    size = v_bases.shape[4]
+    size = u_bases.shape[4]
     x = jnp.concatenate([b[...] for b in blocks], 0)
     kept_ref[0] = blocks[0][...]
     kept_ref[1] = blocks[n_row // 2][...]
@@ -94,7 +97,7 @@
     low_ref[...] = total[...].astype(bf16)
 
 
-def adjoint_kernel(n_row, n_got, own_v, own_u, lanes, live_ref, u_bases, v_bases, own_ref, sum_ref, *refs):
+def adjoint_kernel(n_row, n_got, own_v, own_u, lanes, live_ref, u_turned, v_bases, own_ref, sum_ref, *refs):
     got, outs, own_out = refs[:n_got], refs[n_got : n_got + n_row], refs[n_got + n_row]
     p, c = lax.axis_index("row"), lax.axis_index(("col", "cplx"))
     many = own_u // own_v
@@ -115,7 +118,7 @@
     low = (beta2 - high.astype(f32)).astype(bf16)
     tail = jnp.where(iota((16, lanes), 0) == 0, high.astype(f32), low.astype(f32)).astype(bf16)
     x = (res * shrink).astype(bf16)
-    parts = through(u_bases, v_bases, live_ref, lambda q: x, own_v)
+    parts = through(u_turned, v_bases, live_ref, lambda q: x, own_v)
     wide = jnp.concatenate(parts, 1).astype(bf16)
     strips = wide.shape[1] // lanes
     for k, out in enumerate(outs):
@@ -253,6 +256,8 @@
     second = [*range(2, n_row), 1]
     v_low = jnp.swapaxes(v_unit, 0, 1).reshape(block, wide).astype(bf16)
     blocks = [v_low] + [flip(v_low, "row", k) for k in first]
+    tiles, _, ranks, size = u_bases.shape[1:]
+    u_turned = jnp.swapaxes(u_bases.reshape(tiles, 2 * ranks, size), 1, 2)
     low, own, kept = call(
         partial(forward_kernel, n_row, first, own_v, own_u),
         [((2 * rhs, tile_size), bf16), ((2 * own_u, tile_size), f32), ((2, block, wide), bf16)],
@@ -275,7 +280,7 @@
         partial(adjoint_kernel, n_row, len(got), own_v, own_u, lanes),
         [((2 * block * (wide // lanes) + 16, lanes), bf16)] * n_row + [((2 * own_u, tile_size), f32)],
         live,
-        u_bases,
+        u_turned,
         v_bases,
         own,
         low,

time: 33.1 us -> 33.1 us (level)
  transfers between devices with their start and end apart: 12 -> 12, of which waited for: 8 -> 8; matrix products, arithmetic and copies ran while one was open for 0% -> 1% of each run, Pallas kernels for 3% -> 3%
where the time goes in v8:
time: 33.1 us; the launch traced here: 32.9 us
  waiting for transfers between devices  14 us (42%)
  starting transfers between devices  13.9 us (42%)
  Pallas kernels  2.46 us (7%)
  local copies, waits for them, and re-layouts  0.93 us (3%)
  other arithmetic  0.89 us (3%)
  between operations  0.72 us (2%)
    ppermute x12, waiting for transfers between devices, flip(): lax.ppermute(x, axes, [(i, i ^ mask) for i in range(lax.axis_size(axes))])  14 us
    ppermute x12, starting transfers between devices, flip(): lax.ppermute(x, axes, [(i, i ^ mask) for i in range(lax.axis_size(axes))])  13.9 us
    pallas_call x6, Pallas kernels, call(): pl.pallas_call(kernel, out_shape=[jax.ShapeDtypeStruct(s, d) for s, d in...  2.46 us
    convert_element_type x1, other arithmetic, body(): v_low = jnp.swapaxes(v_unit, 0, 1).reshape(block, wide).astype(bf16)  0.87 us
    unnamed x20, local copies, waits for them, and re-layouts  0.72 us
  transfers between devices with their start and end apart: 12, of which 8 were waited for; matrix products, arithmetic and copies ran while one was open for 1% of the time, Pallas kernels for 3%

profile of v8, /device:TPU:0, one launch (start us, length us, event | category | flops | bytes accessed | tf_op | source)
XLA Modules:
  0.0 32.9 jit_solution(3509231828272294121)
XLA Ops:
  0.6 0.9 %convert_bitcast_fusion = bf16[2,8,1024]{2,0,1:T(2,128)(2,1)S(1)} fusion(f32[8,2,1024]{2,1,0:T(2,128)} %v_ref.1), kind=kLoop, calls=%fused_computation.2 | loop fusion | flops 16384 | bytes 98304 | tf_op jit(solution)/shard_map/convert_element_type | solution.py:257
  1.5 4.1 %collective-permute-start.2 = (bf16[16,1024]{1,0:T(8,128)(2,1)S(1)}, bf16[16,1024]{1,0:T(8,128)(2,1)S(1)}, u32[]{:S(2)}, u32[]{:S(2)}) collective-permute-start(bf16[16,1024]{1,0:T(8,128)(2,1)S(1)} %bitcast.15), channel_id=1, source_target_pairs={{0,8},{4,12},{8,0},{12,4},{1,9},{5,13},{9,1},{13,5},{2,10},{6,14},... | collective-permute-start | bytes 98312 | tf_op jit(solution)/shard_map/ppermute | solution.py:217
  5.6 1.3 %collective-permute-start.1 = (bf16[16,1024]{1,0:T(8,128)(2,1)S(1)}, bf16[16,1024]{1,0:T(8,128)(2,1)S(1)}, u32[]{:S(2)}, u32[]{:S(2)}) collective-permute-start(bf16[16,1024]{1,0:T(8,128)(2,1)S(1)} %bitcast.16), channel_id=1, source_target_pairs={{0,12},{4,8},{8,4},{12,0},{1,13},{5,9},{9,5},{13,1},{2,14},{6,10},... | collective-permute-start | bytes 98312 | tf_op jit(solution)/shard_map/ppermute | solution.py:217
  7.0 0.2 collective-permute-start
  7.2 0.6 %copy-done.9 = f32[32]{0:T(128)S(1)} copy-done((f32[32]{0:T(128)S(1)}, f32[32]{0:T(128)}, u32[]{:S(2)}) %copy-start.9) | copy-done | bytes 152
  8.0 3.3 %collective-permute-done.1.refs_2_ = bf16[16,1024]{1,0:T(8,128)(2,1)S(1)} collective-permute-done((bf16[16,1024]{1,0:T(8,128)(2,1)S(1)}, bf16[16,1024]{1,0:T(8,128)(2,1)S(1)}, u32[]{:S(2)}, u32[]{:S(2)}) %collective-permute-start.1) | collective-permute-done | bytes 32800 | tf_op jit(solution)/shard_map/ppermute | solution.py:217
  11.4 0.5 %shard_map.154 = (bf16[64,512]{1,0:T(8,128)(2,1)S(1)}, f32[16,512]{1,0:T(8,128)S(1)}, bf16[2,16,1024]{2,1,0:T(8,128)(2,1)S(1)}) custom-call(f32[2,128]{1,0:T(2,128)S(1)} %get-tuple-element.28.live_ref, bf16[1,2,2,128,512]{4,3,2,1,0:T(8,128)(2,1)S(1)} %copy-done, bf16[1,2,2,128,512]{4,3,2,1,0:T(8,128)(2,1)S(1)} %copy-done.1, f32[8,2,512]{2,1,0:T(2,128)S(1)} %copy-done.3, ...), custom_call_target="tpu_custom_call" | custom-call | tf_op jit(solution)/shard_map/pallas_call | solution.py:18
  11.9 1.2 %collective-permute-done.3.refs_0_ = bf16[64,512]{1,0:T(8,128)(2,1)S(1)} collective-permute-done((bf16[64,512]{1,0:T(8,128)(2,1)S(1)}, bf16[64,512]{1,0:T(8,128)(2,1)S(1)}, u32[]{:S(2)}, u32[]{:S(2)}) %collective-permute-start.3) | collective-permute-done | bytes 65568 | tf_op jit(solution)/shard_map/ppermute | solution.py:217
  13.2 1.6 %collective-permute-start.4 = (bf16[64,512]{1,0:T(8,128)(2,1)S(1)}, bf16[64,512]{1,0:T(8,128)(2,1)S(1)}, u32[]{:S(2)}, u32[]{:S(2)}) collective-permute-start(bf16[64,512]{1,0:T(8,128)(2,1)S(1)} %add_convert_fusion.sum_ref), channel_id=1, source_target_pairs={{0,2},{1,3},{2,0},{3,1},{4,6},{5,7},{6,4},{7,5},{8,10},{9,11},{10,... | collective-permute-start | bytes 196616 | tf_op jit(solution)/shard_map/ppermute | solution.py:217
  14.9 2.6 %collective-permute-done.4.refs_1_ = bf16[64,512]{1,0:T(8,128)(2,1)S(1)} collective-permute-done((bf16[64,512]{1,0:T(8,128)(2,1)S(1)}, bf16[64,512]{1,0:T(8,128)(2,1)S(1)}, u32[]{:S(2)}, u32[]{:S(2)}) %collective-permute-start.4) | collective-permute-done | bytes 65568 | tf_op jit(solution)/shard_map/ppermute | solution.py:217
  17.5 0.4 %shard_map.155 = (bf16[272,128]{1,0:T(8,128)(2,1)S(1)}, bf16[272,128]{1,0:T(8,128)(2,1)S(1)}, bf16[272,128]{1,0:T(8,128)(2,1)S(1)}, bf16[272,128]{1,0:T(8,128)(2,1)S(1)}, f32[16,512]{1,0:T(8,128)S(1)}) custom-call(f32[2,128]{1,0:T(2,128)S(1)} %get-tuple-element.28.live_ref, bf16[2,512,256]{2,1,0:T(8,128)(2,1)S(1)} %bitcast.14, ...), custom_call_target="tpu_custom_call" | custom-call | tf_op jit(solution)/shard_map/pallas_call | solution.py:18
  17.9 1.3 %collective-permute-start.5 = (bf16[272,128]{1,0:T(8,128)(2,1)S(1)}, bf16[272,128]{1,0:T(8,128)(2,1)S(1)}, u32[]{:S(2)}, u32[]{:S(2)}) collective-permute-start(bf16[272,128]{1,0:T(8,128)(2,1)S(1)} %get-tuple-element.34), channel_id=1, source_target_pairs={{0,8},{4,12},{8,0},{12,4},{1,9},{5,13},{9,1},{13,5},{2,10},{6,14},... | collective-permute-start | bytes 208904 | tf_op jit(solution)/shard_map/ppermute | solution.py:217
  19.2 1.0 %collective-permute-start.6 = (bf16[272,128]{1,0:T(8,128)(2,1)S(1)}, bf16[272,128]{1,0:T(8,128)(2,1)S(1)}, u32[]{:S(2)}, u32[]{:S(2)}) collective-permute-start(bf16[272,128]{1,0:T(8,128)(2,1)S(1)} %get-tuple-element.35), channel_id=1, source_target_pairs={{0,12},{4,8},{8,4},{12,0},{1,13},{5,9},{9,5},{13,1},{2,14},{6,10},... | collective-permute-start | bytes 208904 | tf_op jit(solution)/shard_map/ppermute | solution.py:217
  20.2 1.2 %collective-permute-start.7 = (bf16[272,128]{1,0:T(8,128)(2,1)S(1)}, bf16[272,128]{1,0:T(8,128)(2,1)S(1)}, u32[]{:S(2)}, u32[]{:S(2)}) collective-permute-start(bf16[272,128]{1,0:T(8,128)(2,1)S(1)} %get-tuple-element.36), channel_id=1, source_target_pairs={{0,4},{4,0},{8,12},{12,8},{1,5},{5,1},{9,13},{13,9},{2,6},{6,2},{1... | collective-permute-start | bytes 208904 | tf_op jit(solution)/shard_map/ppermute | solution.py:217
  21.4 2.9 %collective-permute-done.5.refs_1_ = bf16[272,128]{1,0:T(8,128)(2,1)S(1)} collective-permute-done((bf16[272,128]{1,0:T(8,128)(2,1)S(1)}, bf16[272,128]{1,0:T(8,128)(2,1)S(1)}, u32[]{:S(2)}, u32[]{:S(2)}) %collective-permute-start.5) | collective-permute-done | bytes 69664 | tf_op jit(solution)/shard_map/ppermute | solution.py:217
  24.4 1.1 %collective-permute-done.6.refs_2_ = bf16[272,128]{1,0:T(8,128)(2,1)S(1)} collective-permute-done((bf16[272,128]{1,0:T(8,128)(2,1)S(1)}, bf16[272,128]{1,0:T(8,128)(2,1)S(1)}, u32[]{:S(2)}, u32[]{:S(2)}) %collective-permute-start.6) | collective-permute-done | bytes 69664 | tf_op jit(solution)/shard_map/ppermute | solution.py:217
  25.4 0.4 %collective-permute-done.7.refs_3_ = bf16[272,128]{1,0:T(8,128)(2,1)S(1)} collective-permute-done((bf16[272,128]{1,0:T(8,128)(2,1)S(1)}, bf16[272,128]{1,0:T(8,128)(2,1)S(1)}, u32[]{:S(2)}, u32[]{:S(2)}) %collective-permute-start.7) | collective-permute-done | bytes 69664 | tf_op jit(solution)/shard_map/ppermute | solution.py:217
  26.1 1.1 %collective-permute-done.8 = f32[1,128]{1,0:T(1,128)S(1)} collective-permute-done((f32[1,128]{1,0:T(1,128)S(1)}, f32[1,128]{1,0:T(1,128)S(1)}, u32[]{:S(2)}, u32[]{:S(2)}) %collective-permute-start.8) | collective-permute-done | bytes 544 | tf_op jit(solution)/shard_map/ppermute | solution.py:217
  27.2 1.3 %collective-permute-start.9 = (f32[1,128]{1,0:T(1,128)S(1)}, f32[1,128]{1,0:T(1,128)S(1)}, u32[]{:S(2)}, u32[]{:S(2)}) collective-permute-start(f32[1,128]{1,0:T(1,128)S(1)} %add.7.norms_ref), channel_id=1, source_target_pairs={{0,3},{1,2},{2,1},{3,0},{4,7},{5,6},{6,5},{7,4},{8,11},{9,10},{10,... | collective-permute-start | bytes 1544 | tf_op jit(solution)/shard_map/ppermute | solution.py:217
  28.5 0.5 %collective-permute-start.11 = (f32[1,128]{1,0:T(1,128)S(1)}, f32[1,128]{1,0:T(1,128)S(1)}, u32[]{:S(2)}, u32[]{:S(2)}) collective-permute-start(f32[1,128]{1,0:T(1,128)S(1)} %add.7.norms_ref), channel_id=1, source_target_pairs={{0,7},{1,6},{2,5},{3,4},{4,3},{5,2},{6,1},{7,0},{8,15},{9,14},{10,... | collective-permute-start | bytes 1544 | tf_op jit(solution)/shard_map/ppermute | solution.py:217
  29.0 1.3 %collective-permute-start.10 = (f32[1,128]{1,0:T(1,128)S(1)}, f32[1,128]{1,0:T(1,128)S(1)}, u32[]{:S(2)}, u32[]{:S(2)}) collective-permute-start(f32[1,128]{1,0:T(1,128)S(1)} %add.7.norms_ref), channel_id=1, source_target_pairs={{0,5},{1,4},{2,7},{3,6},{4,1},{5,0},{6,3},{7,2},{8,13},{9,12},{10,... | collective-permute-start | bytes 1544 | tf_op jit(solution)/shard_map/ppermute | solution.py:217
  30.2 0.8 %shard_map.157 = (f32[8,2,1024]{2,1,0:T(2,128)}, f32[8,2,1024]{2,1,0:T(2,128)}, f32[8,2,512]{2,1,0:T(2,128)}, f32[8,2,1024]{2,1,0:T(2,128)}, f32[1,128]{1,0:T(1,128)S(1)}) custom-call(f32[1,128]{1,0:T(1,128)S(1)} %add.7.norms_ref, f32[1,128]{1,0:T(1,128)S(1)} %collective-permute-done.9.got_ref, f32[1,128]{1,0:T(1,128)S(1)} %get-tuple-element.38.beta_ref, ...), custom_call_target="tpu_custom_call" | custom-call | flops 1000000000 | bytes 8388608 | tf_op jit(solution)/shard_map/pallas_call | solution.py:18
  31.0 1.3 %collective-permute-done.11.refs_2_ = f32[1,128]{1,0:T(1,128)S(1)} collective-permute-done((f32[1,128]{1,0:T(1,128)S(1)}, f32[1,128]{1,0:T(1,128)S(1)}, u32[]{:S(2)}, u32[]{:S(2)}) %collective-permute-start.11) | collective-permute-done | bytes 544 | tf_op jit(solution)/shard_map/ppermute | solution.py:217
  32.4 0.5 %shard_map.158 = (f32[1,32]{1,0:T(1,128)}, f32[1,32]{1,0:T(1,128)}, f32[1,32]{1,0:T(1,128)}) custom-call(f32[1,128]{1,0:T(1,128)S(1)} %get-tuple-element.38.beta_ref, f32[3,32]{1,0:T(4,128)S(1)} %get-tuple-element.29.alpha_ref.scalars_ref, f32[1,128]{1,0:T(1,128)S(1)} %get-tuple-element.45.refs_0_, f32[1,128]{1,0:T(1,128)S(1)} %collective-permute-done.10.refs_1_, ...), custom_call_target="tpu_custom_call" | custom-call | tf_op jit(solution)/shard_map/pallas_call | solution.py:18
  (31 shorter events, 0.7 us)
Async XLA Ops:
  1.5 6.5 %collective-permute-start.2 = (bf16[16,1024]{1,0:T(8,128)(2,1)S(1)}, bf16[16,1024]{1,0:T(8,128)(2,1)S(1)}, u32[]{:S(2)}, u32[]{:S(2)}) collective-permute-start(bf16[16,1024]{1,0:T(8,128)(2,1)S(1)} %bitcast.15), channel_id=1, source_target_pairs={{0,8},{4,12},{8,0},{12,4},{1,9},{5,13},{9,1},{13,5},{2,10},{6,14},... | collective-permute-start | bytes 98312 | tf_op jit(solution)/shard_map/ppermute | solution.py:217
  5.6 5.7 %collective-permute-start.1 = (bf16[16,1024]{1,0:T(8,128)(2,1)S(1)}, bf16[16,1024]{1,0:T(8,128)(2,1)S(1)}, u32[]{:S(2)}, u32[]{:S(2)}) collective-permute-start(bf16[16,1024]{1,0:T(8,128)(2,1)S(1)} %bitcast.16), channel_id=1, source_target_pairs={{0,12},{4,8},{8,4},{12,0},{1,13},{5,9},{9,5},{13,1},{2,14},{6,10},... | collective-permute-start | bytes 98312 | tf_op jit(solution)/shard_map/ppermute | solution.py:217
  7.0 4.4 %collective-permute-start = (bf16[16,1024]{1,0:T(8,128)(2,1)S(1)}, bf16[16,1024]{1,0:T(8,128)(2,1)S(1)}, u32[]{:S(2)}, u32[]{:S(2)}) collective-permute-start(bf16[16,1024]{1,0:T(8,128)(2,1)S(1)} %bitcast.17), channel_id=1, source_target_pairs={{0,4},{4,0},{8,12},{12,8},{1,5},{5,1},{9,13},{13,9},{2,6},{6,2},{1... | collective-permute-start | bytes 98312 | tf_op jit(solution)/shard_map/ppermute | solution.py:217
  7.2 0.7 %copy-start.9 = (f32[32]{0:T(128)S(1)}, f32[32]{0:T(128)}, u32[]{:S(2)}) copy-start(f32[32]{0:T(128)} %param.19) | copy-start | bytes 388
  7.2 0.7 %copy-start.6 = (s32[1,2]{1,0:T(1,128)S(1)}, s32[1,2]{1,0:T(1,128)}, u32[]{:S(2)}) copy-start(s32[1,2]{1,0:T(1,128)} %ranks_ref.1) | copy-start | bytes 28
  7.2 0.7 %copy-start.7 = (f32[32]{0:T(128)S(1)}, f32[32]{0:T(128)}, u32[]{:S(2)}) copy-start(f32[32]{0:T(128)} %param.17) | copy-start | bytes 388
  7.2 0.7 %copy-start.8 = (f32[32]{0:T(128)S(1)}, f32[32]{0:T(128)}, u32[]{:S(2)}) copy-start(f32[32]{0:T(128)} %param.18) | copy-start | bytes 388
  7.9 3.4 %copy-start = (bf16[1,2,2,128,512]{4,3,2,1,0:T(8,128)(2,1)S(1)}, bf16[1,2,2,128,512]{4,3,2,1,0:T(8,128)(2,1)}, u32[]{:S(2)}) copy-start(bf16[1,2,2,128,512]{4,3,2,1,0:T(8,128)(2,1)} %u_bases.1) | copy-start | bytes 1572868
  7.9 3.4 %copy-start.1 = (bf16[1,2,2,128,512]{4,3,2,1,0:T(8,128)(2,1)S(1)}, bf16[1,2,2,128,512]{4,3,2,1,0:T(8,128)(2,1)}, u32[]{:S(2)}) copy-start(bf16[1,2,2,128,512]{4,3,2,1,0:T(8,128)(2,1)} %v_bases.3) | copy-start | bytes 1572868
  7.9 3.4 %copy-start.3 = (f32[8,2,512]{2,1,0:T(2,128)S(1)}, f32[8,2,512]{2,1,0:T(2,128)}, u32[]{:S(2)}) copy-start(f32[8,2,512]{2,1,0:T(2,128)} %u_ref.1) | copy-start | bytes 98308
  11.8 1.3 %collective-permute-start.3 = (bf16[64,512]{1,0:T(8,128)(2,1)S(1)}, bf16[64,512]{1,0:T(8,128)(2,1)S(1)}, u32[]{:S(2)}, u32[]{:S(2)}) collective-permute-start(bf16[64,512]{1,0:T(8,128)(2,1)S(1)} %get-tuple-element.32), channel_id=1, source_target_pairs={{0,1},{1,0},{2,3},{3,2},{4,5},{5,4},{6,7},{7,6},{8,9},{9,8},{10,11... | collective-permute-start | bytes 196616 | tf_op jit(solution)/shard_map/ppermute | solution.py:217
  13.2 4.3 %collective-permute-start.4 = (bf16[64,512]{1,0:T(8,128)(2,1)S(1)}, bf16[64,512]{1,0:T(8,128)(2,1)S(1)}, u32[]{:S(2)}, u32[]{:S(2)}) collective-permute-start(bf16[64,512]{1,0:T(8,128)(2,1)S(1)} %add_convert_fusion.sum_ref), channel_id=1, source_target_pairs={{0,2},{1,3},{2,0},{3,1},{4,6},{5,7},{6,4},{7,5},{8,10},{9,11},{10,... | collective-permute-start | bytes 196616 | tf_op jit(solution)/shard_map/ppermute | solution.py:217
  17.5 8.3 %copy-start.2 = (f32[8,2,1024]{2,1,0:T(2,128)S(1)}, f32[8,2,1024]{2,1,0:T(2,128)}, u32[]{:S(2)}) copy-start(f32[8,2,1024]{2,1,0:T(2,128)} %v_ref.1) | copy-start | bytes 196612
  17.9 6.5 %collective-permute-start.5 = (bf16[272,128]{1,0:T(8,128)(2,1)S(1)}, bf16[272,128]{1,0:T(8,128)(2,1)S(1)}, u32[]{:S(2)}, u32[]{:S(2)}) collective-permute-start(bf16[272,128]{1,0:T(8,128)(2,1)S(1)} %get-tuple-element.34), channel_id=1, source_target_pairs={{0,8},{4,12},{8,0},{12,4},{1,9},{5,13},{9,1},{13,5},{2,10},{6,14},... | collective-permute-start | bytes 208904 | tf_op jit(solution)/shard_map/ppermute | solution.py:217
  19.2 6.3 %collective-permute-start.6 = (bf16[272,128]{1,0:T(8,128)(2,1)S(1)}, bf16[272,128]{1,0:T(8,128)(2,1)S(1)}, u32[]{:S(2)}, u32[]{:S(2)}) collective-permute-start(bf16[272,128]{1,0:T(8,128)(2,1)S(1)} %get-tuple-element.35), channel_id=1, source_target_pairs={{0,12},{4,8},{8,4},{12,0},{1,13},{5,9},{9,5},{13,1},{2,14},{6,10},... | collective-permute-start | bytes 208904 | tf_op jit(solution)/shard_map/ppermute | solution.py:217
  20.2 5.6 %collective-permute-start.7 = (bf16[272,128]{1,0:T(8,128)(2,1)S(1)}, bf16[272,128]{1,0:T(8,128)(2,1)S(1)}, u32[]{:S(2)}, u32[]{:S(2)}) collective-permute-start(bf16[272,128]{1,0:T(8,128)(2,1)S(1)} %get-tuple-element.36), channel_id=1, source_target_pairs={{0,4},{4,0},{8,12},{12,8},{1,5},{5,1},{9,13},{13,9},{2,6},{6,2},{1... | collective-permute-start | bytes 208904 | tf_op jit(solution)/shard_map/ppermute | solution.py:217
  25.8 4.4 %copy-start.4 = (f32[8,2,1024]{2,1,0:T(2,128)S(1)}, f32[8,2,1024]{2,1,0:T(2,128)}, u32[]{:S(2)}) copy-start(f32[8,2,1024]{2,1,0:T(2,128)} %x_ref.1) | copy-start | bytes 196612
  25.8 4.4 %copy-start.5 = (f32[8,2,1024]{2,1,0:T(2,128)S(1)}, f32[8,2,1024]{2,1,0:T(2,128)}, u32[]{:S(2)}) copy-start(f32[8,2,1024]{2,1,0:T(2,128)} %w_ref.1) | copy-start | bytes 196612
  26.0 1.2 %collective-permute-start.8 = (f32[1,128]{1,0:T(1,128)S(1)}, f32[1,128]{1,0:T(1,128)S(1)}, u32[]{:S(2)}, u32[]{:S(2)}) collective-permute-start(f32[1,128]{1,0:T(1,128)S(1)} %get-tuple-element.37), channel_id=1, source_target_pairs={{0,1},{1,0},{2,3},{3,2},{4,5},{5,4},{6,7},{7,6},{8,9},{9,8},{10,11... | collective-permute-start | bytes 1544 | tf_op jit(solution)/shard_map/ppermute | solution.py:217
  27.2 3.0 %collective-permute-start.9 = (f32[1,128]{1,0:T(1,128)S(1)}, f32[1,128]{1,0:T(1,128)S(1)}, u32[]{:S(2)}, u32[]{:S(2)}) collective-permute-start(f32[1,128]{1,0:T(1,128)S(1)} %add.7.norms_ref), channel_id=1, source_target_pairs={{0,3},{1,2},{2,1},{3,0},{4,7},{5,6},{6,5},{7,4},{8,11},{9,10},{10,... | collective-permute-start | bytes 1544 | tf_op jit(solution)/shard_map/ppermute | solution.py:217
  28.5 3.9 %collective-permute-start.11 = (f32[1,128]{1,0:T(1,128)S(1)}, f32[1,128]{1,0:T(1,128)S(1)}, u32[]{:S(2)}, u32[]{:S(2)}) collective-permute-start(f32[1,128]{1,0:T(1,128)S(1)} %add.7.norms_ref), channel_id=1, source_target_pairs={{0,7},{1,6},{2,5},{3,4},{4,3},{5,2},{6,1},{7,0},{8,15},{9,14},{10,... | collective-permute-start | bytes 1544 | tf_op jit(solution)/shard_map/ppermute | solution.py:217
  29.0 3.4 %collective-permute-start.10 = (f32[1,128]{1,0:T(1,128)S(1)}, f32[1,128]{1,0:T(1,128)S(1)}, u32[]{:S(2)}, u32[]{:S(2)}) collective-permute-start(f32[1,128]{1,0:T(1,128)S(1)} %add.7.norms_ref), channel_id=1, source_target_pairs={{0,5},{1,4},{2,7},{3,6},{4,1},{5,0},{6,3},{7,2},{8,13},{9,12},{10,... | collective-permute-start | bytes 1544 | tf_op jit(solution)/shard_map/ppermute | solution.py:217

commit v9 on v7

--- a/solution.py
+++ b/solution.py
@@ -132,10 +132,11 @@
     return values[0]
 
 
-def residual_kernel(n_row, order, rows_total, cols_total, lanes, v_ref, kept_ref, *refs):
-    blocks, (res_ref, beta_ref, norm_ref) = in_order(refs[:n_row], order), refs[n_row:]
+def residual_kernel(n_row, order, rows_total, cols_total, lanes, kept_ref, *refs):
+    blocks, (beta_ref, norm_ref) = in_order(refs[:n_row], order), refs[n_row:]
     p = lax.axis_index("row")
-    own_v, _, wide = v_ref.shape
+    _, block, wide = kept_ref.shape
+    own_v = block // 2
     strips = wide // lanes
     end = 2 * strips * 2 * own_v
     beta2 = pairs([b[end : end + 1, :].astype(f32) + b[end + 1 : end + 2, :].astype(f32) for b in blocks])
@@ -155,10 +156,6 @@
             at = (h * strips + t) * 2 * own_v
             back = scale * pairs([b[at : at + 2 * own_v, :].astype(f32) for b in blocks])
             strip = slice(t * lanes, (t + 1) * lanes)
-            if h == 0:
-                for i in range(2):
-                    half = slice(i * own_v, (i + 1) * own_v)
-                    res_ref[half, strip] = back[half] - beta_here[half] * v_ref[:, i, strip]
             res = back - beta_here * kept_ref[h, :, strip].astype(f32)
             total = total + res * res
         squares.append(total)
@@ -172,7 +169,8 @@
     return rho, rhobar / rho, beta / rho, phibar
 
 
-def vectors_kernel(cols_total, norms_ref, got_ref, beta_ref, res_ref, own_ref, x_ref, w_ref, scalars_ref, x_out, w_out, u_out, v_out, sum_out):
+def vectors_kernel(n_row, order, rows_total, cols_total, norms_ref, got_ref, beta_ref, v_ref, own_ref, x_ref, w_ref, scalars_ref, *refs):
+    blocks, (x_out, w_out, u_out, v_out, sum_out) = in_order(refs[:n_row], order), refs[n_row:]
     p, c = lax.axis_index("row"), lax.axis_index(("col", "cplx"))
     own_v = x_ref.shape[0]
     own_u = u_out.shape[0]
@@ -186,12 +184,18 @@
     alpha = jnp.sqrt(alpha2 / (2 * cols_total) + epsilon)
     step_x = to_column(cosine * phibar / rho, p * own_v, own_v)
     step_w = to_column(sine / rho, p * own_v, own_v) * alpha
-    for i in range(2):
-        w = w_ref[:, i, :]
-        v = res_ref[i * own_v : (i + 1) * own_v, :] / alpha
-        x_out[:, i, :] = x_ref[:, i, :] + step_x * w
-        v_out[:, i, :] = v
-        w_out[:, i, :] = v - step_w * w
+    beta_here = to_column(beta, p * own_v, own_v)
+    scale = rows_total / cols_total / shrink / beta_here
+    lanes = norms_ref.shape[1]
+    for t in range(x_ref.shape[2] // lanes):
+        strip = slice(t * lanes, (t + 1) * lanes)
+        back = pairs([b[t * 2 * own_v : (t + 1) * 2 * own_v, :].astype(f32) for b in blocks])
+        for i in range(2):
+            w = w_ref[:, i, strip]
+            v = (scale * back[i * own_v : (i + 1) * own_v] - beta_here * v_ref[:, i, strip]) / alpha
+            x_out[:, i, strip] = x_ref[:, i, strip] + step_x * w
+            v_out[:, i, strip] = v
+            w_out[:, i, strip] = v - step_w * w
     for b in range(many):
         beta_own = to_column(beta, c * own_u + b * own_v, own_v)
         for i in range(2):
@@ -283,10 +287,9 @@
         vmem=vmem,
     )
     sums = [outs[0]] + [flip(outs[k], "row", k) for k in second]
-    residual_v, beta, norms = call(
+    beta, norms = call(
         partial(residual_kernel, n_row, second, rows_total, cols_total, lanes),
-        [((block, wide), f32), ((1, lanes), f32), ((1, lanes), f32)],
-        v_unit,
+        [((1, lanes), f32), ((1, lanes), f32)],
         kept,
         *sums,
     )
@@ -298,16 +301,17 @@
     across = [mask] + [k * n_cols + m for k in range(1, n_row // 2) for m in (0, mask)]
     got = [flip(norms, ("row", "col", "cplx"), m + 1) for m in across]
     x_next, w_next, u_next, v_next, norms = call(
-        partial(vectors_kernel, cols_total),
+        partial(vectors_kernel, n_row, second, rows_total, cols_total),
         [(x_solution.shape, f32), (w_direction.shape, f32), (u_unit.shape, f32), (v_unit.shape, f32), ((1, lanes), f32)],
         norms,
         got[0],
         beta,
-        residual_v,
+        v_unit,
         own,
         x_solution,
         w_direction,
         scalars,
+        *sums,
         cost=pl.CostEstimate(flops=10**9, bytes_accessed=2**23, transcendentals=0),
     )
     alpha, rhobar, phibar = call(

time: 33.1 us -> 33.1 us (level)
  no operation moved by 1% of the time
where the time goes in v9:
time: 33.1 us; the launch traced here: 33 us
  waiting for transfers between devices  14 us (42%)
  starting transfers between devices  13.9 us (42%)
  Pallas kernels  2.71 us (8%)
  other arithmetic  0.89 us (3%)
  local copies, waits for them, and re-layouts  0.73 us (2%)
  between operations  0.72 us (2%)
    ppermute x12, waiting for transfers between devices, flip(): lax.ppermute(x, axes, [(i, i ^ mask) for i in range(lax.axis_size(axes))])  14 us
    ppermute x12, starting transfers between devices, flip(): lax.ppermute(x, axes, [(i, i ^ mask) for i in range(lax.axis_size(axes))])  13.9 us
    pallas_call x6, Pallas kernels, call(): pl.pallas_call(kernel, out_shape=[jax.ShapeDtypeStruct(s, d) for s, d in...  2.71 us
    convert_element_type x1, other arithmetic, body(): v_low = jnp.swapaxes(v_unit, 0, 1).reshape(block, wide).astype(bf16)  0.87 us
    unnamed x20, local copies, waits for them, and re-layouts  0.72 us
  transfers between devices with their start and end apart: 12, of which 8 were waited for; matrix products, arithmetic and copies ran while one was open for 0% of the time, Pallas kernels for 3%

profile of v9, /device:TPU:0, one launch (start us, length us, event | category | flops | bytes accessed | tf_op | source)
XLA Modules:
  0.0 33.0 jit_solution(13187431360842335636)
XLA Ops:
  0.6 0.9 %convert_bitcast_fusion = bf16[2,8,1024]{2,0,1:T(2,128)(2,1)S(1)} fusion(f32[8,2,1024]{2,1,0:T(2,128)} %v_ref.1), kind=kLoop, calls=%fused_computation.2 | loop fusion | flops 16384 | bytes 98304 | tf_op jit(solution)/shard_map/convert_element_type | solution.py:258
  1.5 4.1 %collective-permute-start.2 = (bf16[16,1024]{1,0:T(8,128)(2,1)S(1)}, bf16[16,1024]{1,0:T(8,128)(2,1)S(1)}, u32[]{:S(2)}, u32[]{:S(2)}) collective-permute-start(bf16[16,1024]{1,0:T(8,128)(2,1)S(1)} %bitcast.11), channel_id=1, source_target_pairs={{0,8},{4,12},{8,0},{12,4},{1,9},{5,13},{9,1},{13,5},{2,10},{6,14},... | collective-permute-start | bytes 98312 | tf_op jit(solution)/shard_map/ppermute | solution.py:218
  5.6 1.3 %collective-permute-start.1 = (bf16[16,1024]{1,0:T(8,128)(2,1)S(1)}, bf16[16,1024]{1,0:T(8,128)(2,1)S(1)}, u32[]{:S(2)}, u32[]{:S(2)}) collective-permute-start(bf16[16,1024]{1,0:T(8,128)(2,1)S(1)} %bitcast.12), channel_id=1, source_target_pairs={{0,12},{4,8},{8,4},{12,0},{1,13},{5,9},{9,5},{13,1},{2,14},{6,10},... | collective-permute-start | bytes 98312 | tf_op jit(solution)/shard_map/ppermute | solution.py:218
  7.0 0.2 collective-permute-start
  7.2 0.6 %copy-done.9 = f32[32]{0:T(128)S(1)} copy-done((f32[32]{0:T(128)S(1)}, f32[32]{0:T(128)}, u32[]{:S(2)}) %copy-start.9) | copy-done | bytes 152
  8.0 3.3 %collective-permute-done.1.refs_2_ = bf16[16,1024]{1,0:T(8,128)(2,1)S(1)} collective-permute-done((bf16[16,1024]{1,0:T(8,128)(2,1)S(1)}, bf16[16,1024]{1,0:T(8,128)(2,1)S(1)}, u32[]{:S(2)}, u32[]{:S(2)}) %collective-permute-start.1) | collective-permute-done | bytes 32800 | tf_op jit(solution)/shard_map/ppermute | solution.py:218
  11.4 0.5 %shard_map.154 = (bf16[64,512]{1,0:T(8,128)(2,1)S(1)}, f32[16,512]{1,0:T(8,128)S(1)}, bf16[2,16,1024]{2,1,0:T(8,128)(2,1)S(1)}) custom-call(f32[2,128]{1,0:T(2,128)S(1)} %get-tuple-element.27.live_ref, bf16[1,2,2,128,512]{4,3,2,1,0:T(8,128)(2,1)S(1)} %copy-done, bf16[1,2,2,128,512]{4,3,2,1,0:T(8,128)(2,1)S(1)} %copy-done.1, f32[8,2,512]{2,1,0:T(2,128)S(1)} %copy-done.3, ...), custom_call_target="tpu_custom_call" | custom-call | tf_op jit(solution)/shard_map/pallas_call | solution.py:18
  11.9 1.2 %collective-permute-done.3.refs_0_ = bf16[64,512]{1,0:T(8,128)(2,1)S(1)} collective-permute-done((bf16[64,512]{1,0:T(8,128)(2,1)S(1)}, bf16[64,512]{1,0:T(8,128)(2,1)S(1)}, u32[]{:S(2)}, u32[]{:S(2)}) %collective-permute-start.3) | collective-permute-done | bytes 65568 | tf_op jit(solution)/shard_map/ppermute | solution.py:218
  13.2 1.6 %collective-permute-start.4 = (bf16[64,512]{1,0:T(8,128)(2,1)S(1)}, bf16[64,512]{1,0:T(8,128)(2,1)S(1)}, u32[]{:S(2)}, u32[]{:S(2)}) collective-permute-start(bf16[64,512]{1,0:T(8,128)(2,1)S(1)} %add_convert_fusion.sum_ref), channel_id=1, source_target_pairs={{0,2},{1,3},{2,0},{3,1},{4,6},{5,7},{6,4},{7,5},{8,10},{9,11},{10,... | collective-permute-start | bytes 196616 | tf_op jit(solution)/shard_map/ppermute | solution.py:218
  14.7 2.8 %collective-permute-done.4.refs_1_ = bf16[64,512]{1,0:T(8,128)(2,1)S(1)} collective-permute-done((bf16[64,512]{1,0:T(8,128)(2,1)S(1)}, bf16[64,512]{1,0:T(8,128)(2,1)S(1)}, u32[]{:S(2)}, u32[]{:S(2)}) %collective-permute-start.4) | collective-permute-done | bytes 65568 | tf_op jit(solution)/shard_map/ppermute | solution.py:218
  17.5 0.5 %shard_map.155 = (bf16[272,128]{1,0:T(8,128)(2,1)S(1)}, bf16[272,128]{1,0:T(8,128)(2,1)S(1)}, bf16[272,128]{1,0:T(8,128)(2,1)S(1)}, bf16[272,128]{1,0:T(8,128)(2,1)S(1)}, f32[16,512]{1,0:T(8,128)S(1)}) custom-call(f32[2,128]{1,0:T(2,128)S(1)} %get-tuple-element.27.live_ref, bf16[1,2,2,128,512]{4,3,2,1,0:T(8,128)(2,1)S(1)} %copy-done, ...), custom_call_target="tpu_custom_call" | custom-call | tf_op jit(solution)/shard_map/pallas_call | solution.py:18
  18.0 1.3 %collective-permute-start.5 = (bf16[272,128]{1,0:T(8,128)(2,1)S(1)}, bf16[272,128]{1,0:T(8,128)(2,1)S(1)}, u32[]{:S(2)}, u32[]{:S(2)}) collective-permute-start(bf16[272,128]{1,0:T(8,128)(2,1)S(1)} %get-tuple-element.33), channel_id=1, source_target_pairs={{0,8},{4,12},{8,0},{12,4},{1,9},{5,13},{9,1},{13,5},{2,10},{6,14},... | collective-permute-start | bytes 208904 | tf_op jit(solution)/shard_map/ppermute | solution.py:218
  19.3 1.0 %collective-permute-start.6 = (bf16[272,128]{1,0:T(8,128)(2,1)S(1)}, bf16[272,128]{1,0:T(8,128)(2,1)S(1)}, u32[]{:S(2)}, u32[]{:S(2)}) collective-permute-start(bf16[272,128]{1,0:T(8,128)(2,1)S(1)} %get-tuple-element.34), channel_id=1, source_target_pairs={{0,12},{4,8},{8,4},{12,0},{1,13},{5,9},{9,5},{13,1},{2,14},{6,10},... | collective-permute-start | bytes 208904 | tf_op jit(solution)/shard_map/ppermute | solution.py:218
  20.3 1.2 %collective-permute-start.7 = (bf16[272,128]{1,0:T(8,128)(2,1)S(1)}, bf16[272,128]{1,0:T(8,128)(2,1)S(1)}, u32[]{:S(2)}, u32[]{:S(2)}) collective-permute-start(bf16[272,128]{1,0:T(8,128)(2,1)S(1)} %get-tuple-element.35), channel_id=1, source_target_pairs={{0,4},{4,0},{8,12},{12,8},{1,5},{5,1},{9,13},{13,9},{2,6},{6,2},{1... | collective-permute-start | bytes 208904 | tf_op jit(solution)/shard_map/ppermute | solution.py:218
  21.5 2.9 %collective-permute-done.5.refs_1_ = bf16[272,128]{1,0:T(8,128)(2,1)S(1)} collective-permute-done((bf16[272,128]{1,0:T(8,128)(2,1)S(1)}, bf16[272,128]{1,0:T(8,128)(2,1)S(1)}, u32[]{:S(2)}, u32[]{:S(2)}) %collective-permute-start.5) | collective-permute-done | bytes 69664 | tf_op jit(solution)/shard_map/ppermute | solution.py:218
  24.4 1.1 %collective-permute-done.6.refs_2_ = bf16[272,128]{1,0:T(8,128)(2,1)S(1)} collective-permute-done((bf16[272,128]{1,0:T(8,128)(2,1)S(1)}, bf16[272,128]{1,0:T(8,128)(2,1)S(1)}, u32[]{:S(2)}, u32[]{:S(2)}) %collective-permute-start.6) | collective-permute-done | bytes 69664 | tf_op jit(solution)/shard_map/ppermute | solution.py:218
  25.5 0.4 %collective-permute-done.7.refs_3_ = bf16[272,128]{1,0:T(8,128)(2,1)S(1)} collective-permute-done((bf16[272,128]{1,0:T(8,128)(2,1)S(1)}, bf16[272,128]{1,0:T(8,128)(2,1)S(1)}, u32[]{:S(2)}, u32[]{:S(2)}) %collective-permute-start.7) | collective-permute-done | bytes 69664 | tf_op jit(solution)/shard_map/ppermute | solution.py:218
  26.2 1.1 %collective-permute-done.8 = f32[1,128]{1,0:T(1,128)S(1)} collective-permute-done((f32[1,128]{1,0:T(1,128)S(1)}, f32[1,128]{1,0:T(1,128)S(1)}, u32[]{:S(2)}, u32[]{:S(2)}) %collective-permute-start.8) | collective-permute-done | bytes 544 | tf_op jit(solution)/shard_map/ppermute | solution.py:218
  27.3 1.3 %collective-permute-start.9 = (f32[1,128]{1,0:T(1,128)S(1)}, f32[1,128]{1,0:T(1,128)S(1)}, u32[]{:S(2)}, u32[]{:S(2)}) collective-permute-start(f32[1,128]{1,0:T(1,128)S(1)} %add.7.norms_ref), channel_id=1, source_target_pairs={{0,3},{1,2},{2,1},{3,0},{4,7},{5,6},{6,5},{7,4},{8,11},{9,10},{10,... | collective-permute-start | bytes 1544 | tf_op jit(solution)/shard_map/ppermute | solution.py:218
  28.6 0.5 %collective-permute-start.11 = (f32[1,128]{1,0:T(1,128)S(1)}, f32[1,128]{1,0:T(1,128)S(1)}, u32[]{:S(2)}, u32[]{:S(2)}) collective-permute-start(f32[1,128]{1,0:T(1,128)S(1)} %add.7.norms_ref), channel_id=1, source_target_pairs={{0,7},{1,6},{2,5},{3,4},{4,3},{5,2},{6,1},{7,0},{8,15},{9,14},{10,... | collective-permute-start | bytes 1544 | tf_op jit(solution)/shard_map/ppermute | solution.py:218
  29.0 1.3 %collective-permute-start.10 = (f32[1,128]{1,0:T(1,128)S(1)}, f32[1,128]{1,0:T(1,128)S(1)}, u32[]{:S(2)}, u32[]{:S(2)}) collective-permute-start(f32[1,128]{1,0:T(1,128)S(1)} %add.7.norms_ref), channel_id=1, source_target_pairs={{0,5},{1,4},{2,7},{3,6},{4,1},{5,0},{6,3},{7,2},{8,13},{9,12},{10,... | collective-permute-start | bytes 1544 | tf_op jit(solution)/shard_map/ppermute | solution.py:218
  30.3 1.0 %shard_map.157 = (f32[8,2,1024]{2,1,0:T(2,128)}, f32[8,2,1024]{2,1,0:T(2,128)}, f32[8,2,512]{2,1,0:T(2,128)}, f32[8,2,1024]{2,1,0:T(2,128)}, f32[1,128]{1,0:T(1,128)S(1)}) custom-call(f32[1,128]{1,0:T(1,128)S(1)} %add.7.norms_ref, f32[1,128]{1,0:T(1,128)S(1)} %collective-permute-done.9.got_ref, f32[1,128]{1,0:T(1,128)S(1)} %get-tuple-element.37.beta_ref, ...), custom_call_target="tpu_custom_call" | custom-call | flops 1000000000 | bytes 8388608 | tf_op jit(solution)/shard_map/pallas_call | solution.py:18
  31.3 1.1 %collective-permute-done.11.refs_2_ = f32[1,128]{1,0:T(1,128)S(1)} collective-permute-done((f32[1,128]{1,0:T(1,128)S(1)}, f32[1,128]{1,0:T(1,128)S(1)}, u32[]{:S(2)}, u32[]{:S(2)}) %collective-permute-start.11) | collective-permute-done | bytes 544 | tf_op jit(solution)/shard_map/ppermute | solution.py:218
  32.4 0.5 %shard_map.158 = (f32[1,32]{1,0:T(1,128)}, f32[1,32]{1,0:T(1,128)}, f32[1,32]{1,0:T(1,128)}) custom-call(f32[1,128]{1,0:T(1,128)S(1)} %get-tuple-element.37.beta_ref, f32[3,32]{1,0:T(4,128)S(1)} %get-tuple-element.28.alpha_ref.scalars_ref, f32[1,128]{1,0:T(1,128)S(1)} %get-tuple-element.43.refs_0_, f32[1,128]{1,0:T(1,128)S(1)} %collective-permute-done.10.refs_1_, ...), custom_call_target="tpu_custom_call" | custom-call | tf_op jit(solution)/shard_map/pallas_call | solution.py:18
  (30 shorter events, 0.5 us)
Async XLA Ops:
  1.5 6.5 %collective-permute-start.2 = (bf16[16,1024]{1,0:T(8,128)(2,1)S(1)}, bf16[16,1024]{1,0:T(8,128)(2,1)S(1)}, u32[]{:S(2)}, u32[]{:S(2)}) collective-permute-start(bf16[16,1024]{1,0:T(8,128)(2,1)S(1)} %bitcast.11), channel_id=1, source_target_pairs={{0,8},{4,12},{8,0},{12,4},{1,9},{5,13},{9,1},{13,5},{2,10},{6,14},... | collective-permute-start | bytes 98312 | tf_op jit(solution)/shard_map/ppermute | solution.py:218
  5.6 5.7 %collective-permute-start.1 = (bf16[16,1024]{1,0:T(8,128)(2,1)S(1)}, bf16[16,1024]{1,0:T(8,128)(2,1)S(1)}, u32[]{:S(2)}, u32[]{:S(2)}) collective-permute-start(bf16[16,1024]{1,0:T(8,128)(2,1)S(1)} %bitcast.12), channel_id=1, source_target_pairs={{0,12},{4,8},{8,4},{12,0},{1,13},{5,9},{9,5},{13,1},{2,14},{6,10},... | collective-permute-start | bytes 98312 | tf_op jit(solution)/shard_map/ppermute | solution.py:218
  7.0 4.4 %collective-permute-start = (bf16[16,1024]{1,0:T(8,128)(2,1)S(1)}, bf16[16,1024]{1,0:T(8,128)(2,1)S(1)}, u32[]{:S(2)}, u32[]{:S(2)}) collective-permute-start(bf16[16,1024]{1,0:T(8,128)(2,1)S(1)} %bitcast.13), channel_id=1, source_target_pairs={{0,4},{4,0},{8,12},{12,8},{1,5},{5,1},{9,13},{13,9},{2,6},{6,2},{1... | collective-permute-start | bytes 98312 | tf_op jit(solution)/shard_map/ppermute | solution.py:218
  7.2 0.7 %copy-start.9 = (f32[32]{0:T(128)S(1)}, f32[32]{0:T(128)}, u32[]{:S(2)}) copy-start(f32[32]{0:T(128)} %param.19) | copy-start | bytes 388
  7.2 0.7 %copy-start.6 = (s32[1,2]{1,0:T(1,128)S(1)}, s32[1,2]{1,0:T(1,128)}, u32[]{:S(2)}) copy-start(s32[1,2]{1,0:T(1,128)} %ranks_ref.1) | copy-start | bytes 28
  7.2 0.7 %copy-start.7 = (f32[32]{0:T(128)S(1)}, f32[32]{0:T(128)}, u32[]{:S(2)}) copy-start(f32[32]{0:T(128)} %param.17) | copy-start | bytes 388
  7.2 0.7 %copy-start.8 = (f32[32]{0:T(128)S(1)}, f32[32]{0:T(128)}, u32[]{:S(2)}) copy-start(f32[32]{0:T(128)} %param.18) | copy-start | bytes 388
  7.9 3.4 %copy-start = (bf16[1,2,2,128,512]{4,3,2,1,0:T(8,128)(2,1)S(1)}, bf16[1,2,2,128,512]{4,3,2,1,0:T(8,128)(2,1)}, u32[]{:S(2)}) copy-start(bf16[1,2,2,128,512]{4,3,2,1,0:T(8,128)(2,1)} %u_bases.3) | copy-start | bytes 1572868
  7.9 3.4 %copy-start.1 = (bf16[1,2,2,128,512]{4,3,2,1,0:T(8,128)(2,1)S(1)}, bf16[1,2,2,128,512]{4,3,2,1,0:T(8,128)(2,1)}, u32[]{:S(2)}) copy-start(bf16[1,2,2,128,512]{4,3,2,1,0:T(8,128)(2,1)} %v_bases.3) | copy-start | bytes 1572868
  7.9 3.4 %copy-start.3 = (f32[8,2,512]{2,1,0:T(2,128)S(1)}, f32[8,2,512]{2,1,0:T(2,128)}, u32[]{:S(2)}) copy-start(f32[8,2,512]{2,1,0:T(2,128)} %u_ref.1) | copy-start | bytes 98308
  11.8 1.3 %collective-permute-start.3 = (bf16[64,512]{1,0:T(8,128)(2,1)S(1)}, bf16[64,512]{1,0:T(8,128)(2,1)S(1)}, u32[]{:S(2)}, u32[]{:S(2)}) collective-permute-start(bf16[64,512]{1,0:T(8,128)(2,1)S(1)} %get-tuple-element.31), channel_id=1, source_target_pairs={{0,1},{1,0},{2,3},{3,2},{4,5},{5,4},{6,7},{7,6},{8,9},{9,8},{10,11... | collective-permute-start | bytes 196616 | tf_op jit(solution)/shard_map/ppermute | solution.py:218
  13.2 4.3 %collective-permute-start.4 = (bf16[64,512]{1,0:T(8,128)(2,1)S(1)}, bf16[64,512]{1,0:T(8,128)(2,1)S(1)}, u32[]{:S(2)}, u32[]{:S(2)}) collective-permute-start(bf16[64,512]{1,0:T(8,128)(2,1)S(1)} %add_convert_fusion.sum_ref), channel_id=1, source_target_pairs={{0,2},{1,3},{2,0},{3,1},{4,6},{5,7},{6,4},{7,5},{8,10},{9,11},{10,... | collective-permute-start | bytes 196616 | tf_op jit(solution)/shard_map/ppermute | solution.py:218
  18.0 6.5 %collective-permute-start.5 = (bf16[272,128]{1,0:T(8,128)(2,1)S(1)}, bf16[272,128]{1,0:T(8,128)(2,1)S(1)}, u32[]{:S(2)}, u32[]{:S(2)}) collective-permute-start(bf16[272,128]{1,0:T(8,128)(2,1)S(1)} %get-tuple-element.33), channel_id=1, source_target_pairs={{0,8},{4,12},{8,0},{12,4},{1,9},{5,13},{9,1},{13,5},{2,10},{6,14},... | collective-permute-start | bytes 208904 | tf_op jit(solution)/shard_map/ppermute | solution.py:218
  19.3 6.3 %collective-permute-start.6 = (bf16[272,128]{1,0:T(8,128)(2,1)S(1)}, bf16[272,128]{1,0:T(8,128)(2,1)S(1)}, u32[]{:S(2)}, u32[]{:S(2)}) collective-permute-start(bf16[272,128]{1,0:T(8,128)(2,1)S(1)} %get-tuple-element.34), channel_id=1, source_target_pairs={{0,12},{4,8},{8,4},{12,0},{1,13},{5,9},{9,5},{13,1},{2,14},{6,10},... | collective-permute-start | bytes 208904 | tf_op jit(solution)/shard_map/ppermute | solution.py:218
  20.3 5.6 %collective-permute-start.7 = (bf16[272,128]{1,0:T(8,128)(2,1)S(1)}, bf16[272,128]{1,0:T(8,128)(2,1)S(1)}, u32[]{:S(2)}, u32[]{:S(2)}) collective-permute-start(bf16[272,128]{1,0:T(8,128)(2,1)S(1)} %get-tuple-element.35), channel_id=1, source_target_pairs={{0,4},{4,0},{8,12},{12,8},{1,5},{5,1},{9,13},{13,9},{2,6},{6,2},{1... | collective-permute-start | bytes 208904 | tf_op jit(solution)/shard_map/ppermute | solution.py:218
  25.9 4.4 %copy-start.2 = (f32[8,2,1024]{2,1,0:T(2,128)S(1)}, f32[8,2,1024]{2,1,0:T(2,128)}, u32[]{:S(2)}) copy-start(f32[8,2,1024]{2,1,0:T(2,128)} %v_ref.1) | copy-start | bytes 196612
  25.9 4.4 %copy-start.4 = (f32[8,2,1024]{2,1,0:T(2,128)S(1)}, f32[8,2,1024]{2,1,0:T(2,128)}, u32[]{:S(2)}) copy-start(f32[8,2,1024]{2,1,0:T(2,128)} %x_ref.1) | copy-start | bytes 196612
  25.9 4.4 %copy-start.5 = (f32[8,2,1024]{2,1,0:T(2,128)S(1)}, f32[8,2,1024]{2,1,0:T(2,128)}, u32[]{:S(2)}) copy-start(f32[8,2,1024]{2,1,0:T(2,128)} %w_ref.1) | copy-start | bytes 196612
  26.1 1.2 %collective-permute-start.8 = (f32[1,128]{1,0:T(1,128)S(1)}, f32[1,128]{1,0:T(1,128)S(1)}, u32[]{:S(2)}, u32[]{:S(2)}) collective-permute-start(f32[1,128]{1,0:T(1,128)S(1)} %get-tuple-element.36), channel_id=1, source_target_pairs={{0,1},{1,0},{2,3},{3,2},{4,5},{5,4},{6,7},{7,6},{8,9},{9,8},{10,11... | collective-permute-start | bytes 1544 | tf_op jit(solution)/shard_map/ppermute | solution.py:218
  27.3 3.0 %collective-permute-start.9 = (f32[1,128]{1,0:T(1,128)S(1)}, f32[1,128]{1,0:T(1,128)S(1)}, u32[]{:S(2)}, u32[]{:S(2)}) collective-permute-start(f32[1,128]{1,0:T(1,128)S(1)} %add.7.norms_ref), channel_id=1, source_target_pairs={{0,3},{1,2},{2,1},{3,0},{4,7},{5,6},{6,5},{7,4},{8,11},{9,10},{10,... | collective-permute-start | bytes 1544 | tf_op jit(solution)/shard_map/ppermute | solution.py:218
  28.6 3.9 %collective-permute-start.11 = (f32[1,128]{1,0:T(1,128)S(1)}, f32[1,128]{1,0:T(1,128)S(1)}, u32[]{:S(2)}, u32[]{:S(2)}) collective-permute-start(f32[1,128]{1,0:T(1,128)S(1)} %add.7.norms_ref), channel_id=1, source_target_pairs={{0,7},{1,6},{2,5},{3,4},{4,3},{5,2},{6,1},{7,0},{8,15},{9,14},{10,... | collective-permute-start | bytes 1544 | tf_op jit(solution)/shard_map/ppermute | solution.py:218
  29.0 3.4 %collective-permute-start.10 = (f32[1,128]{1,0:T(1,128)S(1)}, f32[1,128]{1,0:T(1,128)S(1)}, u32[]{:S(2)}, u32[]{:S(2)}) collective-permute-start(f32[1,128]{1,0:T(1,128)S(1)} %add.7.norms_ref), channel_id=1, source_target_pairs={{0,5},{1,4},{2,7},{3,6},{4,1},{5,0},{6,3},{7,2},{8,13},{9,12},{10,... | collective-permute-start | bytes 1544 | tf_op jit(solution)/shard_map/ppermute | solution.py:218

commit v10 on v9

--- a/solution.py
+++ b/solution.py
@@ -47,9 +47,12 @@
 
 
 def through(inner, outer, live_ref, x, own):
-    tiles, _, ranks, size = inner.shape[1:]
+    tiles, _, ranks, size = outer.shape[1:]
     mids = []
-    gs = [dot(x(q), inner[0, q].reshape(2 * ranks, size), True) for q in range(tiles)]
+    if len(inner.shape) == 3:
+        gs = [dot(x(q), inner[q], False) for q in range(tiles)]
+    else:
+        gs = [dot(x(q), inner[0, q].reshape(2 * ranks, size), True) for q in range(tiles)]
     for q, g in enumerate(gs):
         rows = g.shape[0]
         g = g.reshape(rows // (2 * own), 2, own, 2 * ranks)
@@ -94,7 +97,7 @@
     low_ref[...] = total[...].astype(bf16)
 
 
-def adjoint_kernel(n_row, n_got, own_v, own_u, lanes, live_ref, u_bases, v_bases, own_ref, sum_ref, *refs):
+def adjoint_kernel(n_row, n_got, own_v, own_u, lanes, live_ref, u_turned, v_bases, own_ref, sum_ref, *refs):
     got, outs, own_out = refs[:n_got], refs[n_got : n_got + n_row], refs[n_got + n_row]
     p, c = lax.axis_index("row"), lax.axis_index(("col", "cplx"))
     many = own_u // own_v
@@ -115,7 +118,7 @@
     low = (beta2 - high.astype(f32)).astype(bf16)
     tail = jnp.where(iota((16, lanes), 0) == 0, high.astype(f32), low.astype(f32)).astype(bf16)
     x = (res * shrink).astype(bf16)
-    parts = through(u_bases, v_bases, live_ref, lambda q: x, own_v)
+    parts = through(u_turned, v_bases, live_ref, lambda q: x, own_v)
     wide = jnp.concatenate(parts, 1).astype(bf16)
     strips = wide.shape[1] // lanes
     for k, out in enumerate(outs):
@@ -257,6 +260,8 @@
     second = [*range(2, n_row), 1]
     v_low = jnp.swapaxes(v_unit, 0, 1).reshape(block, wide).astype(bf16)
     blocks = [v_low] + [flip(v_low, "row", k) for k in first]
+    tiles, _, ranks, size = u_bases.shape[1:]
+    u_turned = jnp.swapaxes(u_bases.reshape(tiles, 2 * ranks, size), 1, 2)
     low, own, kept = call(
         partial(forward_kernel, n_row, first, own_v, own_u),
         [((2 * rhs, tile_size), bf16), ((2 * own_u, tile_size), f32), ((2, block, wide), bf16)],
@@ -279,7 +284,7 @@
         partial(adjoint_kernel, n_row, len(got), own_v, own_u, lanes),
         [((2 * block * (wide // lanes) + 16, lanes), bf16)] * n_row + [((2 * own_u, tile_size), f32)],
         live,
-        u_bases,
+        u_turned,
         v_bases,
         own,
         low,

time: 33.1 us -> 33.1 us (level)
  transfers between devices with their start and end apart: 12 -> 12, of which waited for: 8 -> 8; matrix products, arithmetic and copies ran while one was open for 0% -> 1% of each run, Pallas kernels for 3% -> 3%
where the time goes in v10:
time: 33.1 us; the launch traced here: 32.9 us
  starting transfers between devices  13.9 us (42%)
  waiting for transfers between devices  13.8 us (42%)
  Pallas kernels  2.63 us (8%)
  local copies, waits for them, and re-layouts  0.93 us (3%)
  other arithmetic  0.89 us (3%)
  between operations  0.73 us (2%)
    ppermute x12, starting transfers between devices, flip(): lax.ppermute(x, axes, [(i, i ^ mask) for i in range(lax.axis_size(axes))])  13.9 us
    ppermute x12, waiting for transfers between devices, flip(): lax.ppermute(x, axes, [(i, i ^ mask) for i in range(lax.axis_size(axes))])  13.8 us
    pallas_call x6, Pallas kernels, call(): pl.pallas_call(kernel, out_shape=[jax.ShapeDtypeStruct(s, d) for s, d in...  2.63 us
    convert_element_type x1, other arithmetic, body(): v_low = jnp.swapaxes(v_unit, 0, 1).reshape(block, wide).astype(bf16)  0.87 us
    unnamed x20, local copies, waits for them, and re-layouts  0.72 us
  transfers between devices with their start and end apart: 12, of which 8 were waited for; matrix products, arithmetic and copies ran while one was open for 1% of the time, Pallas kernels for 3%

profile of v10, /device:TPU:0, one launch (start us, length us, event | category | flops | bytes accessed | tf_op | source)
XLA Modules:
  0.0 32.9 jit_solution(17388462820048409703)
XLA Ops:
  0.6 0.9 %convert_bitcast_fusion = bf16[2,8,1024]{2,0,1:T(2,128)(2,1)S(1)} fusion(f32[8,2,1024]{2,1,0:T(2,128)} %v_ref.1), kind=kLoop, calls=%fused_computation.2 | loop fusion | flops 16384 | bytes 98304 | tf_op jit(solution)/shard_map/convert_element_type | solution.py:261
  1.5 4.1 %collective-permute-start.2 = (bf16[16,1024]{1,0:T(8,128)(2,1)S(1)}, bf16[16,1024]{1,0:T(8,128)(2,1)S(1)}, u32[]{:S(2)}, u32[]{:S(2)}) collective-permute-start(bf16[16,1024]{1,0:T(8,128)(2,1)S(1)} %bitcast.15), channel_id=1, source_target_pairs={{0,8},{4,12},{8,0},{12,4},{1,9},{5,13},{9,1},{13,5},{2,10},{6,14},... | collective-permute-start | bytes 98312 | tf_op jit(solution)/shard_map/ppermute | solution.py:221
  5.6 1.3 %collective-permute-start.1 = (bf16[16,1024]{1,0:T(8,128)(2,1)S(1)}, bf16[16,1024]{1,0:T(8,128)(2,1)S(1)}, u32[]{:S(2)}, u32[]{:S(2)}) collective-permute-start(bf16[16,1024]{1,0:T(8,128)(2,1)S(1)} %bitcast.16), channel_id=1, source_target_pairs={{0,12},{4,8},{8,4},{12,0},{1,13},{5,9},{9,5},{13,1},{2,14},{6,10},... | collective-permute-start | bytes 98312 | tf_op jit(solution)/shard_map/ppermute | solution.py:221
  7.0 0.2 collective-permute-start
  7.2 0.6 %copy-done.9 = f32[32]{0:T(128)S(1)} copy-done((f32[32]{0:T(128)S(1)}, f32[32]{0:T(128)}, u32[]{:S(2)}) %copy-start.9) | copy-done | bytes 152
  8.0 3.3 %collective-permute-done.1.refs_2_ = bf16[16,1024]{1,0:T(8,128)(2,1)S(1)} collective-permute-done((bf16[16,1024]{1,0:T(8,128)(2,1)S(1)}, bf16[16,1024]{1,0:T(8,128)(2,1)S(1)}, u32[]{:S(2)}, u32[]{:S(2)}) %collective-permute-start.1) | collective-permute-done | bytes 32800 | tf_op jit(solution)/shard_map/ppermute | solution.py:221
  11.4 0.5 %shard_map.154 = (bf16[64,512]{1,0:T(8,128)(2,1)S(1)}, f32[16,512]{1,0:T(8,128)S(1)}, bf16[2,16,1024]{2,1,0:T(8,128)(2,1)S(1)}) custom-call(f32[2,128]{1,0:T(2,128)S(1)} %get-tuple-element.27.live_ref, bf16[1,2,2,128,512]{4,3,2,1,0:T(8,128)(2,1)S(1)} %copy-done, bf16[1,2,2,128,512]{4,3,2,1,0:T(8,128)(2,1)S(1)} %copy-done.1, f32[8,2,512]{2,1,0:T(2,128)S(1)} %copy-done.3, ...), custom_call_target="tpu_custom_call" | custom-call | tf_op jit(solution)/shard_map/pallas_call | solution.py:18
  11.9 1.2 %collective-permute-done.3.refs_0_ = bf16[64,512]{1,0:T(8,128)(2,1)S(1)} collective-permute-done((bf16[64,512]{1,0:T(8,128)(2,1)S(1)}, bf16[64,512]{1,0:T(8,128)(2,1)S(1)}, u32[]{:S(2)}, u32[]{:S(2)}) %collective-permute-start.3) | collective-permute-done | bytes 65568 | tf_op jit(solution)/shard_map/ppermute | solution.py:221
  13.2 1.6 %collective-permute-start.4 = (bf16[64,512]{1,0:T(8,128)(2,1)S(1)}, bf16[64,512]{1,0:T(8,128)(2,1)S(1)}, u32[]{:S(2)}, u32[]{:S(2)}) collective-permute-start(bf16[64,512]{1,0:T(8,128)(2,1)S(1)} %add_convert_fusion.sum_ref), channel_id=1, source_target_pairs={{0,2},{1,3},{2,0},{3,1},{4,6},{5,7},{6,4},{7,5},{8,10},{9,11},{10,... | collective-permute-start | bytes 196616 | tf_op jit(solution)/shard_map/ppermute | solution.py:221
  14.9 2.6 %collective-permute-done.4.refs_1_ = bf16[64,512]{1,0:T(8,128)(2,1)S(1)} collective-permute-done((bf16[64,512]{1,0:T(8,128)(2,1)S(1)}, bf16[64,512]{1,0:T(8,128)(2,1)S(1)}, u32[]{:S(2)}, u32[]{:S(2)}) %collective-permute-start.4) | collective-permute-done | bytes 65568 | tf_op jit(solution)/shard_map/ppermute | solution.py:221
  17.5 0.4 %shard_map.155 = (bf16[272,128]{1,0:T(8,128)(2,1)S(1)}, bf16[272,128]{1,0:T(8,128)(2,1)S(1)}, bf16[272,128]{1,0:T(8,128)(2,1)S(1)}, bf16[272,128]{1,0:T(8,128)(2,1)S(1)}, f32[16,512]{1,0:T(8,128)S(1)}) custom-call(f32[2,128]{1,0:T(2,128)S(1)} %get-tuple-element.27.live_ref, bf16[2,512,256]{2,1,0:T(8,128)(2,1)S(1)} %bitcast.14, ...), custom_call_target="tpu_custom_call" | custom-call | tf_op jit(solution)/shard_map/pallas_call | solution.py:18
  17.9 1.3 %collective-permute-start.5 = (bf16[272,128]{1,0:T(8,128)(2,1)S(1)}, bf16[272,128]{1,0:T(8,128)(2,1)S(1)}, u32[]{:S(2)}, u32[]{:S(2)}) collective-permute-start(bf16[272,128]{1,0:T(8,128)(2,1)S(1)} %get-tuple-element.33), channel_id=1, source_target_pairs={{0,8},{4,12},{8,0},{12,4},{1,9},{5,13},{9,1},{13,5},{2,10},{6,14},... | collective-permute-start | bytes 208904 | tf_op jit(solution)/shard_map/ppermute | solution.py:221
  19.2 1.0 %collective-permute-start.6 = (bf16[272,128]{1,0:T(8,128)(2,1)S(1)}, bf16[272,128]{1,0:T(8,128)(2,1)S(1)}, u32[]{:S(2)}, u32[]{:S(2)}) collective-permute-start(bf16[272,128]{1,0:T(8,128)(2,1)S(1)} %get-tuple-element.34), channel_id=1, source_target_pairs={{0,12},{4,8},{8,4},{12,0},{1,13},{5,9},{9,5},{13,1},{2,14},{6,10},... | collective-permute-start | bytes 208904 | tf_op jit(solution)/shard_map/ppermute | solution.py:221
  20.2 1.2 %collective-permute-start.7 = (bf16[272,128]{1,0:T(8,128)(2,1)S(1)}, bf16[272,128]{1,0:T(8,128)(2,1)S(1)}, u32[]{:S(2)}, u32[]{:S(2)}) collective-permute-start(bf16[272,128]{1,0:T(8,128)(2,1)S(1)} %get-tuple-element.35), channel_id=1, source_target_pairs={{0,4},{4,0},{8,12},{12,8},{1,5},{5,1},{9,13},{13,9},{2,6},{6,2},{1... | collective-permute-start | bytes 208904 | tf_op jit(solution)/shard_map/ppermute | solution.py:221
  21.4 2.9 %collective-permute-done.5.refs_1_ = bf16[272,128]{1,0:T(8,128)(2,1)S(1)} collective-permute-done((bf16[272,128]{1,0:T(8,128)(2,1)S(1)}, bf16[272,128]{1,0:T(8,128)(2,1)S(1)}, u32[]{:S(2)}, u32[]{:S(2)}) %collective-permute-start.5) | collective-permute-done | bytes 69664 | tf_op jit(solution)/shard_map/ppermute | solution.py:221
  24.4 1.1 %collective-permute-done.6.refs_2_ = bf16[272,128]{1,0:T(8,128)(2,1)S(1)} collective-permute-done((bf16[272,128]{1,0:T(8,128)(2,1)S(1)}, bf16[272,128]{1,0:T(8,128)(2,1)S(1)}, u32[]{:S(2)}, u32[]{:S(2)}) %collective-permute-start.6) | collective-permute-done | bytes 69664 | tf_op jit(solution)/shard_map/ppermute | solution.py:221
  25.4 0.4 %collective-permute-done.7.refs_3_ = bf16[272,128]{1,0:T(8,128)(2,1)S(1)} collective-permute-done((bf16[272,128]{1,0:T(8,128)(2,1)S(1)}, bf16[272,128]{1,0:T(8,128)(2,1)S(1)}, u32[]{:S(2)}, u32[]{:S(2)}) %collective-permute-start.7) | collective-permute-done | bytes 69664 | tf_op jit(solution)/shard_map/ppermute | solution.py:221
  26.1 1.1 %collective-permute-done.8 = f32[1,128]{1,0:T(1,128)S(1)} collective-permute-done((f32[1,128]{1,0:T(1,128)S(1)}, f32[1,128]{1,0:T(1,128)S(1)}, u32[]{:S(2)}, u32[]{:S(2)}) %collective-permute-start.8) | collective-permute-done | bytes 544 | tf_op jit(solution)/shard_map/ppermute | solution.py:221
  27.2 1.3 %collective-permute-start.9 = (f32[1,128]{1,0:T(1,128)S(1)}, f32[1,128]{1,0:T(1,128)S(1)}, u32[]{:S(2)}, u32[]{:S(2)}) collective-permute-start(f32[1,128]{1,0:T(1,128)S(1)} %add.7.norms_ref), channel_id=1, source_target_pairs={{0,3},{1,2},{2,1},{3,0},{4,7},{5,6},{6,5},{7,4},{8,11},{9,10},{10,... | collective-permute-start | bytes 1544 | tf_op jit(solution)/shard_map/ppermute | solution.py:221
  28.5 0.5 %collective-permute-start.11 = (f32[1,128]{1,0:T(1,128)S(1)}, f32[1,128]{1,0:T(1,128)S(1)}, u32[]{:S(2)}, u32[]{:S(2)}) collective-permute-start(f32[1,128]{1,0:T(1,128)S(1)} %add.7.norms_ref), channel_id=1, source_target_pairs={{0,7},{1,6},{2,5},{3,4},{4,3},{5,2},{6,1},{7,0},{8,15},{9,14},{10,... | collective-permute-start | bytes 1544 | tf_op jit(solution)/shard_map/ppermute | solution.py:221
  28.9 1.3 %collective-permute-start.10 = (f32[1,128]{1,0:T(1,128)S(1)}, f32[1,128]{1,0:T(1,128)S(1)}, u32[]{:S(2)}, u32[]{:S(2)}) collective-permute-start(f32[1,128]{1,0:T(1,128)S(1)} %add.7.norms_ref), channel_id=1, source_target_pairs={{0,5},{1,4},{2,7},{3,6},{4,1},{5,0},{6,3},{7,2},{8,13},{9,12},{10,... | collective-permute-start | bytes 1544 | tf_op jit(solution)/shard_map/ppermute | solution.py:221
  30.2 1.0 %shard_map.157 = (f32[8,2,1024]{2,1,0:T(2,128)}, f32[8,2,1024]{2,1,0:T(2,128)}, f32[8,2,512]{2,1,0:T(2,128)}, f32[8,2,1024]{2,1,0:T(2,128)}, f32[1,128]{1,0:T(1,128)S(1)}) custom-call(f32[1,128]{1,0:T(1,128)S(1)} %add.7.norms_ref, f32[1,128]{1,0:T(1,128)S(1)} %collective-permute-done.9.got_ref, f32[1,128]{1,0:T(1,128)S(1)} %get-tuple-element.37.beta_ref, ...), custom_call_target="tpu_custom_call" | custom-call | flops 1000000000 | bytes 8388608 | tf_op jit(solution)/shard_map/pallas_call | solution.py:18
  31.2 1.1 %collective-permute-done.11.refs_2_ = f32[1,128]{1,0:T(1,128)S(1)} collective-permute-done((f32[1,128]{1,0:T(1,128)S(1)}, f32[1,128]{1,0:T(1,128)S(1)}, u32[]{:S(2)}, u32[]{:S(2)}) %collective-permute-start.11) | collective-permute-done | bytes 544 | tf_op jit(solution)/shard_map/ppermute | solution.py:221
  32.4 0.5 %shard_map.158 = (f32[1,32]{1,0:T(1,128)}, f32[1,32]{1,0:T(1,128)}, f32[1,32]{1,0:T(1,128)}) custom-call(f32[1,128]{1,0:T(1,128)S(1)} %get-tuple-element.37.beta_ref, f32[3,32]{1,0:T(4,128)S(1)} %get-tuple-element.28.alpha_ref.scalars_ref, f32[1,128]{1,0:T(1,128)S(1)} %get-tuple-element.43.refs_0_, f32[1,128]{1,0:T(1,128)S(1)} %collective-permute-done.10.refs_1_, ...), custom_call_target="tpu_custom_call" | custom-call | tf_op jit(solution)/shard_map/pallas_call | solution.py:18
  (31 shorter events, 0.7 us)
Async XLA Ops:
  1.5 6.5 %collective-permute-start.2 = (bf16[16,1024]{1,0:T(8,128)(2,1)S(1)}, bf16[16,1024]{1,0:T(8,128)(2,1)S(1)}, u32[]{:S(2)}, u32[]{:S(2)}) collective-permute-start(bf16[16,1024]{1,0:T(8,128)(2,1)S(1)} %bitcast.15), channel_id=1, source_target_pairs={{0,8},{4,12},{8,0},{12,4},{1,9},{5,13},{9,1},{13,5},{2,10},{6,14},... | collective-permute-start | bytes 98312 | tf_op jit(solution)/shard_map/ppermute | solution.py:221
  5.6 5.7 %collective-permute-start.1 = (bf16[16,1024]{1,0:T(8,128)(2,1)S(1)}, bf16[16,1024]{1,0:T(8,128)(2,1)S(1)}, u32[]{:S(2)}, u32[]{:S(2)}) collective-permute-start(bf16[16,1024]{1,0:T(8,128)(2,1)S(1)} %bitcast.16), channel_id=1, source_target_pairs={{0,12},{4,8},{8,4},{12,0},{1,13},{5,9},{9,5},{13,1},{2,14},{6,10},... | collective-permute-start | bytes 98312 | tf_op jit(solution)/shard_map/ppermute | solution.py:221
  7.0 4.4 %collective-permute-start = (bf16[16,1024]{1,0:T(8,128)(2,1)S(1)}, bf16[16,1024]{1,0:T(8,128)(2,1)S(1)}, u32[]{:S(2)}, u32[]{:S(2)}) collective-permute-start(bf16[16,1024]{1,0:T(8,128)(2,1)S(1)} %bitcast.17), channel_id=1, source_target_pairs={{0,4},{4,0},{8,12},{12,8},{1,5},{5,1},{9,13},{13,9},{2,6},{6,2},{1... | collective-permute-start | bytes 98312 | tf_op jit(solution)/shard_map/ppermute | solution.py:221
  7.2 0.7 %copy-start.9 = (f32[32]{0:T(128)S(1)}, f32[32]{0:T(128)}, u32[]{:S(2)}) copy-start(f32[32]{0:T(128)} %param.19) | copy-start | bytes 388
  7.2 0.7 %copy-start.6 = (s32[1,2]{1,0:T(1,128)S(1)}, s32[1,2]{1,0:T(1,128)}, u32[]{:S(2)}) copy-start(s32[1,2]{1,0:T(1,128)} %ranks_ref.1) | copy-start | bytes 28
  7.2 0.7 %copy-start.7 = (f32[32]{0:T(128)S(1)}, f32[32]{0:T(128)}, u32[]{:S(2)}) copy-start(f32[32]{0:T(128)} %param.17) | copy-start | bytes 388
  7.2 0.7 %copy-start.8 = (f32[32]{0:T(128)S(1)}, f32[32]{0:T(128)}, u32[]{:S(2)}) copy-start(f32[32]{0:T(128)} %param.18) | copy-start | bytes 388
  7.9 3.4 %copy-start = (bf16[1,2,2,128,512]{4,3,2,1,0:T(8,128)(2,1)S(1)}, bf16[1,2,2,128,512]{4,3,2,1,0:T(8,128)(2,1)}, u32[]{:S(2)}) copy-start(bf16[1,2,2,128,512]{4,3,2,1,0:T(8,128)(2,1)} %u_bases.1) | copy-start | bytes 1572868
  7.9 3.4 %copy-start.1 = (bf16[1,2,2,128,512]{4,3,2,1,0:T(8,128)(2,1)S(1)}, bf16[1,2,2,128,512]{4,3,2,1,0:T(8,128)(2,1)}, u32[]{:S(2)}) copy-start(bf16[1,2,2,128,512]{4,3,2,1,0:T(8,128)(2,1)} %v_bases.3) | copy-start | bytes 1572868
  7.9 3.4 %copy-start.3 = (f32[8,2,512]{2,1,0:T(2,128)S(1)}, f32[8,2,512]{2,1,0:T(2,128)}, u32[]{:S(2)}) copy-start(f32[8,2,512]{2,1,0:T(2,128)} %u_ref.1) | copy-start | bytes 98308
  11.8 1.3 %collective-permute-start.3 = (bf16[64,512]{1,0:T(8,128)(2,1)S(1)}, bf16[64,512]{1,0:T(8,128)(2,1)S(1)}, u32[]{:S(2)}, u32[]{:S(2)}) collective-permute-start(bf16[64,512]{1,0:T(8,128)(2,1)S(1)} %get-tuple-element.31), channel_id=1, source_target_pairs={{0,1},{1,0},{2,3},{3,2},{4,5},{5,4},{6,7},{7,6},{8,9},{9,8},{10,11... | collective-permute-start | bytes 196616 | tf_op jit(solution)/shard_map/ppermute | solution.py:221
  13.2 4.3 %collective-permute-start.4 = (bf16[64,512]{1,0:T(8,128)(2,1)S(1)}, bf16[64,512]{1,0:T(8,128)(2,1)S(1)}, u32[]{:S(2)}, u32[]{:S(2)}) collective-permute-start(bf16[64,512]{1,0:T(8,128)(2,1)S(1)} %add_convert_fusion.sum_ref), channel_id=1, source_target_pairs={{0,2},{1,3},{2,0},{3,1},{4,6},{5,7},{6,4},{7,5},{8,10},{9,11},{10,... | collective-permute-start | bytes 196616 | tf_op jit(solution)/shard_map/ppermute | solution.py:221
  17.9 6.5 %collective-permute-start.5 = (bf16[272,128]{1,0:T(8,128)(2,1)S(1)}, bf16[272,128]{1,0:T(8,128)(2,1)S(1)}, u32[]{:S(2)}, u32[]{:S(2)}) collective-permute-start(bf16[272,128]{1,0:T(8,128)(2,1)S(1)} %get-tuple-element.33), channel_id=1, source_target_pairs={{0,8},{4,12},{8,0},{12,4},{1,9},{5,13},{9,1},{13,5},{2,10},{6,14},... | collective-permute-start | bytes 208904 | tf_op jit(solution)/shard_map/ppermute | solution.py:221
  19.2 6.3 %collective-permute-start.6 = (bf16[272,128]{1,0:T(8,128)(2,1)S(1)}, bf16[272,128]{1,0:T(8,128)(2,1)S(1)}, u32[]{:S(2)}, u32[]{:S(2)}) collective-permute-start(bf16[272,128]{1,0:T(8,128)(2,1)S(1)} %get-tuple-element.34), channel_id=1, source_target_pairs={{0,12},{4,8},{8,4},{12,0},{1,13},{5,9},{9,5},{13,1},{2,14},{6,10},... | collective-permute-start | bytes 208904 | tf_op jit(solution)/shard_map/ppermute | solution.py:221
  20.2 5.6 %collective-permute-start.7 = (bf16[272,128]{1,0:T(8,128)(2,1)S(1)}, bf16[272,128]{1,0:T(8,128)(2,1)S(1)}, u32[]{:S(2)}, u32[]{:S(2)}) collective-permute-start(bf16[272,128]{1,0:T(8,128)(2,1)S(1)} %get-tuple-element.35), channel_id=1, source_target_pairs={{0,4},{4,0},{8,12},{12,8},{1,5},{5,1},{9,13},{13,9},{2,6},{6,2},{1... | collective-permute-start | bytes 208904 | tf_op jit(solution)/shard_map/ppermute | solution.py:221
  25.8 4.4 %copy-start.2 = (f32[8,2,1024]{2,1,0:T(2,128)S(1)}, f32[8,2,1024]{2,1,0:T(2,128)}, u32[]{:S(2)}) copy-start(f32[8,2,1024]{2,1,0:T(2,128)} %v_ref.1) | copy-start | bytes 196612
  25.8 4.4 %copy-start.4 = (f32[8,2,1024]{2,1,0:T(2,128)S(1)}, f32[8,2,1024]{2,1,0:T(2,128)}, u32[]{:S(2)}) copy-start(f32[8,2,1024]{2,1,0:T(2,128)} %x_ref.1) | copy-start | bytes 196612
  25.8 4.4 %copy-start.5 = (f32[8,2,1024]{2,1,0:T(2,128)S(1)}, f32[8,2,1024]{2,1,0:T(2,128)}, u32[]{:S(2)}) copy-start(f32[8,2,1024]{2,1,0:T(2,128)} %w_ref.1) | copy-start | bytes 196612
  26.0 1.2 %collective-permute-start.8 = (f32[1,128]{1,0:T(1,128)S(1)}, f32[1,128]{1,0:T(1,128)S(1)}, u32[]{:S(2)}, u32[]{:S(2)}) collective-permute-start(f32[1,128]{1,0:T(1,128)S(1)} %get-tuple-element.36), channel_id=1, source_target_pairs={{0,1},{1,0},{2,3},{3,2},{4,5},{5,4},{6,7},{7,6},{8,9},{9,8},{10,11... | collective-permute-start | bytes 1544 | tf_op jit(solution)/shard_map/ppermute | solution.py:221
  27.2 3.0 %collective-permute-start.9 = (f32[1,128]{1,0:T(1,128)S(1)}, f32[1,128]{1,0:T(1,128)S(1)}, u32[]{:S(2)}, u32[]{:S(2)}) collective-permute-start(f32[1,128]{1,0:T(1,128)S(1)} %add.7.norms_ref), channel_id=1, source_target_pairs={{0,3},{1,2},{2,1},{3,0},{4,7},{5,6},{6,5},{7,4},{8,11},{9,10},{10,... | collective-permute-start | bytes 1544 | tf_op jit(solution)/shard_map/ppermute | solution.py:221
  28.5 3.9 %collective-permute-start.11 = (f32[1,128]{1,0:T(1,128)S(1)}, f32[1,128]{1,0:T(1,128)S(1)}, u32[]{:S(2)}, u32[]{:S(2)}) collective-permute-start(f32[1,128]{1,0:T(1,128)S(1)} %add.7.norms_ref), channel_id=1, source_target_pairs={{0,7},{1,6},{2,5},{3,4},{4,3},{5,2},{6,1},{7,0},{8,15},{9,14},{10,... | collective-permute-start | bytes 1544 | tf_op jit(solution)/shard_map/ppermute | solution.py:221
  28.9 3.4 %collective-permute-start.10 = (f32[1,128]{1,0:T(1,128)S(1)}, f32[1,128]{1,0:T(1,128)S(1)}, u32[]{:S(2)}, u32[]{:S(2)}) collective-permute-start(f32[1,128]{1,0:T(1,128)S(1)} %add.7.norms_ref), channel_id=1, source_target_pairs={{0,5},{1,4},{2,7},{3,6},{4,1},{5,0},{6,3},{7,2},{8,13},{9,12},{10,... | collective-permute-start | bytes 1544 | tf_op jit(solution)/shard_map/ppermute | solution.py:221
